TPU v7x, 32 devices: a whole 2x2x4 slice. The times are simulated.
32 devices in a mesh: lat: 16 (over z, y, x), lev: 2 (over core).
Axes of the slice: x: 2, y: 2, z: 4, core: 2. Of those that a mesh axis runs over, the one named last changes fastest.
Arguments:
- fields: bfloat16 [4, 4, 32, 2816], P('lev', None, 'lat'), may hold values from -6 to 6
- rows_first: int32 [32], P('lat'), may hold values from 0 to 28, as said below
- points: int32 [32], replicated, may hold values from 2753 to 2816, as said below
- starts: int32 [32, 4, 2816], P('lat'), may hold values from -60 to 2939, as said below
- weights: bfloat16 [32, 4, 4, 2816], P('lat'), may hold values from -1.5 to 1.5
- thickness: float32 [4], P('lev'), may hold values from 0.05 to 0.4
- legendre: bfloat16 [640, 32, 1281], P('lat'), may hold values from -1 to 1
Outputs:
- spectra: bfloat16 [4, 5, 2, 640, 1281], P('lev', None, None, 'lat')
Inputs may be any that keep to these rules, and one draw needn't show every extreme that they name: rows_first[j] is j - 2 or j - 1, moved into 0 to 28 at the ends. Columns of latitude j from points[j] on are padding. For every point k below points[j], starts[j, t, k] - k lies between minus half of 256 and half of 256 minus 4, and both ends are taken.
All inputs are finite; a program needn't handle non-finite values.
Results may differ from a plain program's by a relative error of at most 0.0064.
Values may be sent and summed in bfloat16 or wider, within the bound.
No kernel may reach another device: no remote copies, remote signals or barrier semaphores. Data moves between devices by JAX's collectives and lax.ppermute only.
A program may use at most 64 MiB of HBM per device.

v0:
```python
import functools

import jax
import jax.numpy as jnp
import numpy as np
from jax import lax
from jax.experimental import pallas as pl
from jax.experimental.pallas import tpu as pltpu
from jax.sharding import PartitionSpec as P

LANES = 128
SUB = 8
HALF = 64
STENCIL = 4
LIMIT = 56 * 1024 * 1024


def lane_gather(values, lanes):
    return jnp.take_along_axis(values, lanes, axis=1, mode="promise_in_bounds")


def turn_parts(product, total, inverse):
    turns = (product - jnp.floor(product * inverse + 0.5) * total) * inverse
    halves = jnp.floor(2.0 * turns + 0.5)
    sign = 1.0 - 2.0 * jnp.abs(halves)
    x = (turns - 0.5 * halves) * np.float32(2.0 * np.pi)
    y = x * x
    sine = -1.0 / 39916800.0
    for term in (1.0 / 362880.0, -1.0 / 5040.0, 1.0 / 120.0, -1.0 / 6.0, 1.0):
        sine = sine * y + np.float32(term)
    cosine = 1.0 / 479001600.0
    for term in (-1.0 / 3628800.0, 1.0 / 40320.0, -1.0 / 720.0, 1.0 / 24.0, -0.5, 1.0):
        cosine = cosine * y + np.float32(term)
    return sign * cosine, sign * (sine * x)


def extend(source, row, total, ext, slot):
    levels, fields, _, lon = source.shape
    blocks = lon // LANES
    for level in range(levels):
        for field in range(fields):
            place = level * fields + field
            line = source[level, field].astype(jnp.float32)
            for block in range(blocks):
                ext[slot, block + 1, place : place + 1, :] = line[
                    row : row + 1, block * LANES : (block + 1) * LANES
                ]
    lane = lax.broadcasted_iota(jnp.int32, (SUB, LANES), 1)
    missing = lon - total
    ahead = lane + missing
    behind = lane - missing
    first = lane_gather(ext[slot, 1], ahead & (LANES - 1))
    second = lane_gather(ext[slot, 2], ahead & (LANES - 1))
    last = ext[slot, blocks]
    final = lane_gather(last, behind & (LANES - 1))
    before = lane_gather(ext[slot, blocks - 1], behind & (LANES - 1))
    ext[slot, 0] = jnp.where(behind >= 0, final, before)
    ext[slot, blocks] = jnp.where(ahead < LANES, last, first)
    ext[slot, blocks + 1] = jnp.where(ahead < LANES, first, second)


def spread_rows(starts, begins):
    for latitude in range(starts.shape[0]):
        for row in range(STENCIL):
            begins[latitude, row] = starts[latitude, row : row + 1, :]


def gathered(block, latitude, picks, ext, starts, weights):
    offset = pl.multiple_of(block * LANES, LANES)
    total = jnp.zeros((SUB, LANES), jnp.float32)
    for row, slot in picks:
        start = starts[latitude, row, :, pl.ds(offset, LANES)] - (offset - LANES)
        start = jnp.broadcast_to(start, (SUB, LANES))
        factors = weights[latitude, row, :, pl.ds(offset, LANES)].astype(jnp.float32)
        parts = [ext[slot, block + piece] for piece in range(3)]
        for column in range(4):
            place = start + column
            lane = place & (LANES - 1)
            low, middle, high = [lane_gather(part, lane) for part in parts]
            value = jnp.where(place < LANES, low, jnp.where(place < 2 * LANES, middle, high))
            total = total + factors[column : column + 1] * value
    return total


def near_kernel(
    pair_total, pair_count, rows_first, points, fields, starts, weights,
    partial, table, twiddle, ext, fine, begins,
):
    lat_count = starts.shape[0]
    spread_rows(starts, begins)
    blocks = partial.shape[1]
    columns = table.shape[2] // 2
    first_lat = lax.axis_index("lat") * lat_count
    for latitude in range(lat_count):
        extend(fields, latitude, points[first_lat + latitude], ext, latitude)
    for latitude in range(lat_count):
        mine = first_lat - rows_first[latitude]
        picks = [(mine + row, row) for row in range(lat_count)]

        def one(block, carry, latitude=latitude, picks=picks):
            partial[latitude, block] = gathered(block, latitude, picks, ext, begins, weights)
            return carry

        lax.fori_loop(0, blocks, one, 0, unroll=11)
    for latitude in range(lat_count):
        total = jnp.full((1, 1), points[first_lat + latitude], jnp.int32).astype(jnp.float32)
        inverse = 1.0 / total
        scaling = jnp.sqrt(2.0 * inverse)
        width = min(columns, 512)

        def chunk(index, carry, latitude=latitude, total=total, inverse=inverse, scaling=scaling):
            at = pl.multiple_of(index * width, width)
            numbers = wavenumbers_at(at, width, pair_count, pair_total)
            step = lax.broadcasted_iota(jnp.int32, (blocks, width), 0).astype(jnp.float32)
            cosine, sine = turn_parts(numbers * step * float(LANES), total, inverse)
            twiddle[latitude, :, pl.ds(at, width)] = scaling * cosine
            twiddle[latitude, :, pl.ds(columns + at, width)] = scaling * sine
            step = lax.broadcasted_iota(jnp.int32, (16, width), 0).astype(jnp.float32)
            low_cos, low_sin = turn_parts(numbers * step, total, inverse)
            step = lax.broadcasted_iota(jnp.int32, (SUB, width), 0).astype(jnp.float32)
            high_cos, high_sin = turn_parts(numbers * step * 16.0, total, inverse)
            fine[0] = high_cos
            fine[1] = high_sin
            for high in range(SUB):
                this_cos = fine[0, high : high + 1, :]
                this_sin = fine[1, high : high + 1, :]
                rows = pl.ds(16 * high, 16)
                table[latitude, rows, pl.ds(at, width)] = (
                    this_cos * low_cos - this_sin * low_sin
                ).astype(jnp.bfloat16)
                table[latitude, rows, pl.ds(columns + at, width)] = (
                    this_cos * low_sin + this_sin * low_cos
                ).astype(jnp.bfloat16)
            return carry

        lax.fori_loop(0, columns // width, chunk, 0)


def wavenumbers_at(at, width, pair_count, pair_total):
    column = lax.broadcasted_iota(jnp.int32, (1, width), 1) + at
    lane = column & (LANES - 1)
    second = lane >= HALF
    inner = jnp.where(second, lane - HALF, lane)
    pair = (column >> 7) * pair_count + inner
    number = jnp.where(second, 2 * pair_total - 1 - pair, pair)
    return jnp.where(inner < pair_count, number, 0).astype(jnp.float32)


def far_kernel(
    rows_first, points, below, above, starts, weights, partial, table, twiddle,
    out, ext, grid, begins,
):
    lat_count = starts.shape[0]
    spread_rows(starts, begins)
    blocks = partial.shape[1]
    columns = table.shape[2] // 2
    first_lat = lax.axis_index("lat") * lat_count
    lat_total = points.shape[0]
    for row in range(lat_count):
        under = jnp.maximum(first_lat - lat_count + row, 0)
        over = jnp.minimum(first_lat + lat_count + row, lat_total - 1)
        extend(below, row, points[under], ext, row)
        extend(above, row, points[over], ext, lat_count + row)
    lane = lax.broadcasted_iota(jnp.int32, (SUB, LANES), 1)
    for latitude in range(lat_count):
        mine = first_lat - rows_first[latitude]
        one_row = jnp.where(mine >= 1, 0, 2)
        two_row = jnp.where(mine <= 1, 3, 1)
        picks = []
        for row in (one_row, two_row):
            picks.append((row, jnp.where(row < mine, row - mine + 2, row - mine)))

        def one(block, carry, latitude=latitude, picks=picks):
            value = partial[latitude, block] + gathered(
                block, latitude, picks, ext, begins, weights
            )
            live = lane + block * LANES < points[first_lat + latitude]
            grid[block] = jnp.where(live, value, 0.0)
            return carry

        lax.fori_loop(0, blocks, one, 0, unroll=11)
        rows = grid[...].reshape(blocks * SUB, LANES).astype(jnp.bfloat16)
        width = 2 * LANES

        def chunk(index, carry, latitude=latitude, rows=rows):
            at = pl.multiple_of(index * width, width)
            real = jnp.dot(
                rows, table[latitude, :, pl.ds(at, width)], preferred_element_type=jnp.float32
            ).reshape(blocks, SUB, width)
            imag = jnp.dot(
                rows,
                table[latitude, :, pl.ds(columns + at, width)],
                preferred_element_type=jnp.float32,
            ).reshape(blocks, SUB, width)
            cosine = jnp.zeros((SUB, width), jnp.float32)
            sine = jnp.zeros((SUB, width), jnp.float32)
            for block in range(blocks):
                turn_cos = twiddle[latitude, block : block + 1, pl.ds(at, width)]
                turn_sin = twiddle[latitude, block : block + 1, pl.ds(columns + at, width)]
                cosine = cosine + (real[block] * turn_cos - imag[block] * turn_sin)
                sine = sine - (real[block] * turn_sin + imag[block] * turn_cos)
            both = jnp.concatenate([cosine, sine], axis=0).astype(jnp.bfloat16)
            for piece in range(width // LANES):
                out[index * (width // LANES) + piece, 2 * SUB * latitude : 2 * SUB * (latitude + 1), :] = (
                    both[:, piece * LANES : (piece + 1) * LANES]
                )
            return carry

        lax.fori_loop(0, columns // width, chunk, 0)


def legendre_kernel(
    level_count, field_count, thickness, received, totals, legendre, out, wide, left,
):
    owners, packed_rows, _ = received.shape
    lat_total = wide.shape[0] // (2 * SUB)
    pair_count = legendre.shape[0]
    tile = legendre.shape[2]
    groups = [(at, min(SUB, pair_count - at)) for at in range(0, pair_count, SUB)]
    out_rows = level_count * (field_count + 1) * 2
    step = pl.program_id(0)

    @pl.when(step == 0)
    def build():
        wide[...] = received[...].astype(jnp.float32).reshape(wide.shape)
        level_place = lax.axis_index("lev")
        lines = {}
        for part in range(2):
            running = jnp.zeros((lat_total, LANES), jnp.float32)
            for other in range(1, totals.shape[0]):
                running = running + jnp.where(other > level_place, totals[other, part], 0.0)
            for level in reversed(range(level_count)):
                for field in range(field_count):
                    place = part * SUB + level * field_count + field
                    lines[level, field, part] = wide[pl.ds(place, lat_total, stride=2 * SUB), :]
                running = running + thickness[level] * (
                    lines[level, 2, part] + 0.61 * lines[level, 3, part]
                )
                lines[level, field_count, part] = running
        depth = SUB * lat_total
        spread = (
            lax.broadcasted_iota(jnp.int32, (lat_total, depth), 0)
            == lax.broadcasted_iota(jnp.int32, (lat_total, depth), 1) % lat_total
        ).astype(jnp.bfloat16)
        keep = (
            lax.broadcasted_iota(jnp.int32, (SUB, depth), 0)
            == lax.broadcasted_iota(jnp.int32, (SUB, depth), 1) // lat_total
        )
        order = [
            (level, field, part)
            for level in range(level_count)
            for field in range(field_count + 1)
            for part in range(2)
        ]
        for place in range(0, out_rows, 2):
            couple = [
                lax.dot_general(
                    lines[key].astype(jnp.bfloat16),
                    spread,
                    (((0,), (0,)), ((), ())),
                    preferred_element_type=jnp.float32,
                )
                for key in order[place : place + 2]
            ]
            for member in range(2):
                for group, (at, _) in enumerate(groups):
                    begin = member * HALF + at
                    pieces = [jnp.where(keep, one[begin : begin + SUB], 0.0) for one in couple]
                    into = (member * out_rows + place) * SUB
                    left[group, into : into + 2 * SUB, :] = jnp.concatenate(
                        pieces, axis=0
                    ).astype(jnp.bfloat16)

    first_pair = lax.axis_index("lat") * pair_count
    pair_total = pair_count * owners
    parts = []
    for group, (at, size) in enumerate(groups):
        depth = size * lat_total
        values = legendre[at : at + size].reshape(depth, tile)
        sums = jnp.dot(left[group, :, :depth], values, preferred_element_type=jnp.float32)
        sums = sums.reshape(2, out_rows, SUB, tile)
        slot = lax.broadcasted_iota(jnp.int32, (SUB, tile), 1) + step * tile
        pair = lax.broadcasted_iota(jnp.int32, (SUB, tile), 0) + (first_pair + at)
        first = slot + pair < 2 * pair_total
        chosen = jnp.where(first, sums[0], sums[1])
        parts.append(chosen[:, :size])
    out[...] = jnp.concatenate(parts, axis=1).astype(jnp.bfloat16).reshape(out.shape)


def local(fields, rows_first, points, starts, weights, thickness, legendre):
    level_count, field_count, lat_count, lon_count = fields.shape
    pair_count, lat_total, degrees = legendre.shape
    owners = lax.axis_size("lat")
    level_owners = lax.axis_size("lev")
    blocks = lon_count // LANES
    columns = owners * LANES
    up = [(i, i + 1) for i in range(owners - 1)]
    below = lax.ppermute(fields, "lat", up)
    above = lax.ppermute(fields, "lat", [(j, i) for i, j in up])

    scalar = pl.BlockSpec(memory_space=pltpu.SMEM)
    vector = pl.BlockSpec(memory_space=pltpu.VMEM)
    params = pltpu.CompilerParams(vmem_limit_bytes=LIMIT)
    partial, table, twiddle = pl.pallas_call(
        functools.partial(near_kernel, pair_count * owners, pair_count),
        out_shape=(
            jax.ShapeDtypeStruct((lat_count, blocks, SUB, LANES), jnp.float32),
            jax.ShapeDtypeStruct((lat_count, LANES, 2 * columns), jnp.bfloat16),
            jax.ShapeDtypeStruct((lat_count, blocks, 2 * columns), jnp.float32),
        ),
        in_specs=[scalar, scalar, vector, vector, vector],
        out_specs=(vector, vector, vector),
        scratch_shapes=[
            pltpu.VMEM((lat_count, blocks + 2, SUB, LANES), jnp.float32),
            pltpu.VMEM((2, SUB, min(columns, 512)), jnp.float32),
            pltpu.VMEM((lat_count, STENCIL, 1, lon_count), jnp.int32),
        ],
        compiler_params=params,
        cost_estimate=pl.CostEstimate(flops=10_000_000, bytes_accessed=4_000_000, transcendentals=0),
        name="near_rows",
    )(rows_first, points, fields, starts, weights)

    coefficients = pl.pallas_call(
        far_kernel,
        out_shape=jax.ShapeDtypeStruct((owners, 2 * SUB * lat_count, LANES), jnp.bfloat16),
        in_specs=[scalar, scalar] + [vector] * 7,
        out_specs=vector,
        scratch_shapes=[
            pltpu.VMEM((2 * lat_count, blocks + 2, SUB, LANES), jnp.float32),
            pltpu.VMEM((blocks, SUB, LANES), jnp.float32),
            pltpu.VMEM((lat_count, STENCIL, 1, lon_count), jnp.int32),
        ],
        compiler_params=params,
        name="far_rows",
    )(rows_first, points, below, above, starts, weights, partial, table, twiddle)

    received = lax.all_to_all(coefficients, "lat", split_axis=0, concat_axis=0, tiled=True)
    by_level = received.reshape(lat_total, 2, level_count, field_count, LANES).astype(jnp.float32)
    virtual = by_level[:, :, :, 2] + 0.61 * by_level[:, :, :, 3]
    total = jnp.sum(thickness[None, None, :, None] * virtual, axis=2).transpose(1, 0, 2)
    totals = lax.all_gather(total, "lev")

    tile = 256
    out_rows = level_count * (field_count + 1) * 2
    steps = (degrees + tile - 1) // tile
    group_count = (pair_count + SUB - 1) // SUB
    return pl.pallas_call(
        functools.partial(legendre_kernel, level_count, field_count),
        grid=(steps,),
        out_shape=jax.ShapeDtypeStruct(
            (level_count, field_count + 1, 2, pair_count, degrees), jnp.bfloat16
        ),
        in_specs=[
            scalar,
            pl.BlockSpec(received.shape, lambda i: (0, 0, 0)),
            pl.BlockSpec(totals.shape, lambda i: (0, 0, 0, 0)),
            pl.BlockSpec((pair_count, lat_total, tile), lambda i: (0, 0, i)),
        ],
        out_specs=pl.BlockSpec(
            (level_count, field_count + 1, 2, pair_count, tile), lambda i: (0, 0, 0, 0, i)
        ),
        scratch_shapes=[
            pltpu.VMEM((lat_total * 2 * SUB, LANES), jnp.float32),
            pltpu.VMEM((group_count, 2 * out_rows * SUB, SUB * lat_total), jnp.bfloat16),
        ],
        compiler_params=params,
        name="degree_sums",
    )(thickness, received, totals, legendre)


def solution(mesh):
    placed = (
        P("lev", None, "lat", None),
        P("lat"),
        P(),
        P("lat", None, None),
        P("lat", None, None, None),
        P("lev"),
        P("lat", None, None),
    )
    return jax.shard_map(
        local,
        mesh=mesh,
        in_specs=placed,
        out_specs=P("lev", None, None, "lat", None),
        check_vma=False,
    )
```

profile of v0, /device:TPU:0, one launch (start us, length us, event | category | flops | bytes accessed | tf_op | source)
XLA Modules:
  0.0 47.3 jit_solution(1018211520973904925)
XLA Ops:
  0.0 0.0 copy-start.3
  0.0 5.0 %collective-permute-start = (bf16[2,4,2,2816]{3,2,1,0:T(2,128)(2,1)}, bf16[2,4,2,2816]{3,2,1,0:T(2,128)(2,1)S(1)}, u32[]{:S(2)}, u32[]{:S(2)}) collective-permute-start(bf16[2,4,2,2816]{3,2,1,0:T(2,128)(2,1)} %fields.1), channel_id=1, source_target_pairs={{0,2},{2,4},{4,6},{6,8},{8,10},{10,12},{12,14},{14,16},{16,18},{18... | collective-permute-start | bytes 270344 | tf_op jit(solution)/shard_map/ppermute | solution.py:298
  5.0 1.3 %collective-permute-start.1 = (bf16[2,4,2,2816]{3,2,1,0:T(2,128)(2,1)}, bf16[2,4,2,2816]{3,2,1,0:T(2,128)(2,1)S(1)}, u32[]{:S(2)}, u32[]{:S(2)}) collective-permute-start(bf16[2,4,2,2816]{3,2,1,0:T(2,128)(2,1)} %fields.1), channel_id=1, source_target_pairs={{2,0},{4,2},{6,4},{8,6},{10,8},{12,10},{14,12},{16,14},{18,16},{20... | collective-permute-start | bytes 270344 | tf_op jit(solution)/shard_map/ppermute | solution.py:299
  6.3 7.0 %near_rows.1 = (f32[2,22,8,128]{3,2,1,0:T(8,128)}, bf16[2,128,4096]{2,1,0:T(8,128)(2,1)}, f32[2,22,4096]{2,1,0:T(8,128)}) custom-call(s32[2]{0:T(128)} %rows_first.3, s32[32]{0:T(128)} %points.3, bf16[2,4,2,2816]{3,2,1,0:T(2,128)(2,1)} %fields.1, s32[2,4,2816]{2,1,0:T(4,128)} %starts.3, bf16[2,4,4,2816]{3,2,1,0:T(4,128)(2,1)} %weights.3), custom_call_target="tpu_custom_call" | custom-call | flops 10000000 | bytes 4000000 | tf_op jit(solution)/shard_map/near_rows/pallas_call | solution.py:304
  13.2 0.0 collective-permute-done.below
  13.2 0.0 copy-start.1
  13.2 0.0 collective-permute-done.1.above
  13.2 0.0 copy-start.2
  13.3 0.6 %copy-done.1 = bf16[2,4,2,2816]{3,2,1,0:T(2,128)(2,1)} copy-done((bf16[2,4,2,2816]{3,2,1,0:T(2,128)(2,1)}, bf16[2,4,2,2816]{3,2,1,0:T(2,128)(2,1)S(1)}, u32[]{:S(2)}) %copy-start.1) | copy-done | bytes 90136
  13.9 0.0 copy-done.2
  13.9 8.6 %far_rows.1 = bf16[16,32,128]{2,1,0:T(8,128)(2,1)} custom-call(s32[2]{0:T(128)} %rows_first.3, s32[32]{0:T(128)} %points.3, bf16[2,4,2,2816]{3,2,1,0:T(2,128)(2,1)} %copy-done.1, bf16[2,4,2,2816]{3,2,1,0:T(2,128)(2,1)} %copy-done.2, s32[2,4,2816]{2,1,0:T(4,128)} %starts.3, bf16[2,4,4,2816]{3,2,1,0:T(4,128)(2,1)} %weights.3, ...), custom_call_target="tpu_custom_call" | custom-call | tf_op jit(solution)/shard_map/far_rows/pallas_call | solution.py:323
  22.5 15.8 %all_to_all.5.received = bf16[16,32,128]{2,1,0:T(8,128)(2,1)S(1)} all-to-all(bf16[16,32,128]{2,1,0:T(8,128)(2,1)} %far_rows.1), channel_id=1, replica_groups=mesh['lat'=16,'lev'=2] {'lat'}, dimensions={0} | all-to-all | bytes 262144 | tf_op jit(solution)/shard_map/all_to_all | solution.py:337
  38.4 0.0 copy-start
  38.4 0.1 fusion.1
  38.5 0.0 copy-done.3
  38.5 0.2 fusion
  38.7 2.0 %all-gather = f32[4,32,128]{2,1,0:T(8,128)} all-gather(f32[2,32,128]{2,1,0:T(8,128)S(1)} %copy.10), channel_id=2, replica_groups=mesh['lat'=16,'lev'=2] {'lev'}, dimensions={0}, use_global_device_ids=true | all-gather | bytes 98304 | tf_op jit(solution)/shard_map/all_gather | solution.py:341
  40.7 0.0 copy-done
  40.7 6.6 %degree_sums.1 = bf16[2,5,2,40,1281]{4,3,2,1,0:T(8,128)(2,1)} custom-call(f32[2]{0:T(128)} %thickness.1, bf16[16,32,128]{2,1,0:T(8,128)(2,1)} %copy-done, f32[2,2,32,128]{3,2,1,0:T(8,128)} %bitcast.11, bf16[40,32,1281]{2,1,0:T(8,128)(2,1)} %legendre.1), custom_call_target="tpu_custom_call" | custom-call | tf_op jit(solution)/shard_map/degree_sums/pallas_call | solution.py:347
  (1 shorter events, 0.0 us)
Async XLA Ops:
  0.0 38.5 %copy-start.3 = (f32[2]{0:T(128)S(1)}, f32[2]{0:T(128)}, u32[]{:S(2)}) copy-start(f32[2]{0:T(128)} %thickness.1) | copy-start | bytes 28
  0.0 13.2 %collective-permute-start = (bf16[2,4,2,2816]{3,2,1,0:T(2,128)(2,1)}, bf16[2,4,2,2816]{3,2,1,0:T(2,128)(2,1)S(1)}, u32[]{:S(2)}, u32[]{:S(2)}) collective-permute-start(bf16[2,4,2,2816]{3,2,1,0:T(2,128)(2,1)} %fields.1), channel_id=1, source_target_pairs={{0,2},{2,4},{4,6},{6,8},{8,10},{10,12},{12,14},{14,16},{16,18},{18... | collective-permute-start | bytes 270344 | tf_op jit(solution)/shard_map/ppermute | solution.py:298
  5.0 8.3 %collective-permute-start.1 = (bf16[2,4,2,2816]{3,2,1,0:T(2,128)(2,1)}, bf16[2,4,2,2816]{3,2,1,0:T(2,128)(2,1)S(1)}, u32[]{:S(2)}, u32[]{:S(2)}) collective-permute-start(bf16[2,4,2,2816]{3,2,1,0:T(2,128)(2,1)} %fields.1), channel_id=1, source_target_pairs={{2,0},{4,2},{6,4},{8,6},{10,8},{12,10},{14,12},{16,14},{18,16},{20... | collective-permute-start | bytes 270344 | tf_op jit(solution)/shard_map/ppermute | solution.py:299
  13.2 0.6 %copy-start.1 = (bf16[2,4,2,2816]{3,2,1,0:T(2,128)(2,1)}, bf16[2,4,2,2816]{3,2,1,0:T(2,128)(2,1)S(1)}, u32[]{:S(2)}) copy-start(bf16[2,4,2,2816]{3,2,1,0:T(2,128)(2,1)S(1)} %collective-permute-done.below) | copy-start | bytes 270340
  13.2 0.7 %copy-start.2 = (bf16[2,4,2,2816]{3,2,1,0:T(2,128)(2,1)}, bf16[2,4,2,2816]{3,2,1,0:T(2,128)(2,1)S(1)}, u32[]{:S(2)}) copy-start(bf16[2,4,2,2816]{3,2,1,0:T(2,128)(2,1)S(1)} %collective-permute-done.1.above) | copy-start | bytes 270340
  38.4 2.3 %copy-start = (bf16[16,32,128]{2,1,0:T(8,128)(2,1)}, bf16[16,32,128]{2,1,0:T(8,128)(2,1)S(1)}, u32[]{:S(2)}) copy-start(bf16[16,32,128]{2,1,0:T(8,128)(2,1)S(1)} %all_to_all.5.received) | copy-start | bytes 393220
where the time goes:
time: 47.7 us; the launch traced here: 47.3 us
  Pallas kernels  22.2 us (47%)
  blocking collectives  17.8 us (37%)
  starting transfers between devices  6.26 us (13%)
  local copies, waits for them, and re-layouts  0.78 us (2%)
    all_to_all x1, blocking collectives, local(): lax.all_to_all(coefficients, 'lat', split_axis=0, concat_axis=0, tiled=True)  15.8 us
    pallas_call x1, Pallas kernels, local(): pl.pallas_call(far_kernel, out_shape=jax.ShapeDtypeStruct((owners, 2 * SU...  8.64 us
    pallas_call x1, Pallas kernels, local(): pl.pallas_call(functools.partial(near_kernel, pair_count * owners, pair_c...  6.96 us
    pallas_call x1, Pallas kernels, local(): pl.pallas_call(functools.partial(legendre_kernel, level_count, field_coun...  6.65 us
    ppermute x1, starting transfers between devices, local(): below = lax.ppermute(fields, 'lat', up)  4.97 us
    all_gather x1, blocking collectives, local(): totals = lax.all_gather(total, 'lev')  1.99 us
    ppermute x1, starting transfers between devices, local(): above = lax.ppermute(fields, 'lat', [(j, i) for i, j in up])  1.29 us
  transfers between devices with their start and end apart: 2, of which 0 were waited for; matrix products, arithmetic and copies ran while one was open for 0% of the time, Pallas kernels for 15%

commit v1 on v0

v1 whole, which is shorter than its diff:
```python
import functools

import jax
import jax.numpy as jnp
import numpy as np
from jax import lax
from jax.experimental import pallas as pl
from jax.experimental.pallas import tpu as pltpu
from jax.sharding import PartitionSpec as P

LANES = 128
SUB = 8
STENCIL = 4
LIMIT = 24 * 1024 * 1024


def lane_gather(values, lanes):
    return jnp.take_along_axis(values, lanes, axis=1, mode="promise_in_bounds")


def turn_parts(product, total, inverse):
    turns = (product - jnp.floor(product * inverse + 0.5) * total) * inverse
    halves = jnp.floor(2.0 * turns + 0.5)
    sign = 1.0 - 2.0 * jnp.abs(halves)
    x = (turns - 0.5 * halves) * np.float32(2.0 * np.pi)
    y = x * x
    sine = -1.0 / 39916800.0
    for term in (1.0 / 362880.0, -1.0 / 5040.0, 1.0 / 120.0, -1.0 / 6.0, 1.0):
        sine = sine * y + np.float32(term)
    cosine = 1.0 / 479001600.0
    for term in (-1.0 / 3628800.0, 1.0 / 40320.0, -1.0 / 720.0, 1.0 / 24.0, -0.5, 1.0):
        cosine = cosine * y + np.float32(term)
    return sign * cosine, sign * (sine * x)


def wavenumbers(at, width, pair_count, pair_total):
    column = lax.broadcasted_iota(jnp.int32, (1, width), 1) + at
    owner = column // (2 * pair_count)
    inner = column - owner * (2 * pair_count)
    second = inner >= pair_count
    pair = owner * pair_count + jnp.where(second, inner - pair_count, inner)
    return jnp.where(second, 2 * pair_total - 1 - pair, pair).astype(jnp.float32)


def extend(lines, row, rows_each, missing, ext, slot):
    blocks = ext.shape[1] - 2
    for block in range(blocks):
        ext[slot, block + 1] = lines[
            pl.ds(block * rows_each + row, SUB, stride=blocks * rows_each), :
        ]
    lane = lax.broadcasted_iota(jnp.int32, (SUB, LANES), 1)
    ahead = lane + missing
    behind = lane - missing
    first = lane_gather(ext[slot, 1], ahead & (LANES - 1))
    second = lane_gather(ext[slot, 2], ahead & (LANES - 1))
    last = ext[slot, blocks]
    final = lane_gather(last, behind & (LANES - 1))
    before = lane_gather(ext[slot, blocks - 1], behind & (LANES - 1))
    ext[slot, 0] = jnp.where(behind >= 0, final, before)
    ext[slot, blocks] = jnp.where(ahead < LANES, last, first)
    ext[slot, blocks + 1] = jnp.where(ahead < LANES, first, second)


def spread_rows(starts, begins):
    lat_count, _, blocks = begins.shape[:3]
    for latitude in range(lat_count):
        for block in range(blocks):
            for row in range(STENCIL):
                lanes = slice(block * LANES, (block + 1) * LANES)
                begins[latitude, row, block] = (
                    starts[latitude, row : row + 1, lanes] - (block - 1) * LANES
                )


def spread_lines(source, lines):
    first, second, rows, lon = source.shape
    at = 0
    for one in range(first):
        for two in range(second):
            values = source[one, two].astype(jnp.float32)
            for block in range(lon // LANES):
                lines[at : at + rows, :] = values[:, block * LANES : (block + 1) * LANES]
                at += rows


def gathered(couple, latitude, picks, ext, begins, factors):
    totals = [jnp.zeros((SUB, LANES), jnp.float32) for _ in range(2)]
    couples = begins.shape[2] // 2
    for row, slot in picks:
        at = ((latitude * STENCIL + row) * couples + couple) * SUB
        scale = factors[pl.ds(pl.multiple_of(at, SUB), SUB), :]
        parts = [ext[slot, 2 * couple + piece] for piece in range(4)]
        for side in range(2):
            start = jnp.broadcast_to(begins[latitude, row, 2 * couple + side], (SUB, LANES))
            for column in range(4):
                place = start + column
                lane = place & (LANES - 1)
                low, middle, high = [
                    lane_gather(part, lane) for part in parts[side : side + 3]
                ]
                value = jnp.where(place < LANES, low, jnp.where(place < 2 * LANES, middle, high))
                line = STENCIL * side + column
                totals[side] = totals[side] + scale[line : line + 1] * value
    return totals


def near_kernel(
    pair_total, pair_count, rows_first, points, fields, starts, weights,
    partial, table, twiddle, lines, ext, fine, begins, factors,
):
    lat_count, couples = partial.shape[:2]
    lon = 2 * couples * LANES
    columns = table.shape[2] // 2
    first_lat = lax.axis_index("lat") * lat_count
    spread_rows(starts, begins)
    spread_lines(weights, factors)
    spread_lines(fields, lines)
    for latitude in range(lat_count):
        extend(lines, latitude, lat_count, lon - points[first_lat + latitude], ext, latitude)
    for latitude in range(lat_count):
        mine = first_lat - rows_first[latitude]
        picks = [(mine + row, row) for row in range(lat_count)]
        for couple in range(couples):
            totals = gathered(couple, latitude, picks, ext, begins, factors)
            for side in range(2):
                partial[latitude, couple, :, side * LANES : (side + 1) * LANES] = totals[side]
    width = 256
    for latitude in range(lat_count):
        total = jnp.full((1, 1), points[first_lat + latitude], jnp.int32).astype(jnp.float32)
        inverse = 1.0 / total
        scaling = jnp.sqrt(2.0 * inverse)

        def chunk(index, carry, latitude=latitude, total=total, inverse=inverse, scaling=scaling):
            at = pl.multiple_of(index * width, width)
            numbers = wavenumbers(at, width, pair_count, pair_total)
            step = lax.broadcasted_iota(jnp.int32, (couples, width), 0).astype(jnp.float32)
            cosine, sine = turn_parts(numbers * step * float(2 * LANES), total, inverse)
            twiddle[latitude, :, pl.ds(at, width)] = scaling * cosine
            twiddle[latitude, :, pl.ds(columns + at, width)] = scaling * sine
            step = lax.broadcasted_iota(jnp.int32, (16, width), 0).astype(jnp.float32)
            low_cos, low_sin = turn_parts(numbers * step, total, inverse)
            high_cos, high_sin = turn_parts(numbers * step * 16.0, total, inverse)
            fine[0] = high_cos
            fine[1] = high_sin
            for high in range(16):
                this_cos = fine[0, high : high + 1, :]
                this_sin = fine[1, high : high + 1, :]
                rows = pl.ds(16 * high, 16)
                table[latitude, rows, pl.ds(at, width)] = (
                    this_cos * low_cos - this_sin * low_sin
                ).astype(jnp.bfloat16)
                table[latitude, rows, pl.ds(columns + at, width)] = (
                    this_cos * low_sin + this_sin * low_cos
                ).astype(jnp.bfloat16)
            return carry

        lax.fori_loop(0, columns // width, chunk, 0)


def far_kernel(
    rows_first, points, below, above, starts, weights, partial, table, twiddle,
    out, lines, ext, grid, begins, factors, waves,
):
    lat_count, couples = partial.shape[:2]
    lon = 2 * couples * LANES
    columns = table.shape[2] // 2
    owners = out.shape[0]
    first_lat = lax.axis_index("lat") * lat_count
    lat_total = points.shape[0]
    spread_rows(starts, begins)
    spread_lines(weights, factors)
    for side, source in enumerate((below, above)):
        spread_lines(source, lines.at[side])
        for row in range(lat_count):
            if side == 0:
                place = jnp.maximum(first_lat - lat_count + row, 0)
            else:
                place = jnp.minimum(first_lat + lat_count + row, lat_total - 1)
            extend(
                lines.at[side], row, lat_count, lon - points[place], ext, side * lat_count + row
            )
    lane = lax.broadcasted_iota(jnp.int32, (SUB, LANES), 1)
    width = 256
    for latitude in range(lat_count):
        mine = first_lat - rows_first[latitude]
        one_row = jnp.where(mine >= 1, 0, 2)
        two_row = jnp.where(mine <= 1, 3, 1)
        picks = []
        for row in (one_row, two_row):
            picks.append((row, jnp.where(row < mine, row - mine + lat_count, row - mine)))
        for couple in range(couples):
            totals = gathered(couple, latitude, picks, ext, begins, factors)
            for side in range(2):
                lanes = pl.ds(side * LANES, LANES)
                live = lane + (2 * couple + side) * LANES < points[first_lat + latitude]
                value = partial[latitude, couple, :, lanes] + totals[side]
                grid[couple, :, lanes] = jnp.where(live, value, 0.0)
        rows = grid[...].reshape(couples * SUB, 2 * LANES).astype(jnp.bfloat16)
        for at in range(0, columns, width):
            real = jnp.dot(
                rows, table[latitude, :, at : at + width], preferred_element_type=jnp.float32
            )
            imag = jnp.dot(
                rows,
                table[latitude, :, columns + at : columns + at + width],
                preferred_element_type=jnp.float32,
            )
            cosine = jnp.zeros((SUB, width), jnp.float32)
            sine = jnp.zeros((SUB, width), jnp.float32)
            for couple in range(couples):
                turn_cos = twiddle[latitude, couple : couple + 1, at : at + width]
                turn_sin = twiddle[latitude, couple : couple + 1, columns + at : columns + at + width]
                here = slice(couple * SUB, (couple + 1) * SUB)
                cosine = cosine + (real[here] * turn_cos - imag[here] * turn_sin)
                sine = sine - (real[here] * turn_sin + imag[here] * turn_cos)
            waves[0:SUB, at : at + width] = cosine
            waves[SUB : 2 * SUB, at : at + width] = sine
        waves[:, columns:] = jnp.zeros((2 * SUB, waves.shape[1] - columns), jnp.float32)
        used = columns // owners
        for owner in range(owners):
            out[owner, 2 * SUB * latitude : 2 * SUB * (latitude + 1), :] = waves[
                :, owner * used : owner * used + LANES
            ].astype(jnp.bfloat16)


def legendre_kernel(
    level_count, field_count, thickness, received, totals, legendre, out, wide, left, planes, sent,
):
    owners = received.shape[0]
    lat_total = wide.shape[0] // (2 * SUB)
    pair_count, _, degrees = legendre.shape
    pair_total = pair_count * owners
    groups = [(at, min(SUB, pair_count - at)) for at in range(0, pair_count, SUB)]
    keys = [(field, part) for field in range(field_count + 1) for part in range(2)]
    half = len(keys) * SUB
    level_place = lax.axis_index("lev")
    first_pair = lax.axis_index("lat") * pair_count
    wide[...] = received[...].astype(jnp.float32).reshape(wide.shape)
    lines = {}
    for part in range(2):
        running = jnp.zeros((lat_total, LANES), jnp.float32)
        for other in range(1, totals.shape[0]):
            running = running + jnp.where(other > level_place, totals[other, part], 0.0)
        for level in reversed(range(level_count)):
            for field in range(field_count):
                place = part * SUB + level * field_count + field
                lines[level, field, part] = wide[pl.ds(place, lat_total, stride=2 * SUB), :]
            running = running + thickness[level] * (
                lines[level, 2, part] + 0.61 * lines[level, 3, part]
            )
            lines[level, field_count, part] = running
    depth = SUB * lat_total
    spread = (
        lax.broadcasted_iota(jnp.int32, (lat_total, depth), 0)
        == lax.broadcasted_iota(jnp.int32, (lat_total, depth), 1) % lat_total
    ).astype(jnp.bfloat16)
    keep = (
        lax.broadcasted_iota(jnp.int32, (SUB, depth), 0)
        == lax.broadcasted_iota(jnp.int32, (SUB, depth), 1) // lat_total
    )
    copies = []
    for level in range(level_count):
        for place in range(0, len(keys), 2):
            couple = [
                lax.dot_general(
                    lines[(level,) + key].astype(jnp.bfloat16),
                    spread,
                    (((0,), (0,)), ((), ())),
                    preferred_element_type=jnp.float32,
                )
                for key in keys[place : place + 2]
            ]
            for member in range(2):
                for group, (at, _) in enumerate(groups):
                    begin = member * pair_count + at
                    pieces = [jnp.where(keep, one[begin : begin + SUB], 0.0) for one in couple]
                    into = member * half + place * SUB
                    left[level, group, into : into + 2 * SUB, :] = jnp.concatenate(
                        pieces, axis=0
                    ).astype(jnp.bfloat16)
        for start in range(0, degrees, 256):
            stop = min(start + 256, degrees)
            low = 0 if start < 2 * pair_total else half
            high = 2 * half if stop > pair_total + 1 else half
            parts = []
            for group, (at, size) in enumerate(groups):
                values = legendre[at : at + size, :, start:stop].reshape(
                    size * lat_total, stop - start
                )
                sums = jnp.dot(
                    left[level, group, low:high, : size * lat_total],
                    values,
                    preferred_element_type=jnp.float32,
                ).reshape((high - low) // SUB, SUB, stop - start)
                if high - low > half:
                    shape = (SUB, stop - start)
                    slot = lax.broadcasted_iota(jnp.int32, shape, 1) + start
                    pair = lax.broadcasted_iota(jnp.int32, shape, 0) + (first_pair + at)
                    sums = jnp.where(
                        slot + pair < 2 * pair_total, sums[: len(keys)], sums[len(keys) :]
                    )
                parts.append(sums[:, :size])
            planes[level, :, :, :, start:stop] = (
                jnp.concatenate(parts, axis=1)
                .astype(jnp.bfloat16)
                .reshape(field_count + 1, 2, pair_count, stop - start)
            )
        copies.append(pltpu.make_async_copy(planes.at[level], out.at[level], sent.at[level]))
        copies[-1].start()
    for copy in copies:
        copy.wait()


def local(fields, rows_first, points, starts, weights, thickness, legendre):
    level_count, field_count, lat_count, lon_count = fields.shape
    pair_count, lat_total, degrees = legendre.shape
    owners = lax.axis_size("lat")
    couples = lon_count // (2 * LANES)
    blocks = 2 * couples
    columns = 2 * owners * pair_count
    up = [(i, i + 1) for i in range(owners - 1)]
    below = lax.ppermute(fields, "lat", up)
    above = lax.ppermute(fields, "lat", [(j, i) for i, j in up])

    scalar = pl.BlockSpec(memory_space=pltpu.SMEM)
    vector = pl.BlockSpec(memory_space=pltpu.VMEM)
    params = pltpu.CompilerParams(vmem_limit_bytes=LIMIT)
    shared = [
        pltpu.VMEM((lat_count, STENCIL, blocks, 1, LANES), jnp.int32),
        pltpu.VMEM((weights.size // LANES, LANES), jnp.float32),
    ]
    partial, table, twiddle = pl.pallas_call(
        functools.partial(near_kernel, pair_count * owners, pair_count),
        out_shape=(
            jax.ShapeDtypeStruct((lat_count, couples, SUB, 2 * LANES), jnp.float32),
            jax.ShapeDtypeStruct((lat_count, 2 * LANES, 2 * columns), jnp.bfloat16),
            jax.ShapeDtypeStruct((lat_count, couples, 2 * columns), jnp.float32),
        ),
        in_specs=[scalar, scalar, vector, vector, vector],
        out_specs=(vector, vector, vector),
        scratch_shapes=[
            pltpu.VMEM((fields.size // LANES, LANES), jnp.float32),
            pltpu.VMEM((lat_count, blocks + 2, SUB, LANES), jnp.float32),
            pltpu.VMEM((2, 16, 256), jnp.float32),
        ]
        + shared,
        compiler_params=params,
        cost_estimate=pl.CostEstimate(flops=10_000_000, bytes_accessed=4_000_000, transcendentals=0),
        name="near_rows",
    )(rows_first, points, fields, starts, weights)

    coefficients = pl.pallas_call(
        far_kernel,
        out_shape=jax.ShapeDtypeStruct((owners, 2 * SUB * lat_count, LANES), jnp.bfloat16),
        in_specs=[scalar, scalar] + [vector] * 7,
        out_specs=vector,
        scratch_shapes=[
            pltpu.VMEM((2, fields.size // LANES, LANES), jnp.float32),
            pltpu.VMEM((2 * lat_count, blocks + 2, SUB, LANES), jnp.float32),
            pltpu.VMEM((couples, SUB, 2 * LANES), jnp.float32),
        ]
        + shared
        + [pltpu.VMEM((2 * SUB, columns + LANES), jnp.float32)],
        compiler_params=params,
        name="far_rows",
    )(rows_first, points, below, above, starts, weights, partial, table, twiddle)

    received = lax.all_to_all(coefficients, "lat", split_axis=0, concat_axis=0, tiled=True)
    by_level = received.reshape(lat_total, 2, level_count, field_count, LANES).astype(jnp.float32)
    virtual = by_level[:, :, :, 2] + 0.61 * by_level[:, :, :, 3]
    total = jnp.sum(thickness[None, None, :, None] * virtual, axis=2).transpose(1, 0, 2)
    totals = lax.all_gather(total, "lev")

    out_shape = (level_count, field_count + 1, 2, pair_count, degrees)
    half = (field_count + 1) * 2 * SUB
    group_count = (pair_count + SUB - 1) // SUB
    return pl.pallas_call(
        functools.partial(legendre_kernel, level_count, field_count),
        out_shape=jax.ShapeDtypeStruct(out_shape, jnp.bfloat16),
        in_specs=[scalar, vector, vector, vector],
        out_specs=pl.BlockSpec(memory_space=pl.ANY),
        scratch_shapes=[
            pltpu.VMEM((lat_total * 2 * SUB, LANES), jnp.float32),
            pltpu.VMEM((level_count, group_count, 2 * half, SUB * lat_total), jnp.bfloat16),
            pltpu.VMEM(out_shape, jnp.bfloat16),
            pltpu.SemaphoreType.DMA((level_count,)),
        ],
        compiler_params=params,
        name="degree_sums",
    )(thickness, received, totals, legendre)


def solution(mesh):
    placed = (
        P("lev", None, "lat", None),
        P("lat"),
        P(),
        P("lat", None, None),
        P("lat", None, None, None),
        P("lev"),
        P("lat", None, None),
    )
    return jax.shard_map(
        local,
        mesh=mesh,
        in_specs=placed,
        out_specs=P("lev", None, None, "lat", None),
        check_vma=False,
    )
```

time: 47.7 us -> 42.3 us (0.89)
  Pallas kernels: 22.2 us -> 11.9 us
  local copies, waits for them, and re-layouts: 0.78 us -> 5.94 us
    unnamed x8 -> x18, local copies, waits for them, and re-layouts: 0.66 us -> 5.82 us
    pallas_call x1, Pallas kernels: 8.64 us -> 3.88 us  [local(): pl.pallas_call(far_kernel, out_shape=jax.ShapeDtypeStruct((owners, 2 * SU...]
    pallas_call x1, Pallas kernels: 6.65 us -> 3.46 us  [local(): pl.pallas_call(functools.partial(legendre_kernel, level_count, field_coun...]
    pallas_call x1, Pallas kernels: 6.96 us -> 4.54 us  [local(): pl.pallas_call(functools.partial(near_kernel, pair_count * owners, pair_c...]
  transfers between devices with their start and end apart: 2 -> 2, of which waited for: 0 -> 0; matrix products, arithmetic and copies ran while one was open for 0% -> 0% of each run, Pallas kernels for 15% -> 11%
where the time goes in v1:
time: 42.3 us; the launch traced here: 41.9 us
  blocking collectives  17.5 us (41%)
  Pallas kernels  11.9 us (28%)
  starting transfers between devices  6.39 us (15%)
  local copies, waits for them, and re-layouts  5.94 us (14%)
    all_to_all x1, blocking collectives, local(): lax.all_to_all(coefficients, 'lat', split_axis=0, concat_axis=0, tiled=True)  15.6 us
    unnamed x18, local copies, waits for them, and re-layouts  5.82 us
    ppermute x1, starting transfers between devices, local(): below = lax.ppermute(fields, 'lat', up)  5.1 us
    pallas_call x1, Pallas kernels, local(): pl.pallas_call(functools.partial(near_kernel, pair_count * owners, pair_c...  4.54 us
    pallas_call x1, Pallas kernels, local(): pl.pallas_call(far_kernel, out_shape=jax.ShapeDtypeStruct((owners, 2 * SU...  3.88 us
    pallas_call x1, Pallas kernels, local(): pl.pallas_call(functools.partial(legendre_kernel, level_count, field_coun...  3.46 us
    all_gather x1, blocking collectives, local(): totals = lax.all_gather(total, 'lev')  1.85 us
    ppermute x1, starting transfers between devices, local(): above = lax.ppermute(fields, 'lat', [(j, i) for i, j in up])  1.29 us
  transfers between devices with their start and end apart: 2, of which 0 were waited for; matrix products, arithmetic and copies ran while one was open for 0% of the time, Pallas kernels for 11%

profile of v1, /device:TPU:0, one launch (start us, length us, event | category | flops | bytes accessed | tf_op | source)
XLA Modules:
  0.0 41.9 jit_solution(5094069515616300871)
XLA Ops:
  0.0 0.0 copy-start
  0.0 5.1 %collective-permute-start = (bf16[2,4,2,2816]{3,2,1,0:T(2,128)(2,1)}, bf16[2,4,2,2816]{3,2,1,0:T(2,128)(2,1)S(1)}, u32[]{:S(2)}, u32[]{:S(2)}) collective-permute-start(bf16[2,4,2,2816]{3,2,1,0:T(2,128)(2,1)} %fields.1), channel_id=1, source_target_pairs={{0,2},{2,4},{4,6},{6,8},{8,10},{10,12},{12,14},{14,16},{16,18},{18... | collective-permute-start | bytes 270344 | tf_op jit(solution)/shard_map/ppermute | solution.py:322
  5.1 1.3 %collective-permute-start.1 = (bf16[2,4,2,2816]{3,2,1,0:T(2,128)(2,1)}, bf16[2,4,2,2816]{3,2,1,0:T(2,128)(2,1)S(1)}, u32[]{:S(2)}, u32[]{:S(2)}) collective-permute-start(bf16[2,4,2,2816]{3,2,1,0:T(2,128)(2,1)} %fields.1), channel_id=1, source_target_pairs={{2,0},{4,2},{6,4},{8,6},{10,8},{12,10},{14,12},{16,14},{18,16},{20... | collective-permute-start | bytes 270344 | tf_op jit(solution)/shard_map/ppermute | solution.py:323
  6.4 0.0 copy-start.1
  6.4 0.9 %copy-done.1 = bf16[2,4,4,2816]{3,2,1,0:T(4,128)(2,1)S(1)} copy-done((bf16[2,4,4,2816]{3,2,1,0:T(4,128)(2,1)S(1)}, bf16[2,4,4,2816]{3,2,1,0:T(4,128)(2,1)}, u32[]{:S(2)}) %copy-start.1) | copy-done | bytes 180248
  7.3 0.0 copy-start.3
  7.3 0.9 %copy-done.3 = s32[2,4,2816]{2,1,0:T(4,128)S(1)} copy-done((s32[2,4,2816]{2,1,0:T(4,128)S(1)}, s32[2,4,2816]{2,1,0:T(4,128)}, u32[]{:S(2)}) %copy-start.3) | copy-done | bytes 90136
  8.2 0.9 %copy-done.5 = bf16[2,4,2,2816]{3,2,1,0:T(2,128)(2,1)S(1)} copy-done((bf16[2,4,2,2816]{3,2,1,0:T(2,128)(2,1)S(1)}, bf16[2,4,2,2816]{3,2,1,0:T(2,128)(2,1)}, u32[]{:S(2)}) %copy-start.5) | copy-done | bytes 90136
  9.1 0.7 %copy-done.6 = s32[2]{0:T(128)S(1)} copy-done((s32[2]{0:T(128)S(1)}, s32[2]{0:T(128)}, u32[]{:S(2)}) %copy-start.6) | copy-done | bytes 32
  9.8 0.7 %copy-done.7 = s32[32]{0:T(128)S(1)} copy-done((s32[32]{0:T(128)S(1)}, s32[32]{0:T(128)}, u32[]{:S(2)}) %copy-start.7) | copy-done | bytes 152
  10.4 4.5 %near_rows.1 = (f32[2,11,8,256]{3,2,1,0:T(8,128)S(1)}, bf16[2,256,2560]{2,1,0:T(8,128)(2,1)S(1)}, f32[2,11,2560]{2,1,0:T(8,128)S(1)}) custom-call(s32[2]{0:T(128)S(1)} %copy-done.6, s32[32]{0:T(128)S(1)} %copy-done.7, bf16[2,4,2,2816]{3,2,1,0:T(2,128)(2,1)S(1)} %copy-done.5, s32[2,4,2816]{2,1,0:T(4,128)S(1)} %copy-done.3, bf16[2,4,4,2816]{3,2,1,0:T(4,128)(2,1)S(1)} %copy-done.1), custom_call_target="tpu_custom_call" | custom-call | flops 10000000 | bytes 4000000 | tf_op jit(solution)/shard_map/near_rows/pallas_call | solution.py:332
  15.0 0.0 collective-permute-done.below
  15.0 0.0 collective-permute-done.1.above
  15.0 0.0 copy-start.2
  15.0 0.9 %copy-done.2 = bf16[2,4,4,2816]{3,2,1,0:T(4,128)(2,1)S(1)} copy-done((bf16[2,4,4,2816]{3,2,1,0:T(4,128)(2,1)S(1)}, bf16[2,4,4,2816]{3,2,1,0:T(4,128)(2,1)}, u32[]{:S(2)}) %copy-start.2) | copy-done | bytes 180248
  15.9 0.9 %copy-done.4 = s32[2,4,2816]{2,1,0:T(4,128)S(1)} copy-done((s32[2,4,2816]{2,1,0:T(4,128)S(1)}, s32[2,4,2816]{2,1,0:T(4,128)}, u32[]{:S(2)}) %copy-start.4) | copy-done | bytes 90136
  16.8 3.9 %far_rows.1 = bf16[16,32,128]{2,1,0:T(8,128)(2,1)S(1)} custom-call(s32[2]{0:T(128)S(1)} %copy-done.6, s32[32]{0:T(128)S(1)} %copy-done.7, bf16[2,4,2,2816]{3,2,1,0:T(2,128)(2,1)S(1)} %collective-permute-done.below, bf16[2,4,2,2816]{3,2,1,0:T(2,128)(2,1)S(1)} %collective-permute-done.1.above, s32[2,4,2816]{2,1,0:T(4,128)S(1)} %copy-done.4, ...), custom_call_target="tpu_custom_call" | custom-call | tf_op jit(solution)/shard_map/far_rows/pallas_call | solution.py:352
  20.7 15.6 %all_to_all.5.received = bf16[16,32,128]{2,1,0:T(8,128)(2,1)S(1)} all-to-all(bf16[16,32,128]{2,1,0:T(8,128)(2,1)S(1)} %far_rows.1), channel_id=1, replica_groups=mesh['lat'=16,'lev'=2] {'lat'}, dimensions={0} | all-to-all | bytes 262144 | tf_op jit(solution)/shard_map/all_to_all | solution.py:368
  36.3 0.1 fusion.1
  36.4 0.0 copy-done.8
  36.4 0.2 fusion
  36.6 1.9 %all-gather = f32[4,32,128]{2,1,0:T(8,128)S(1)} all-gather(f32[2,32,128]{2,1,0:T(8,128)S(1)} %copy.10), channel_id=2, replica_groups=mesh['lat'=16,'lev'=2] {'lev'}, dimensions={0}, use_global_device_ids=true | all-gather | bytes 98304 | tf_op jit(solution)/shard_map/all_gather | solution.py:372
  38.5 0.0 copy-done
  38.5 3.5 %degree_sums.1 = bf16[2,5,2,40,1281]{4,3,2,1,0:T(8,128)(2,1)} custom-call(f32[2]{0:T(128)S(1)} %copy-done.8, bf16[16,32,128]{2,1,0:T(8,128)(2,1)S(1)} %all_to_all.5.received, f32[2,2,32,128]{3,2,1,0:T(8,128)S(1)} %bitcast.11, bf16[40,32,1281]{2,1,0:T(8,128)(2,1)S(1)} %copy-done), custom_call_target="tpu_custom_call" | custom-call | tf_op jit(solution)/shard_map/degree_sums/pallas_call | solution.py:377
  (6 shorter events, 0.0 us)
Async XLA Ops:
  0.0 38.5 %copy-start = (bf16[40,32,1281]{2,1,0:T(8,128)(2,1)S(1)}, bf16[40,32,1281]{2,1,0:T(8,128)(2,1)}, u32[]{:S(2)}) copy-start(bf16[40,32,1281]{2,1,0:T(8,128)(2,1)} %legendre.1) | copy-start | bytes 9838084
  0.0 15.0 %collective-permute-start = (bf16[2,4,2,2816]{3,2,1,0:T(2,128)(2,1)}, bf16[2,4,2,2816]{3,2,1,0:T(2,128)(2,1)S(1)}, u32[]{:S(2)}, u32[]{:S(2)}) collective-permute-start(bf16[2,4,2,2816]{3,2,1,0:T(2,128)(2,1)} %fields.1), channel_id=1, source_target_pairs={{0,2},{2,4},{4,6},{6,8},{8,10},{10,12},{12,14},{14,16},{16,18},{18... | collective-permute-start | bytes 270344 | tf_op jit(solution)/shard_map/ppermute | solution.py:322
  5.1 9.9 %collective-permute-start.1 = (bf16[2,4,2,2816]{3,2,1,0:T(2,128)(2,1)}, bf16[2,4,2,2816]{3,2,1,0:T(2,128)(2,1)S(1)}, u32[]{:S(2)}, u32[]{:S(2)}) collective-permute-start(bf16[2,4,2,2816]{3,2,1,0:T(2,128)(2,1)} %fields.1), channel_id=1, source_target_pairs={{2,0},{4,2},{6,4},{8,6},{10,8},{12,10},{14,12},{16,14},{18,16},{20... | collective-permute-start | bytes 270344 | tf_op jit(solution)/shard_map/ppermute | solution.py:323
  6.4 0.9 %copy-start.1 = (bf16[2,4,4,2816]{3,2,1,0:T(4,128)(2,1)S(1)}, bf16[2,4,4,2816]{3,2,1,0:T(4,128)(2,1)}, u32[]{:S(2)}) copy-start(bf16[2,4,4,2816]{3,2,1,0:T(4,128)(2,1)} %weights.3) | copy-start | bytes 540676
  7.3 0.9 %copy-start.3 = (s32[2,4,2816]{2,1,0:T(4,128)S(1)}, s32[2,4,2816]{2,1,0:T(4,128)}, u32[]{:S(2)}) copy-start(s32[2,4,2816]{2,1,0:T(4,128)} %starts.3) | copy-start | bytes 270340
  8.2 0.9 %copy-start.5 = (bf16[2,4,2,2816]{3,2,1,0:T(2,128)(2,1)S(1)}, bf16[2,4,2,2816]{3,2,1,0:T(2,128)(2,1)}, u32[]{:S(2)}) copy-start(bf16[2,4,2,2816]{3,2,1,0:T(2,128)(2,1)} %fields.1) | copy-start | bytes 270340
  9.1 0.7 %copy-start.6 = (s32[2]{0:T(128)S(1)}, s32[2]{0:T(128)}, u32[]{:S(2)}) copy-start(s32[2]{0:T(128)} %rows_first.3) | copy-start | bytes 28
  9.8 0.7 %copy-start.7 = (s32[32]{0:T(128)S(1)}, s32[32]{0:T(128)}, u32[]{:S(2)}) copy-start(s32[32]{0:T(128)} %points.3) | copy-start | bytes 388
  15.0 0.9 %copy-start.2 = (bf16[2,4,4,2816]{3,2,1,0:T(4,128)(2,1)S(1)}, bf16[2,4,4,2816]{3,2,1,0:T(4,128)(2,1)}, u32[]{:S(2)}) copy-start(bf16[2,4,4,2816]{3,2,1,0:T(4,128)(2,1)} %weights.3) | copy-start | bytes 540676
  15.9 0.9 %copy-start.4 = (s32[2,4,2816]{2,1,0:T(4,128)S(1)}, s32[2,4,2816]{2,1,0:T(4,128)}, u32[]{:S(2)}) copy-start(s32[2,4,2816]{2,1,0:T(4,128)} %starts.3) | copy-start | bytes 270340
  16.8 19.6 %copy-start.8 = (f32[2]{0:T(128)S(1)}, f32[2]{0:T(128)}, u32[]{:S(2)}) copy-start(f32[2]{0:T(128)} %thickness.1) | copy-start | bytes 28

commit v2 on v1

--- a/solution.py
+++ b/solution.py
@@ -105,25 +105,29 @@
 
 
 def near_kernel(
-    pair_total, pair_count, rows_first, points, fields, starts, weights,
-    partial, table, twiddle, lines, ext, fine, begins, factors,
+    pair_total, pair_count, rows_first_far, points_far, fields_far, starts_far, weights_far,
+    partial, table, twiddle, begins, factors,
+    rows_first, points, fields, starts, weights, lines, ext, fine, arrived,
 ):
     lat_count, couples = partial.shape[:2]
     lon = 2 * couples * LANES
     columns = table.shape[2] // 2
     first_lat = lax.axis_index("lat") * lat_count
-    spread_rows(starts, begins)
-    spread_lines(weights, factors)
-    spread_lines(fields, lines)
-    for latitude in range(lat_count):
-        extend(lines, latitude, lat_count, lon - points[first_lat + latitude], ext, latitude)
-    for latitude in range(lat_count):
-        mine = first_lat - rows_first[latitude]
-        picks = [(mine + row, row) for row in range(lat_count)]
-        for couple in range(couples):
-            totals = gathered(couple, latitude, picks, ext, begins, factors)
-            for side in range(2):
-                partial[latitude, couple, :, side * LANES : (side + 1) * LANES] = totals[side]
+    fetches = [
+        pltpu.make_async_copy(source, target, arrived.at[place])
+        for place, (source, target) in enumerate(
+            (
+                (points_far, points),
+                (rows_first_far, rows_first),
+                (starts_far, starts),
+                (weights_far, weights),
+                (fields_far, fields),
+            )
+        )
+    ]
+    for fetch in fetches:
+        fetch.start()
+    fetches[0].wait()
     width = 256
     for latitude in range(lat_count):
         total = jnp.full((1, 1), points[first_lat + latitude], jnp.int32).astype(jnp.float32)
@@ -155,22 +159,43 @@
             return carry
 
         lax.fori_loop(0, columns // width, chunk, 0)
+    for fetch in fetches[1:]:
+        fetch.wait()
+    spread_rows(starts, begins)
+    spread_lines(weights, factors)
+    spread_lines(fields, lines)
+    for latitude in range(lat_count):
+        extend(lines, latitude, lat_count, lon - points[first_lat + latitude], ext, latitude)
+    for latitude in range(lat_count):
+        mine = first_lat - rows_first[latitude]
+        picks = [(mine + row, row) for row in range(lat_count)]
+        for couple in range(couples):
+            totals = gathered(couple, latitude, picks, ext, begins, factors)
+            for side in range(2):
+                partial[latitude, couple, :, side * LANES : (side + 1) * LANES] = totals[side]
 
 
 def far_kernel(
-    rows_first, points, below, above, starts, weights, partial, table, twiddle,
-    out, lines, ext, grid, begins, factors, waves,
+    rows_first_far, points_far, below, above, begins, factors, partial, table, twiddle,
+    out, rows_first, points, lines, ext, grid, waves, arrived,
 ):
+    fetches = [
+        pltpu.make_async_copy(points_far, points, arrived.at[0]),
+        pltpu.make_async_copy(rows_first_far, rows_first, arrived.at[1]),
+    ]
+    for fetch in fetches:
+        fetch.start()
     lat_count, couples = partial.shape[:2]
     lon = 2 * couples * LANES
     columns = table.shape[2] // 2
     owners = out.shape[0]
     first_lat = lax.axis_index("lat") * lat_count
     lat_total = points.shape[0]
-    spread_rows(starts, begins)
-    spread_lines(weights, factors)
     for side, source in enumerate((below, above)):
         spread_lines(source, lines.at[side])
+    for fetch in fetches:
+        fetch.wait()
+    for side in range(2):
         for row in range(lat_count):
             if side == 0:
                 place = jnp.maximum(first_lat - lat_count + row, 0)
@@ -311,6 +336,10 @@
         copy.wait()
 
 
+def held(value):
+    return pltpu.with_memory_space_constraint(value, pltpu.HBM)
+
+
 def local(fields, rows_first, points, starts, weights, thickness, legendre):
     level_count, field_count, lat_count, lon_count = fields.shape
     pair_count, lat_total, degrees = legendre.shape
@@ -325,45 +354,53 @@
     scalar = pl.BlockSpec(memory_space=pltpu.SMEM)
     vector = pl.BlockSpec(memory_space=pltpu.VMEM)
     params = pltpu.CompilerParams(vmem_limit_bytes=LIMIT)
-    shared = [
-        pltpu.VMEM((lat_count, STENCIL, blocks, 1, LANES), jnp.int32),
-        pltpu.VMEM((weights.size // LANES, LANES), jnp.float32),
+    remote = pl.BlockSpec(memory_space=pltpu.HBM)
+    scalars = [
+        pltpu.SMEM(rows_first.shape, jnp.int32),
+        pltpu.SMEM(points.shape, jnp.int32),
     ]
-    partial, table, twiddle = pl.pallas_call(
+    partial, table, twiddle, begins, factors = pl.pallas_call(
         functools.partial(near_kernel, pair_count * owners, pair_count),
         out_shape=(
             jax.ShapeDtypeStruct((lat_count, couples, SUB, 2 * LANES), jnp.float32),
             jax.ShapeDtypeStruct((lat_count, 2 * LANES, 2 * columns), jnp.bfloat16),
             jax.ShapeDtypeStruct((lat_count, couples, 2 * columns), jnp.float32),
+            jax.ShapeDtypeStruct((lat_count, STENCIL, blocks, 1, LANES), jnp.int32),
+            jax.ShapeDtypeStruct((weights.size // LANES, LANES), jnp.float32),
         ),
-        in_specs=[scalar, scalar, vector, vector, vector],
-        out_specs=(vector, vector, vector),
-        scratch_shapes=[
+        in_specs=[remote] * 5,
+        out_specs=(vector,) * 5,
+        scratch_shapes=scalars
+        + [
+            pltpu.VMEM(fields.shape, fields.dtype),
+            pltpu.VMEM(starts.shape, starts.dtype),
+            pltpu.VMEM(weights.shape, weights.dtype),
             pltpu.VMEM((fields.size // LANES, LANES), jnp.float32),
             pltpu.VMEM((lat_count, blocks + 2, SUB, LANES), jnp.float32),
             pltpu.VMEM((2, 16, 256), jnp.float32),
-        ]
-        + shared,
+            pltpu.SemaphoreType.DMA((5,)),
+        ],
         compiler_params=params,
         cost_estimate=pl.CostEstimate(flops=10_000_000, bytes_accessed=4_000_000, transcendentals=0),
         name="near_rows",
-    )(rows_first, points, fields, starts, weights)
+    )(*(held(value) for value in (rows_first, points, fields, starts, weights)))
 
     coefficients = pl.pallas_call(
         far_kernel,
         out_shape=jax.ShapeDtypeStruct((owners, 2 * SUB * lat_count, LANES), jnp.bfloat16),
-        in_specs=[scalar, scalar] + [vector] * 7,
+        in_specs=[remote] * 2 + [vector] * 7,
         out_specs=vector,
-        scratch_shapes=[
+        scratch_shapes=scalars
+        + [
             pltpu.VMEM((2, fields.size // LANES, LANES), jnp.float32),
             pltpu.VMEM((2 * lat_count, blocks + 2, SUB, LANES), jnp.float32),
             pltpu.VMEM((couples, SUB, 2 * LANES), jnp.float32),
-        ]
-        + shared
-        + [pltpu.VMEM((2 * SUB, columns + LANES), jnp.float32)],
+            pltpu.VMEM((2 * SUB, columns + LANES), jnp.float32),
+            pltpu.SemaphoreType.DMA((2,)),
+        ],
         compiler_params=params,
         name="far_rows",
-    )(rows_first, points, below, above, starts, weights, partial, table, twiddle)
+    )(held(rows_first), held(points), below, above, begins, factors, partial, table, twiddle)
 
     received = lax.all_to_all(coefficients, "lat", split_axis=0, concat_axis=0, tiled=True)
     by_level = received.reshape(lat_total, 2, level_count, field_count, LANES).astype(jnp.float32)

time: 42.3 us -> 36.9 us (0.87)
  local copies, waits for them, and re-layouts: 5.94 us -> 0.13 us
  waiting for transfers between devices: 0.01 us -> 0.54 us
    unnamed x18 -> x4, local copies, waits for them, and re-layouts: 5.82 us -> 0.01 us
    ppermute x1, waiting for transfers between devices: 0.01 us -> 0.53 us  [local(): above = lax.ppermute(fields, 'lat', [(j, i) for i, j in up])]
  transfers between devices with their start and end apart: 2 -> 2, of which waited for: 0 -> 1; matrix products, arithmetic and copies ran while one was open for 0% -> 0% of each run, Pallas kernels for 11% -> 13%
where the time goes in v2:
time: 36.9 us; the launch traced here: 36.7 us
  blocking collectives  17.1 us (46%)
  Pallas kernels  12.3 us (33%)
  starting transfers between devices  6.39 us (17%)
  waiting for transfers between devices  0.54 us (1%)
    all_to_all x1, blocking collectives, local(): lax.all_to_all(coefficients, 'lat', split_axis=0, concat_axis=0, tiled=True)  15.2 us
    ppermute x1, starting transfers between devices, local(): below = lax.ppermute(fields, 'lat', up)  5.1 us
    pallas_call x1, Pallas kernels, local(): pl.pallas_call(functools.partial(near_kernel, pair_count * owners, pair_c...  4.78 us
    pallas_call x1, Pallas kernels, local(): pl.pallas_call(far_kernel, out_shape=jax.ShapeDtypeStruct((owners, 2 * SU...  3.97 us
    pallas_call x1, Pallas kernels, local(): pl.pallas_call(functools.partial(legendre_kernel, level_count, field_coun...  3.52 us
    all_gather x1, blocking collectives, local(): totals = lax.all_gather(total, 'lev')  1.85 us
    ppermute x1, starting transfers between devices, local(): above = lax.ppermute(fields, 'lat', [(j, i) for i, j in up])  1.29 us
  transfers between devices with their start and end apart: 2, of which 1 were waited for; matrix products, arithmetic and copies ran while one was open for 0% of the time, Pallas kernels for 13%

profile of v2, /device:TPU:0, one launch (start us, length us, event | category | flops | bytes accessed | tf_op | source)
XLA Modules:
  0.0 36.7 jit_solution(6121040637324950684)
XLA Ops:
  0.0 0.0 copy-start.1
  0.0 0.0 copy-start
  0.0 5.1 %collective-permute-start = (bf16[2,4,2,2816]{3,2,1,0:T(2,128)(2,1)}, bf16[2,4,2,2816]{3,2,1,0:T(2,128)(2,1)S(1)}, u32[]{:S(2)}, u32[]{:S(2)}) collective-permute-start(bf16[2,4,2,2816]{3,2,1,0:T(2,128)(2,1)} %fields_far.1), channel_id=1, source_target_pairs={{0,2},{2,4},{4,6},{6,8},{8,10},{10,12},{12,14},{14,16},{16,18},{18... | collective-permute-start | bytes 270344 | tf_op jit(solution)/shard_map/ppermute | solution.py:351
  5.1 1.3 %collective-permute-start.1 = (bf16[2,4,2,2816]{3,2,1,0:T(2,128)(2,1)}, bf16[2,4,2,2816]{3,2,1,0:T(2,128)(2,1)S(1)}, u32[]{:S(2)}, u32[]{:S(2)}) collective-permute-start(bf16[2,4,2,2816]{3,2,1,0:T(2,128)(2,1)} %fields_far.1), channel_id=1, source_target_pairs={{2,0},{4,2},{6,4},{8,6},{10,8},{12,10},{14,12},{16,14},{18,16},{20... | collective-permute-start | bytes 270344 | tf_op jit(solution)/shard_map/ppermute | solution.py:352
  6.4 4.8 %near_rows.1 = (f32[2,11,8,256]{3,2,1,0:T(8,128)S(1)}, bf16[2,256,2560]{2,1,0:T(8,128)(2,1)S(1)}, f32[2,11,2560]{2,1,0:T(8,128)S(1)}, s32[2,4,22,1,128]{4,3,2,1,0:T(1,128)S(1)}, f32[704,128]{1,0:T(8,128)S(1)}) custom-call(s32[2]{0:T(128)} %rows_first_far.3, s32[32]{0:T(128)} %points_far.3, bf16[2,4,2,2816]{3,2,1,0:T(2,128)(2,1)} %fields_far.1, ...), custom_call_target="tpu_custom_call" | custom-call | flops 10000000 | bytes 4000000 | tf_op jit(solution)/shard_map/near_rows/pallas_call | solution.py:362
  11.2 0.0 collective-permute-done.below
  11.2 0.5 %collective-permute-done.1.above = bf16[2,4,2,2816]{3,2,1,0:T(2,128)(2,1)S(1)} collective-permute-done((bf16[2,4,2,2816]{3,2,1,0:T(2,128)(2,1)}, bf16[2,4,2,2816]{3,2,1,0:T(2,128)(2,1)S(1)}, u32[]{:S(2)}, u32[]{:S(2)}) %collective-permute-start.1) | collective-permute-done | bytes 90144 | tf_op jit(solution)/shard_map/ppermute | solution.py:352
  11.7 4.0 %far_rows.1 = bf16[16,32,128]{2,1,0:T(8,128)(2,1)S(1)} custom-call(s32[2]{0:T(128)} %rows_first_far.3, s32[32]{0:T(128)} %points_far.3, bf16[2,4,2,2816]{3,2,1,0:T(2,128)(2,1)S(1)} %collective-permute-done.below, bf16[2,4,2,2816]{3,2,1,0:T(2,128)(2,1)S(1)} %collective-permute-done.1.above, s32[2,4,22,1,128]{4,3,2,1,0:T(1,128)S(1)} %get-tuple-element.10.begins, ...), custom_call_target="tpu_custom_call" | custom-call | tf_op jit(solution)/shard_map/far_rows/pallas_call | solution.py:388
  15.7 15.2 %all_to_all.5.received = bf16[16,32,128]{2,1,0:T(8,128)(2,1)S(1)} all-to-all(bf16[16,32,128]{2,1,0:T(8,128)(2,1)S(1)} %far_rows.1), channel_id=1, replica_groups=mesh['lat'=16,'lev'=2] {'lat'}, dimensions={0} | all-to-all | bytes 262144 | tf_op jit(solution)/shard_map/all_to_all | solution.py:405
  31.0 0.1 fusion.1
  31.1 0.0 copy-done.1
  31.1 0.2 fusion
  31.3 1.9 %all-gather = f32[4,32,128]{2,1,0:T(8,128)S(1)} all-gather(f32[2,32,128]{2,1,0:T(8,128)S(1)} %copy.10), channel_id=2, replica_groups=mesh['lat'=16,'lev'=2] {'lev'}, dimensions={0}, use_global_device_ids=true | all-gather | bytes 98304 | tf_op jit(solution)/shard_map/all_gather | solution.py:409
  33.1 0.0 copy-done
  33.1 3.5 %degree_sums.1 = bf16[2,5,2,40,1281]{4,3,2,1,0:T(8,128)(2,1)} custom-call(f32[2]{0:T(128)S(1)} %copy-done.1, bf16[16,32,128]{2,1,0:T(8,128)(2,1)S(1)} %all_to_all.5.received, f32[2,2,32,128]{3,2,1,0:T(8,128)S(1)} %bitcast.11, bf16[40,32,1281]{2,1,0:T(8,128)(2,1)S(1)} %copy-done), custom_call_target="tpu_custom_call" | custom-call | tf_op jit(solution)/shard_map/degree_sums/pallas_call | solution.py:414
  (1 shorter events, 0.0 us)
Async XLA Ops:
  0.0 31.1 %copy-start.1 = (f32[2]{0:T(128)S(1)}, f32[2]{0:T(128)}, u32[]{:S(2)}) copy-start(f32[2]{0:T(128)} %thickness.1) | copy-start | bytes 28
  0.0 33.1 %copy-start = (bf16[40,32,1281]{2,1,0:T(8,128)(2,1)S(1)}, bf16[40,32,1281]{2,1,0:T(8,128)(2,1)}, u32[]{:S(2)}) copy-start(bf16[40,32,1281]{2,1,0:T(8,128)(2,1)} %legendre.1) | copy-start | bytes 9838084
  0.0 11.2 %collective-permute-start = (bf16[2,4,2,2816]{3,2,1,0:T(2,128)(2,1)}, bf16[2,4,2,2816]{3,2,1,0:T(2,128)(2,1)S(1)}, u32[]{:S(2)}, u32[]{:S(2)}) collective-permute-start(bf16[2,4,2,2816]{3,2,1,0:T(2,128)(2,1)} %fields_far.1), channel_id=1, source_target_pairs={{0,2},{2,4},{4,6},{6,8},{8,10},{10,12},{12,14},{14,16},{16,18},{18... | collective-permute-start | bytes 270344 | tf_op jit(solution)/shard_map/ppermute | solution.py:351
  5.1 6.6 %collective-permute-start.1 = (bf16[2,4,2,2816]{3,2,1,0:T(2,128)(2,1)}, bf16[2,4,2,2816]{3,2,1,0:T(2,128)(2,1)S(1)}, u32[]{:S(2)}, u32[]{:S(2)}) collective-permute-start(bf16[2,4,2,2816]{3,2,1,0:T(2,128)(2,1)} %fields_far.1), channel_id=1, source_target_pairs={{2,0},{4,2},{6,4},{8,6},{10,8},{12,10},{14,12},{16,14},{18,16},{20... | collective-permute-start | bytes 270344 | tf_op jit(solution)/shard_map/ppermute | solution.py:352

commit v3 on v2

--- a/solution.py
+++ b/solution.py
@@ -176,7 +176,7 @@
 
 
 def far_kernel(
-    rows_first_far, points_far, below, above, begins, factors, partial, table, twiddle,
+    rows_first_far, points_far, near_side, far_side, begins, factors, partial, table, twiddle,
     out, rows_first, points, lines, ext, grid, waves, arrived,
 ):
     fetches = [
@@ -191,8 +191,9 @@
     owners = out.shape[0]
     first_lat = lax.axis_index("lat") * lat_count
     lat_total = points.shape[0]
-    for side, source in enumerate((below, above)):
-        spread_lines(source, lines.at[side])
+    toward = 1 - lax.axis_index("lat") % 2
+    spread_lines(near_side, lines.at[toward])
+    spread_lines(far_side, lines.at[1 - toward])
     for fetch in fetches:
         fetch.wait()
     for side in range(2):
@@ -347,9 +348,10 @@
     couples = lon_count // (2 * LANES)
     blocks = 2 * couples
     columns = 2 * owners * pair_count
-    up = [(i, i + 1) for i in range(owners - 1)]
-    below = lax.ppermute(fields, "lat", up)
-    above = lax.ppermute(fields, "lat", [(j, i) for i, j in up])
+    sides = []
+    for first in range(2):
+        edges = [(i, i + 1) for i in range(first, owners - 1, 2)]
+        sides.append(lax.ppermute(fields, "lat", edges + [(j, i) for i, j in edges]))
 
     scalar = pl.BlockSpec(memory_space=pltpu.SMEM)
     vector = pl.BlockSpec(memory_space=pltpu.VMEM)
@@ -400,7 +402,7 @@
         ],
         compiler_params=params,
         name="far_rows",
-    )(held(rows_first), held(points), below, above, begins, factors, partial, table, twiddle)
+    )(held(rows_first), held(points), *sides, begins, factors, partial, table, twiddle)
 
     received = lax.all_to_all(coefficients, "lat", split_axis=0, concat_axis=0, tiled=True)
     by_level = received.reshape(lat_total, 2, level_count, field_count, LANES).astype(jnp.float32)

time: 36.9 us -> 34.5 us (0.935)
  starting transfers between devices: 6.39 us -> 3.59 us
  blocking collectives: 17.1 us -> 18.1 us
  waiting for transfers between devices: 0.54 us -> 0.01 us
    ppermute x2, starting transfers between devices: 6.39 us -> 3.59 us  [local(): lax.ppermute(fields, 'lat', edges + [(j, i) for i, j in edges])]
    all_to_all x1, blocking collectives: 15.2 us -> 16.2 us  [local(): lax.all_to_all(coefficients, 'lat', split_axis=0, concat_axis=0, tiled=True)]
    ppermute x2, waiting for transfers between devices: 0.54 us -> 0.01 us  [local(): lax.ppermute(fields, 'lat', edges + [(j, i) for i, j in edges])]
  transfers between devices with their start and end apart: 2 -> 2, of which waited for: 1 -> 0; matrix products, arithmetic and copies ran while one was open for 0% -> 0% of each run, Pallas kernels for 13% -> 14%
where the time goes in v3:
time: 34.5 us; the launch traced here: 34.3 us
  blocking collectives  18.1 us (52%)
  Pallas kernels  12.3 us (36%)
  starting transfers between devices  3.59 us (10%)
    all_to_all x1, blocking collectives, local(): lax.all_to_all(coefficients, 'lat', split_axis=0, concat_axis=0, tiled=True)  16.2 us
    pallas_call x1, Pallas kernels, local(): pl.pallas_call(functools.partial(near_kernel, pair_count * owners, pair_c...  4.78 us
    pallas_call x1, Pallas kernels, local(): pl.pallas_call(far_kernel, out_shape=jax.ShapeDtypeStruct((owners, 2 * SU...  3.98 us
    ppermute x2, starting transfers between devices, local(): lax.ppermute(fields, 'lat', edges + [(j, i) for i, j in edges])  3.59 us
    pallas_call x1, Pallas kernels, local(): pl.pallas_call(functools.partial(legendre_kernel, level_count, field_coun...  3.52 us
    all_gather x1, blocking collectives, local(): totals = lax.all_gather(total, 'lev')  1.85 us
  transfers between devices with their start and end apart: 2, of which 0 were waited for; matrix products, arithmetic and copies ran while one was open for 0% of the time, Pallas kernels for 14%

profile of v3, /device:TPU:0, one launch (start us, length us, event | category | flops | bytes accessed | tf_op | source)
XLA Modules:
  0.0 34.3 jit_solution(16845318352652184013)
XLA Ops:
  0.0 0.0 copy-start.1
  0.0 0.0 copy-start
  0.0 2.9 %collective-permute-start = (bf16[2,4,2,2816]{3,2,1,0:T(2,128)(2,1)}, bf16[2,4,2,2816]{3,2,1,0:T(2,128)(2,1)S(1)}, u32[]{:S(2)}, u32[]{:S(2)}) collective-permute-start(bf16[2,4,2,2816]{3,2,1,0:T(2,128)(2,1)} %fields_far.1), channel_id=1, source_target_pairs={{0,2},{4,6},{8,10},{12,14},{16,18},{20,22},{24,26},{28,30},{2,0},{... | collective-permute-start | bytes 270344 | tf_op jit(solution)/shard_map/ppermute | solution.py:354
  2.9 0.7 %collective-permute-start.1 = (bf16[2,4,2,2816]{3,2,1,0:T(2,128)(2,1)}, bf16[2,4,2,2816]{3,2,1,0:T(2,128)(2,1)S(1)}, u32[]{:S(2)}, u32[]{:S(2)}) collective-permute-start(bf16[2,4,2,2816]{3,2,1,0:T(2,128)(2,1)} %fields_far.1), channel_id=1, source_target_pairs={{2,4},{6,8},{10,12},{14,16},{18,20},{22,24},{26,28},{4,2},{8,6},{1... | collective-permute-start | bytes 270344 | tf_op jit(solution)/shard_map/ppermute | solution.py:354
  3.6 4.8 %near_rows.1 = (f32[2,11,8,256]{3,2,1,0:T(8,128)S(1)}, bf16[2,256,2560]{2,1,0:T(8,128)(2,1)S(1)}, f32[2,11,2560]{2,1,0:T(8,128)S(1)}, s32[2,4,22,1,128]{4,3,2,1,0:T(1,128)S(1)}, f32[704,128]{1,0:T(8,128)S(1)}) custom-call(s32[2]{0:T(128)} %rows_first_far.3, s32[32]{0:T(128)} %points_far.3, bf16[2,4,2,2816]{3,2,1,0:T(2,128)(2,1)} %fields_far.1, ...), custom_call_target="tpu_custom_call" | custom-call | flops 10000000 | bytes 4000000 | tf_op jit(solution)/shard_map/near_rows/pallas_call | solution.py:364
  8.4 0.0 collective-permute-done.near_side
  8.4 0.0 collective-permute-done.1.far_side
  8.4 4.0 %far_rows.1 = bf16[16,32,128]{2,1,0:T(8,128)(2,1)S(1)} custom-call(s32[2]{0:T(128)} %rows_first_far.3, s32[32]{0:T(128)} %points_far.3, bf16[2,4,2,2816]{3,2,1,0:T(2,128)(2,1)S(1)} %collective-permute-done.near_side, bf16[2,4,2,2816]{3,2,1,0:T(2,128)(2,1)S(1)} %collective-permute-done.1.far_side, s32[2,4,22,1,128]{4,3,2,1,0:T(1,128)S(1)} %get-tuple-element.10.begins, ...), custom_call_target="tpu_custom_call" | custom-call | tf_op jit(solution)/shard_map/far_rows/pallas_call | solution.py:390
  12.4 16.2 %all_to_all.5.received = bf16[16,32,128]{2,1,0:T(8,128)(2,1)S(1)} all-to-all(bf16[16,32,128]{2,1,0:T(8,128)(2,1)S(1)} %far_rows.1), channel_id=1, replica_groups=mesh['lat'=16,'lev'=2] {'lat'}, dimensions={0} | all-to-all | bytes 262144 | tf_op jit(solution)/shard_map/all_to_all | solution.py:407
  28.6 0.1 fusion.1
  28.8 0.0 copy-done.1
  28.8 0.2 fusion
  29.0 1.9 %all-gather = f32[4,32,128]{2,1,0:T(8,128)S(1)} all-gather(f32[2,32,128]{2,1,0:T(8,128)S(1)} %copy.10), channel_id=2, replica_groups=mesh['lat'=16,'lev'=2] {'lev'}, dimensions={0}, use_global_device_ids=true | all-gather | bytes 98304 | tf_op jit(solution)/shard_map/all_gather | solution.py:411
  30.8 0.0 copy-done
  30.8 3.5 %degree_sums.1 = bf16[2,5,2,40,1281]{4,3,2,1,0:T(8,128)(2,1)} custom-call(f32[2]{0:T(128)S(1)} %copy-done.1, bf16[16,32,128]{2,1,0:T(8,128)(2,1)S(1)} %all_to_all.5.received, f32[2,2,32,128]{3,2,1,0:T(8,128)S(1)} %bitcast.11, bf16[40,32,1281]{2,1,0:T(8,128)(2,1)S(1)} %copy-done), custom_call_target="tpu_custom_call" | custom-call | tf_op jit(solution)/shard_map/degree_sums/pallas_call | solution.py:416
  (1 shorter events, 0.0 us)
Async XLA Ops:
  0.0 28.8 %copy-start.1 = (f32[2]{0:T(128)S(1)}, f32[2]{0:T(128)}, u32[]{:S(2)}) copy-start(f32[2]{0:T(128)} %thickness.1) | copy-start | bytes 28
  0.0 30.8 %copy-start = (bf16[40,32,1281]{2,1,0:T(8,128)(2,1)S(1)}, bf16[40,32,1281]{2,1,0:T(8,128)(2,1)}, u32[]{:S(2)}) copy-start(bf16[40,32,1281]{2,1,0:T(8,128)(2,1)} %legendre.1) | copy-start | bytes 9838084
  0.0 8.4 %collective-permute-start = (bf16[2,4,2,2816]{3,2,1,0:T(2,128)(2,1)}, bf16[2,4,2,2816]{3,2,1,0:T(2,128)(2,1)S(1)}, u32[]{:S(2)}, u32[]{:S(2)}) collective-permute-start(bf16[2,4,2,2816]{3,2,1,0:T(2,128)(2,1)} %fields_far.1), channel_id=1, source_target_pairs={{0,2},{4,6},{8,10},{12,14},{16,18},{20,22},{24,26},{28,30},{2,0},{... | collective-permute-start | bytes 270344 | tf_op jit(solution)/shard_map/ppermute | solution.py:354
  2.9 5.5 %collective-permute-start.1 = (bf16[2,4,2,2816]{3,2,1,0:T(2,128)(2,1)}, bf16[2,4,2,2816]{3,2,1,0:T(2,128)(2,1)S(1)}, u32[]{:S(2)}, u32[]{:S(2)}) collective-permute-start(bf16[2,4,2,2816]{3,2,1,0:T(2,128)(2,1)} %fields_far.1), channel_id=1, source_target_pairs={{2,4},{6,8},{10,12},{14,16},{18,20},{22,24},{26,28},{4,2},{8,6},{1... | collective-permute-start | bytes 270344 | tf_op jit(solution)/shard_map/ppermute | solution.py:354

commit v4 on v3

--- a/solution.py
+++ b/solution.py
@@ -276,9 +276,13 @@
             )
             lines[level, field_count, part] = running
     depth = SUB * lat_total
+    outer, inner = split_of(owners)
+    lat_count = lat_total // owners
+    row = lax.broadcasted_iota(jnp.int32, (lat_total, depth), 0)
+    sender = row // lat_count
+    latitude = (sender % outer * inner + sender // outer) * lat_count + row % lat_count
     spread = (
-        lax.broadcasted_iota(jnp.int32, (lat_total, depth), 0)
-        == lax.broadcasted_iota(jnp.int32, (lat_total, depth), 1) % lat_total
+        latitude == lax.broadcasted_iota(jnp.int32, (lat_total, depth), 1) % lat_total
     ).astype(jnp.bfloat16)
     keep = (
         lax.broadcasted_iota(jnp.int32, (SUB, depth), 0)
@@ -337,6 +341,25 @@
         copy.wait()
 
 
+def split_of(owners):
+    inner = 1
+    while inner * inner < owners:
+        inner *= 2
+    return owners // inner, inner
+
+
+def exchanged(parts, owners):
+    outer, inner = split_of(owners)
+    across = [[high * inner + low for high in range(outer)] for low in range(inner)]
+    within = [[high * inner + low for low in range(inner)] for high in range(outer)]
+    shape = parts.shape
+    parts = parts.reshape(outer, inner, *shape[1:])
+    parts = lax.all_to_all(parts, "lat", 0, 0, axis_index_groups=across, tiled=True)
+    parts = jnp.swapaxes(parts, 0, 1)
+    parts = lax.all_to_all(parts, "lat", 0, 0, axis_index_groups=within, tiled=True)
+    return parts.reshape(shape)
+
+
 def held(value):
     return pltpu.with_memory_space_constraint(value, pltpu.HBM)
 
@@ -404,7 +427,7 @@
         name="far_rows",
     )(held(rows_first), held(points), *sides, begins, factors, partial, table, twiddle)
 
-    received = lax.all_to_all(coefficients, "lat", split_axis=0, concat_axis=0, tiled=True)
+    received = exchanged(coefficients, owners)
     by_level = received.reshape(lat_total, 2, level_count, field_count, LANES).astype(jnp.float32)
     virtual = by_level[:, :, :, 2] + 0.61 * by_level[:, :, :, 3]
     total = jnp.sum(thickness[None, None, :, None] * virtual, axis=2).transpose(1, 0, 2)

time: 34.5 us -> 39.4 us (1.14)
  blocking collectives: 18.1 us -> 22.8 us
    all_to_all x1 -> x2, blocking collectives: 16.2 us -> 20.9 us  [the longest x1 13.5 us: exchanged(): lax.all_to_all(parts, 'lat', 0, 0, axis_index_groups=across, tiled=True)]
  transfers between devices with their start and end apart: 2 -> 2, of which waited for: 0 -> 0; matrix products, arithmetic and copies ran while one was open for 0% -> 0% of each run, Pallas kernels for 14% -> 12%
where the time goes in v4:
time: 39.4 us; the launch traced here: 39.2 us
  blocking collectives  22.8 us (58%)
  Pallas kernels  12.4 us (31%)
  starting transfers between devices  3.59 us (9%)
    all_to_all x1, blocking collectives, exchanged(): lax.all_to_all(parts, 'lat', 0, 0, axis_index_groups=across, tiled=True)  13.5 us
    all_to_all x1, blocking collectives, exchanged(): lax.all_to_all(parts, 'lat', 0, 0, axis_index_groups=within, tiled=True)  7.41 us
    pallas_call x1, Pallas kernels, local(): pl.pallas_call(functools.partial(near_kernel, pair_count * owners, pair_c...  4.78 us
    pallas_call x1, Pallas kernels, local(): pl.pallas_call(far_kernel, out_shape=jax.ShapeDtypeStruct((owners, 2 * SU...  4.11 us
    ppermute x2, starting transfers between devices, local(): lax.ppermute(fields, 'lat', edges + [(j, i) for i, j in edges])  3.59 us
    pallas_call x1, Pallas kernels, local(): pl.pallas_call(functools.partial(legendre_kernel, level_count, field_coun...  3.52 us
    all_gather x1, blocking collectives, local(): totals = lax.all_gather(total, 'lev')  1.85 us
  transfers between devices with their start and end apart: 2, of which 0 were waited for; matrix products, arithmetic and copies ran while one was open for 0% of the time, Pallas kernels for 12%

profile of v4, /device:TPU:0, one launch (start us, length us, event | category | flops | bytes accessed | tf_op | source)
XLA Modules:
  0.0 39.2 jit_solution(5444816657236456004)
XLA Ops:
  0.0 2.9 %collective-permute-start = (bf16[2,4,2,2816]{3,2,1,0:T(2,128)(2,1)}, bf16[2,4,2,2816]{3,2,1,0:T(2,128)(2,1)S(1)}, u32[]{:S(2)}, u32[]{:S(2)}) collective-permute-start(bf16[2,4,2,2816]{3,2,1,0:T(2,128)(2,1)} %fields_far.1), channel_id=1, source_target_pairs={{0,2},{4,6},{8,10},{12,14},{16,18},{20,22},{24,26},{28,30},{2,0},{... | collective-permute-start | bytes 270344 | tf_op jit(solution)/shard_map/ppermute | solution.py:377
  2.9 0.7 %collective-permute-start.1 = (bf16[2,4,2,2816]{3,2,1,0:T(2,128)(2,1)}, bf16[2,4,2,2816]{3,2,1,0:T(2,128)(2,1)S(1)}, u32[]{:S(2)}, u32[]{:S(2)}) collective-permute-start(bf16[2,4,2,2816]{3,2,1,0:T(2,128)(2,1)} %fields_far.1), channel_id=1, source_target_pairs={{2,4},{6,8},{10,12},{14,16},{18,20},{22,24},{26,28},{4,2},{8,6},{1... | collective-permute-start | bytes 270344 | tf_op jit(solution)/shard_map/ppermute | solution.py:377
  3.6 4.8 %near_rows.1 = (f32[2,11,8,256]{3,2,1,0:T(8,128)S(1)}, bf16[2,256,2560]{2,1,0:T(8,128)(2,1)S(1)}, f32[2,11,2560]{2,1,0:T(8,128)S(1)}, s32[2,4,22,1,128]{4,3,2,1,0:T(1,128)S(1)}, f32[704,128]{1,0:T(8,128)S(1)}) custom-call(s32[2]{0:T(128)} %rows_first_far.3, s32[32]{0:T(128)} %points_far.3, bf16[2,4,2,2816]{3,2,1,0:T(2,128)(2,1)} %fields_far.1, ...), custom_call_target="tpu_custom_call" | custom-call | flops 10000000 | bytes 4000000 | tf_op jit(solution)/shard_map/near_rows/pallas_call | solution.py:387
  8.4 0.0 collective-permute-done.near_side
  8.4 0.0 collective-permute-done.1.far_side
  8.4 0.0 copy-start.1
  8.4 0.0 copy-start
  8.4 4.1 %far_rows.1 = bf16[16,32,128]{2,1,0:T(8,128)(2,1)S(1)} custom-call(s32[2]{0:T(128)} %rows_first_far.3, s32[32]{0:T(128)} %points_far.3, bf16[2,4,2,2816]{3,2,1,0:T(2,128)(2,1)S(1)} %collective-permute-done.near_side, bf16[2,4,2,2816]{3,2,1,0:T(2,128)(2,1)S(1)} %collective-permute-done.1.far_side, s32[2,4,22,1,128]{4,3,2,1,0:T(1,128)S(1)} %get-tuple-element.10.begins, ...), custom_call_target="tpu_custom_call" | custom-call | tf_op jit(solution)/shard_map/far_rows/pallas_call | solution.py:413
  12.6 13.5 %all_to_all.10 = bf16[4,4,32,128]{3,2,1,0:T(8,128)(2,1)S(1)} all-to-all(bf16[4,4,32,128]{3,2,1,0:T(8,128)(2,1)S(1)} %bitcast.12), channel_id=1, replica_groups={{0,8,16,24},{2,10,18,26},{4,12,20,28},{6,14,22,30},{1,9,17,25},{3,11,19..., dimensions={0} | all-to-all | bytes 262144 | tf_op jit(solution)/shard_map/all_to_all | solution.py:357
  26.1 7.4 %all_to_all.11 = bf16[4,4,32,128]{3,2,1,0:T(8,128)(2,1)S(1)} all-to-all(bf16[4,4,32,128]{3,2,1,0:T(8,128)(2,1)S(1)} %bitcast.14), channel_id=1, replica_groups={{0,2,4,6},{8,10,12,14},{16,18,20,22},{24,26,28,30},{1,3,5,7},{9,11,13,1..., dimensions={0} | all-to-all | bytes 262144 | tf_op jit(solution)/shard_map/all_to_all | solution.py:359
  33.5 0.1 fusion
  33.6 0.0 copy-done.1
  33.7 0.2 multiply_reduce_fusion
  33.8 1.9 %all-gather = f32[4,32,128]{2,1,0:T(8,128)S(1)} all-gather(f32[2,32,128]{2,1,0:T(8,128)S(1)} %copy.12), channel_id=2, replica_groups=mesh['lat'=16,'lev'=2] {'lev'}, dimensions={0}, use_global_device_ids=true | all-gather | bytes 98304 | tf_op jit(solution)/shard_map/all_gather | solution.py:434
  35.7 0.0 copy-done
  35.7 3.5 %degree_sums.1 = bf16[2,5,2,40,1281]{4,3,2,1,0:T(8,128)(2,1)} custom-call(f32[2]{0:T(128)S(1)} %copy-done.1, bf16[16,32,128]{2,1,0:T(8,128)(2,1)S(1)} %bitcast.11, f32[2,2,32,128]{3,2,1,0:T(8,128)S(1)} %bitcast.13, bf16[40,32,1281]{2,1,0:T(8,128)(2,1)S(1)} %copy-done), custom_call_target="tpu_custom_call" | custom-call | tf_op jit(solution)/shard_map/degree_sums/pallas_call | solution.py:439
  (3 shorter events, 0.0 us)
Async XLA Ops:
  0.0 8.4 %collective-permute-start = (bf16[2,4,2,2816]{3,2,1,0:T(2,128)(2,1)}, bf16[2,4,2,2816]{3,2,1,0:T(2,128)(2,1)S(1)}, u32[]{:S(2)}, u32[]{:S(2)}) collective-permute-start(bf16[2,4,2,2816]{3,2,1,0:T(2,128)(2,1)} %fields_far.1), channel_id=1, source_target_pairs={{0,2},{4,6},{8,10},{12,14},{16,18},{20,22},{24,26},{28,30},{2,0},{... | collective-permute-start | bytes 270344 | tf_op jit(solution)/shard_map/ppermute | solution.py:377
  2.9 5.5 %collective-permute-start.1 = (bf16[2,4,2,2816]{3,2,1,0:T(2,128)(2,1)}, bf16[2,4,2,2816]{3,2,1,0:T(2,128)(2,1)S(1)}, u32[]{:S(2)}, u32[]{:S(2)}) collective-permute-start(bf16[2,4,2,2816]{3,2,1,0:T(2,128)(2,1)} %fields_far.1), channel_id=1, source_target_pairs={{2,4},{6,8},{10,12},{14,16},{18,20},{22,24},{26,28},{4,2},{8,6},{1... | collective-permute-start | bytes 270344 | tf_op jit(solution)/shard_map/ppermute | solution.py:377
  8.4 25.2 %copy-start.1 = (f32[2]{0:T(128)S(1)}, f32[2]{0:T(128)}, u32[]{:S(2)}) copy-start(f32[2]{0:T(128)} %thickness.1) | copy-start | bytes 28
  8.4 27.3 %copy-start = (bf16[40,32,1281]{2,1,0:T(8,128)(2,1)S(1)}, bf16[40,32,1281]{2,1,0:T(8,128)(2,1)}, u32[]{:S(2)}) copy-start(bf16[40,32,1281]{2,1,0:T(8,128)(2,1)} %legendre.1) | copy-start | bytes 9838084

commit v5 on v3

--- a/solution.py
+++ b/solution.py
@@ -10,36 +10,52 @@
 
 LANES = 128
 SUB = 8
+HALF = 64
 STENCIL = 4
 LIMIT = 24 * 1024 * 1024
 
 
 def lane_gather(values, lanes):
     return jnp.take_along_axis(values, lanes, axis=1, mode="promise_in_bounds")
+
+
+SINE = (-70.99342854244645, 81.34076844400118, -41.337142359536955, 6.283164044230117)
+COSINE = (
+    56.2423804697887, -85.2403304160897, 64.93459063550272, -19.739171434929204, 0.9999999534680867,
+)
+
+
+def polynomial(terms, square):
+    value = np.float32(terms[0])
+    for term in terms[1:]:
+        value = value * square + np.float32(term)
+    return value
 
 
 def turn_parts(product, total, inverse):
     turns = (product - jnp.floor(product * inverse + 0.5) * total) * inverse
     halves = jnp.floor(2.0 * turns + 0.5)
     sign = 1.0 - 2.0 * jnp.abs(halves)
-    x = (turns - 0.5 * halves) * np.float32(2.0 * np.pi)
-    y = x * x
-    sine = -1.0 / 39916800.0
-    for term in (1.0 / 362880.0, -1.0 / 5040.0, 1.0 / 120.0, -1.0 / 6.0, 1.0):
-        sine = sine * y + np.float32(term)
-    cosine = 1.0 / 479001600.0
-    for term in (-1.0 / 3628800.0, 1.0 / 40320.0, -1.0 / 720.0, 1.0 / 24.0, -0.5, 1.0):
-        cosine = cosine * y + np.float32(term)
-    return sign * cosine, sign * (sine * x)
+    part = turns - 0.5 * halves
+    square = part * part
+    return sign * polynomial(COSINE, square), (sign * part) * polynomial(SINE, square)
 
 
 def wavenumbers(at, width, pair_count, pair_total):
-    column = lax.broadcasted_iota(jnp.int32, (1, width), 1) + at
-    owner = column // (2 * pair_count)
-    inner = column - owner * (2 * pair_count)
+    column = lax.broadcasted_iota(jnp.int32, (1, width), 1).astype(jnp.float32) + float(at)
+    owner = jnp.floor((column + 0.5) * (1.0 / (2 * pair_count)))
+    inner = column - owner * (2.0 * pair_count)
     second = inner >= pair_count
     pair = owner * pair_count + jnp.where(second, inner - pair_count, inner)
-    return jnp.where(second, 2 * pair_total - 1 - pair, pair).astype(jnp.float32)
+    return jnp.where(second, 2.0 * pair_total - 1.0 - pair, pair)
+
+
+def multiplied(one, two):
+    return one[0] * two[0] - one[1] * two[1], one[0] * two[1] + one[1] * two[0]
+
+
+def row_of(pair, row):
+    return tuple(part[row : row + 1] for part in pair)
 
 
 def extend(lines, row, rows_each, missing, ext, slot):
@@ -107,7 +123,7 @@
 def near_kernel(
     pair_total, pair_count, rows_first_far, points_far, fields_far, starts_far, weights_far,
     partial, table, twiddle, begins, factors,
-    rows_first, points, fields, starts, weights, lines, ext, fine, arrived,
+    rows_first, points, fields, starts, weights, lines, ext, arrived,
 ):
     lat_count, couples = partial.shape[:2]
     lon = 2 * couples * LANES
@@ -129,36 +145,34 @@
         fetch.start()
     fetches[0].wait()
     width = 256
+    scales = []
     for latitude in range(lat_count):
         total = jnp.full((1, 1), points[first_lat + latitude], jnp.int32).astype(jnp.float32)
         inverse = 1.0 / total
-        scaling = jnp.sqrt(2.0 * inverse)
-
-        def chunk(index, carry, latitude=latitude, total=total, inverse=inverse, scaling=scaling):
-            at = pl.multiple_of(index * width, width)
-            numbers = wavenumbers(at, width, pair_count, pair_total)
-            step = lax.broadcasted_iota(jnp.int32, (couples, width), 0).astype(jnp.float32)
-            cosine, sine = turn_parts(numbers * step * float(2 * LANES), total, inverse)
-            twiddle[latitude, :, pl.ds(at, width)] = scaling * cosine
-            twiddle[latitude, :, pl.ds(columns + at, width)] = scaling * sine
-            step = lax.broadcasted_iota(jnp.int32, (16, width), 0).astype(jnp.float32)
-            low_cos, low_sin = turn_parts(numbers * step, total, inverse)
-            high_cos, high_sin = turn_parts(numbers * step * 16.0, total, inverse)
-            fine[0] = high_cos
-            fine[1] = high_sin
-            for high in range(16):
-                this_cos = fine[0, high : high + 1, :]
-                this_sin = fine[1, high : high + 1, :]
-                rows = pl.ds(16 * high, 16)
-                table[latitude, rows, pl.ds(at, width)] = (
-                    this_cos * low_cos - this_sin * low_sin
-                ).astype(jnp.bfloat16)
-                table[latitude, rows, pl.ds(columns + at, width)] = (
-                    this_cos * low_sin + this_sin * low_cos
-                ).astype(jnp.bfloat16)
-            return carry
-
-        lax.fori_loop(0, columns // width, chunk, 0)
+        scales.append((total, inverse, jnp.sqrt(2.0 * inverse)))
+    few = lax.broadcasted_iota(jnp.int32, (SUB, width), 0).astype(jnp.float32)
+    many = lax.broadcasted_iota(jnp.int32, (couples + 3, width), 0)
+    many = jnp.where(many < couples, many * (2 * LANES), (many - (couples - 1)) * HALF)
+    many = many.astype(jnp.float32)
+    for at in range(0, columns, width):
+        numbers = wavenumbers(at, width, pair_count, pair_total)
+        for latitude, (total, inverse, scaling) in enumerate(scales):
+            ones = turn_parts(numbers * few, total, inverse)
+            eights = turn_parts(numbers * (few * float(SUB)), total, inverse)
+            large = turn_parts(numbers * many, total, inverse)
+            here = slice(at, at + width)
+            there = slice(columns + at, columns + at + width)
+            twiddle[latitude, :, here] = scaling * large[0][:couples]
+            twiddle[latitude, :, there] = scaling * large[1][:couples]
+            products = [ones] + [multiplied(row_of(eights, row), ones) for row in range(1, SUB)]
+            block = tuple(jnp.concatenate(parts, axis=0) for parts in zip(*products))
+            for quarter in range(4):
+                turned = block
+                if quarter > 0:
+                    turned = multiplied(row_of(large, couples + quarter - 1), block)
+                rows = slice(HALF * quarter, HALF * (quarter + 1))
+                table[latitude, rows, here] = turned[0].astype(jnp.bfloat16)
+                table[latitude, rows, there] = turned[1].astype(jnp.bfloat16)
     for fetch in fetches[1:]:
         fetch.wait()
     spread_rows(starts, begins)
@@ -220,8 +234,9 @@
                 lanes = pl.ds(side * LANES, LANES)
                 live = lane + (2 * couple + side) * LANES < points[first_lat + latitude]
                 value = partial[latitude, couple, :, lanes] + totals[side]
-                grid[couple, :, lanes] = jnp.where(live, value, 0.0)
-        rows = grid[...].reshape(couples * SUB, 2 * LANES).astype(jnp.bfloat16)
+                grid[latitude, couple, :, lanes] = jnp.where(live, value, 0.0)
+    for latitude in range(lat_count):
+        rows = grid[latitude].reshape(couples * SUB, 2 * LANES).astype(jnp.bfloat16)
         for at in range(0, columns, width):
             real = jnp.dot(
                 rows, table[latitude, :, at : at + width], preferred_element_type=jnp.float32
@@ -239,13 +254,13 @@
                 here = slice(couple * SUB, (couple + 1) * SUB)
                 cosine = cosine + (real[here] * turn_cos - imag[here] * turn_sin)
                 sine = sine - (real[here] * turn_sin + imag[here] * turn_cos)
-            waves[0:SUB, at : at + width] = cosine
-            waves[SUB : 2 * SUB, at : at + width] = sine
-        waves[:, columns:] = jnp.zeros((2 * SUB, waves.shape[1] - columns), jnp.float32)
+            waves[latitude, 0:SUB, at : at + width] = cosine
+            waves[latitude, SUB : 2 * SUB, at : at + width] = sine
+        waves[latitude, :, columns:] = jnp.zeros((2 * SUB, waves.shape[2] - columns), jnp.float32)
         used = columns // owners
         for owner in range(owners):
             out[owner, 2 * SUB * latitude : 2 * SUB * (latitude + 1), :] = waves[
-                :, owner * used : owner * used + LANES
+                latitude, :, owner * used : owner * used + LANES
             ].astype(jnp.bfloat16)
 
 
@@ -258,7 +273,6 @@
     pair_total = pair_count * owners
     groups = [(at, min(SUB, pair_count - at)) for at in range(0, pair_count, SUB)]
     keys = [(field, part) for field in range(field_count + 1) for part in range(2)]
-    half = len(keys) * SUB
     level_place = lax.axis_index("lev")
     first_pair = lax.axis_index("lat") * pair_count
     wide[...] = received[...].astype(jnp.float32).reshape(wide.shape)
@@ -284,54 +298,56 @@
         lax.broadcasted_iota(jnp.int32, (SUB, depth), 0)
         == lax.broadcasted_iota(jnp.int32, (SUB, depth), 1) // lat_total
     )
+    keys = [(level,) + key for level in range(level_count) for key in keys]
+    half = len(keys) * SUB
+    for place in range(0, len(keys), 2):
+        couple = [
+            lax.dot_general(
+                lines[key].astype(jnp.bfloat16),
+                spread,
+                (((0,), (0,)), ((), ())),
+                preferred_element_type=jnp.float32,
+            )
+            for key in keys[place : place + 2]
+        ]
+        for member in range(2):
+            for group, (at, _) in enumerate(groups):
+                begin = member * pair_count + at
+                pieces = [jnp.where(keep, one[begin : begin + SUB], 0.0) for one in couple]
+                into = member * half + place * SUB
+                left[group, into : into + 2 * SUB, :] = jnp.concatenate(pieces, axis=0).astype(
+                    jnp.bfloat16
+                )
     copies = []
-    for level in range(level_count):
-        for place in range(0, len(keys), 2):
-            couple = [
-                lax.dot_general(
-                    lines[(level,) + key].astype(jnp.bfloat16),
-                    spread,
-                    (((0,), (0,)), ((), ())),
-                    preferred_element_type=jnp.float32,
+    for start in range(0, degrees, 256):
+        stop = min(start + 256, degrees)
+        low = 0 if start < 2 * pair_total else half
+        high = 2 * half if stop > pair_total + 1 else half
+        parts = []
+        for group, (at, size) in enumerate(groups):
+            values = legendre[at : at + size, :, start:stop].reshape(size * lat_total, stop - start)
+            sums = jnp.dot(
+                left[group, low:high, : size * lat_total],
+                values,
+                preferred_element_type=jnp.float32,
+            ).reshape((high - low) // SUB, SUB, stop - start)
+            if high - low > half:
+                shape = (SUB, stop - start)
+                slot = lax.broadcasted_iota(jnp.int32, shape, 1) + start
+                pair = lax.broadcasted_iota(jnp.int32, shape, 0) + (first_pair + at)
+                sums = jnp.where(
+                    slot + pair < 2 * pair_total, sums[: len(keys)], sums[len(keys) :]
                 )
-                for key in keys[place : place + 2]
-            ]
-            for member in range(2):
-                for group, (at, _) in enumerate(groups):
-                    begin = member * pair_count + at
-                    pieces = [jnp.where(keep, one[begin : begin + SUB], 0.0) for one in couple]
-                    into = member * half + place * SUB
-                    left[level, group, into : into + 2 * SUB, :] = jnp.concatenate(
-                        pieces, axis=0
-                    ).astype(jnp.bfloat16)
-        for start in range(0, degrees, 256):
-            stop = min(start + 256, degrees)
-            low = 0 if start < 2 * pair_total else half
-            high = 2 * half if stop > pair_total + 1 else half
-            parts = []
-            for group, (at, size) in enumerate(groups):
-                values = legendre[at : at + size, :, start:stop].reshape(
-                    size * lat_total, stop - start
-                )
-                sums = jnp.dot(
-                    left[level, group, low:high, : size * lat_total],
-                    values,
-                    preferred_element_type=jnp.float32,
-                ).reshape((high - low) // SUB, SUB, stop - start)
-                if high - low > half:
-                    shape = (SUB, stop - start)
-                    slot = lax.broadcasted_iota(jnp.int32, shape, 1) + start
-                    pair = lax.broadcasted_iota(jnp.int32, shape, 0) + (first_pair + at)
-                    sums = jnp.where(
-                        slot + pair < 2 * pair_total, sums[: len(keys)], sums[len(keys) :]
-                    )
-                parts.append(sums[:, :size])
-            planes[level, :, :, :, start:stop] = (
-                jnp.concatenate(parts, axis=1)
-                .astype(jnp.bfloat16)
-                .reshape(field_count + 1, 2, pair_count, stop - start)
-            )
-        copies.append(pltpu.make_async_copy(planes.at[level], out.at[level], sent.at[level]))
+            parts.append(sums[:, :size])
+        planes[:, :, :, :, start:stop] = (
+            jnp.concatenate(parts, axis=1).astype(jnp.bfloat16).reshape(planes.shape[:4] + (stop - start,))
+        )
+        here = pl.ds(start, stop - start)
+        copies.append(
+            pltpu.make_async_copy(
+                planes.at[:, :, :, :, here], out.at[:, :, :, :, here], sent.at[len(copies)]
+            )
+        )
         copies[-1].start()
     for copy in copies:
         copy.wait()
@@ -379,7 +395,6 @@
             pltpu.VMEM(weights.shape, weights.dtype),
             pltpu.VMEM((fields.size // LANES, LANES), jnp.float32),
             pltpu.VMEM((lat_count, blocks + 2, SUB, LANES), jnp.float32),
-            pltpu.VMEM((2, 16, 256), jnp.float32),
             pltpu.SemaphoreType.DMA((5,)),
         ],
         compiler_params=params,
@@ -396,8 +411,8 @@
         + [
             pltpu.VMEM((2, fields.size // LANES, LANES), jnp.float32),
             pltpu.VMEM((2 * lat_count, blocks + 2, SUB, LANES), jnp.float32),
-            pltpu.VMEM((couples, SUB, 2 * LANES), jnp.float32),
-            pltpu.VMEM((2 * SUB, columns + LANES), jnp.float32),
+            pltpu.VMEM((lat_count, couples, SUB, 2 * LANES), jnp.float32),
+            pltpu.VMEM((lat_count, 2 * SUB, columns + LANES), jnp.float32),
             pltpu.SemaphoreType.DMA((2,)),
         ],
         compiler_params=params,
@@ -411,7 +426,7 @@
     totals = lax.all_gather(total, "lev")
 
     out_shape = (level_count, field_count + 1, 2, pair_count, degrees)
-    half = (field_count + 1) * 2 * SUB
+    half = level_count * (field_count + 1) * 2 * SUB
     group_count = (pair_count + SUB - 1) // SUB
     return pl.pallas_call(
         functools.partial(legendre_kernel, level_count, field_count),
@@ -420,9 +435,9 @@
         out_specs=pl.BlockSpec(memory_space=pl.ANY),
         scratch_shapes=[
             pltpu.VMEM((lat_total * 2 * SUB, LANES), jnp.float32),
-            pltpu.VMEM((level_count, group_count, 2 * half, SUB * lat_total), jnp.bfloat16),
+            pltpu.VMEM((group_count, 2 * half, SUB * lat_total), jnp.bfloat16),
             pltpu.VMEM(out_shape, jnp.bfloat16),
-            pltpu.SemaphoreType.DMA((level_count,)),
+            pltpu.SemaphoreType.DMA(((degrees + 255) // 256,)),
         ],
         compiler_params=params,
         name="degree_sums",

time: 34.5 us -> 33.2 us (0.962)
  Pallas kernels: 12.3 us -> 11 us
    pallas_call x1, Pallas kernels: 4.78 us -> 4.26 us  [local(): pl.pallas_call(functools.partial(near_kernel, pair_count * owners, pair_c...]
    pallas_call x1, Pallas kernels: 3.52 us -> 3.02 us  [local(): pl.pallas_call(functools.partial(legendre_kernel, level_count, field_coun...]
  transfers between devices with their start and end apart: 2 -> 2, of which waited for: 0 -> 0; matrix products, arithmetic and copies ran while one was open for 0% -> 0% of each run, Pallas kernels for 14% -> 13%
where the time goes in v5:
time: 33.2 us; the launch traced here: 33 us
  blocking collectives  18.1 us (55%)
  Pallas kernels  11 us (33%)
  starting transfers between devices  3.59 us (11%)
    all_to_all x1, blocking collectives, local(): lax.all_to_all(coefficients, 'lat', split_axis=0, concat_axis=0, tiled=True)  16.2 us
    pallas_call x1, Pallas kernels, local(): pl.pallas_call(functools.partial(near_kernel, pair_count * owners, pair_c...  4.26 us
    pallas_call x1, Pallas kernels, local(): pl.pallas_call(far_kernel, out_shape=jax.ShapeDtypeStruct((owners, 2 * SU...  3.67 us
    ppermute x2, starting transfers between devices, local(): lax.ppermute(fields, 'lat', edges + [(j, i) for i, j in edges])  3.59 us
    pallas_call x1, Pallas kernels, local(): pl.pallas_call(functools.partial(legendre_kernel, level_count, field_coun...  3.02 us
    all_gather x1, blocking collectives, local(): totals = lax.all_gather(total, 'lev')  1.85 us
  transfers between devices with their start and end apart: 2, of which 0 were waited for; matrix products, arithmetic and copies ran while one was open for 0% of the time, Pallas kernels for 13%

profile of v5, /device:TPU:0, one launch (start us, length us, event | category | flops | bytes accessed | tf_op | source)
XLA Modules:
  0.0 33.0 jit_solution(8821788858774638858)
XLA Ops:
  0.0 0.0 copy-start.1
  0.0 0.0 copy-start
  0.0 2.9 %collective-permute-start = (bf16[2,4,2,2816]{3,2,1,0:T(2,128)(2,1)}, bf16[2,4,2,2816]{3,2,1,0:T(2,128)(2,1)S(1)}, u32[]{:S(2)}, u32[]{:S(2)}) collective-permute-start(bf16[2,4,2,2816]{3,2,1,0:T(2,128)(2,1)} %fields_far.1), channel_id=1, source_target_pairs={{0,2},{4,6},{8,10},{12,14},{16,18},{20,22},{24,26},{28,30},{2,0},{... | collective-permute-start | bytes 270344 | tf_op jit(solution)/shard_map/ppermute | solution.py:370
  2.9 0.7 %collective-permute-start.1 = (bf16[2,4,2,2816]{3,2,1,0:T(2,128)(2,1)}, bf16[2,4,2,2816]{3,2,1,0:T(2,128)(2,1)S(1)}, u32[]{:S(2)}, u32[]{:S(2)}) collective-permute-start(bf16[2,4,2,2816]{3,2,1,0:T(2,128)(2,1)} %fields_far.1), channel_id=1, source_target_pairs={{2,4},{6,8},{10,12},{14,16},{18,20},{22,24},{26,28},{4,2},{8,6},{1... | collective-permute-start | bytes 270344 | tf_op jit(solution)/shard_map/ppermute | solution.py:370
  3.6 4.3 %near_rows.1 = (f32[2,11,8,256]{3,2,1,0:T(8,128)S(1)}, bf16[2,256,2560]{2,1,0:T(8,128)(2,1)S(1)}, f32[2,11,2560]{2,1,0:T(8,128)S(1)}, s32[2,4,22,1,128]{4,3,2,1,0:T(1,128)S(1)}, f32[704,128]{1,0:T(8,128)S(1)}) custom-call(s32[2]{0:T(128)} %rows_first_far.3, s32[32]{0:T(128)} %points_far.3, bf16[2,4,2,2816]{3,2,1,0:T(2,128)(2,1)} %fields_far.1, ...), custom_call_target="tpu_custom_call" | custom-call | flops 10000000 | bytes 4000000 | tf_op jit(solution)/shard_map/near_rows/pallas_call | solution.py:380
  7.9 0.0 collective-permute-done.near_side
  7.9 0.0 collective-permute-done.1.far_side
  7.9 3.7 %far_rows.1 = bf16[16,32,128]{2,1,0:T(8,128)(2,1)S(1)} custom-call(s32[2]{0:T(128)} %rows_first_far.3, s32[32]{0:T(128)} %points_far.3, bf16[2,4,2,2816]{3,2,1,0:T(2,128)(2,1)S(1)} %collective-permute-done.near_side, bf16[2,4,2,2816]{3,2,1,0:T(2,128)(2,1)S(1)} %collective-permute-done.1.far_side, s32[2,4,22,1,128]{4,3,2,1,0:T(1,128)S(1)} %get-tuple-element.10.begins, ...), custom_call_target="tpu_custom_call" | custom-call | tf_op jit(solution)/shard_map/far_rows/pallas_call | solution.py:405
  11.6 16.2 %all_to_all.5.received = bf16[16,32,128]{2,1,0:T(8,128)(2,1)S(1)} all-to-all(bf16[16,32,128]{2,1,0:T(8,128)(2,1)S(1)} %far_rows.1), channel_id=1, replica_groups=mesh['lat'=16,'lev'=2] {'lat'}, dimensions={0} | all-to-all | bytes 262144 | tf_op jit(solution)/shard_map/all_to_all | solution.py:422
  27.8 0.1 fusion.1
  27.9 0.0 copy-done.1
  27.9 0.2 fusion
  28.1 1.9 %all-gather = f32[4,32,128]{2,1,0:T(8,128)S(1)} all-gather(f32[2,32,128]{2,1,0:T(8,128)S(1)} %copy.10), channel_id=2, replica_groups=mesh['lat'=16,'lev'=2] {'lev'}, dimensions={0}, use_global_device_ids=true | all-gather | bytes 98304 | tf_op jit(solution)/shard_map/all_gather | solution.py:426
  30.0 0.0 copy-done
  30.0 3.0 %degree_sums.1 = bf16[2,5,2,40,1281]{4,3,2,1,0:T(8,128)(2,1)} custom-call(f32[2]{0:T(128)S(1)} %copy-done.1, bf16[16,32,128]{2,1,0:T(8,128)(2,1)S(1)} %all_to_all.5.received, f32[2,2,32,128]{3,2,1,0:T(8,128)S(1)} %bitcast.11, bf16[40,32,1281]{2,1,0:T(8,128)(2,1)S(1)} %copy-done), custom_call_target="tpu_custom_call" | custom-call | tf_op jit(solution)/shard_map/degree_sums/pallas_call | solution.py:431
  (1 shorter events, 0.0 us)
Async XLA Ops:
  0.0 27.9 %copy-start.1 = (f32[2]{0:T(128)S(1)}, f32[2]{0:T(128)}, u32[]{:S(2)}) copy-start(f32[2]{0:T(128)} %thickness.1) | copy-start | bytes 28
  0.0 30.0 %copy-start = (bf16[40,32,1281]{2,1,0:T(8,128)(2,1)S(1)}, bf16[40,32,1281]{2,1,0:T(8,128)(2,1)}, u32[]{:S(2)}) copy-start(bf16[40,32,1281]{2,1,0:T(8,128)(2,1)} %legendre.1) | copy-start | bytes 9838084
  0.0 7.9 %collective-permute-start = (bf16[2,4,2,2816]{3,2,1,0:T(2,128)(2,1)}, bf16[2,4,2,2816]{3,2,1,0:T(2,128)(2,1)S(1)}, u32[]{:S(2)}, u32[]{:S(2)}) collective-permute-start(bf16[2,4,2,2816]{3,2,1,0:T(2,128)(2,1)} %fields_far.1), channel_id=1, source_target_pairs={{0,2},{4,6},{8,10},{12,14},{16,18},{20,22},{24,26},{28,30},{2,0},{... | collective-permute-start | bytes 270344 | tf_op jit(solution)/shard_map/ppermute | solution.py:370
  2.9 4.9 %collective-permute-start.1 = (bf16[2,4,2,2816]{3,2,1,0:T(2,128)(2,1)}, bf16[2,4,2,2816]{3,2,1,0:T(2,128)(2,1)S(1)}, u32[]{:S(2)}, u32[]{:S(2)}) collective-permute-start(bf16[2,4,2,2816]{3,2,1,0:T(2,128)(2,1)} %fields_far.1), channel_id=1, source_target_pairs={{2,4},{6,8},{10,12},{14,16},{18,20},{22,24},{26,28},{4,2},{8,6},{1... | collective-permute-start | bytes 270344 | tf_op jit(solution)/shard_map/ppermute | solution.py:370

commit v6 on v5

--- a/solution.py
+++ b/solution.py
@@ -190,7 +190,7 @@
 
 
 def far_kernel(
-    rows_first_far, points_far, near_side, far_side, begins, factors, partial, table, twiddle,
+    rows_first_far, points_far, first_side, second_side, begins, factors, partial, table, twiddle,
     out, rows_first, points, lines, ext, grid, waves, arrived,
 ):
     fetches = [
@@ -205,9 +205,9 @@
     owners = out.shape[0]
     first_lat = lax.axis_index("lat") * lat_count
     lat_total = points.shape[0]
-    toward = 1 - lax.axis_index("lat") % 2
-    spread_lines(near_side, lines.at[toward])
-    spread_lines(far_side, lines.at[1 - toward])
+    toward = lax.axis_index("lat") % 2
+    spread_lines(first_side, lines.at[toward])
+    spread_lines(second_side, lines.at[1 - toward])
     for fetch in fetches:
         fetch.wait()
     for side in range(2):
@@ -365,7 +365,7 @@
     blocks = 2 * couples
     columns = 2 * owners * pair_count
     sides = []
-    for first in range(2):
+    for first in (1, 0):
         edges = [(i, i + 1) for i in range(first, owners - 1, 2)]
         sides.append(lax.ppermute(fields, "lat", edges + [(j, i) for i, j in edges]))
 

time: 33.2 us -> 33.6 us (1.012)
  starting transfers between devices: 3.59 us -> 6.65 us
  blocking collectives: 18.1 us -> 15.3 us
    ppermute x2, starting transfers between devices: 3.59 us -> 6.65 us  [local(): lax.ppermute(fields, 'lat', edges + [(j, i) for i, j in edges])]
    all_to_all x1, blocking collectives: 16.2 us -> 13.5 us  [local(): lax.all_to_all(coefficients, 'lat', split_axis=0, concat_axis=0, tiled=True)]
  transfers between devices with their start and end apart: 2 -> 2, of which waited for: 0 -> 1; matrix products, arithmetic and copies ran while one was open for 0% -> 0% of each run, Pallas kernels for 13% -> 13%
where the time goes in v6:
time: 33.6 us; the launch traced here: 33.4 us
  blocking collectives  15.3 us (46%)
  Pallas kernels  10.9 us (32%)
  starting transfers between devices  6.65 us (20%)
    all_to_all x1, blocking collectives, local(): lax.all_to_all(coefficients, 'lat', split_axis=0, concat_axis=0, tiled=True)  13.5 us
    ppermute x2, starting transfers between devices, local(): lax.ppermute(fields, 'lat', edges + [(j, i) for i, j in edges])  6.65 us
    pallas_call x1, Pallas kernels, local(): pl.pallas_call(functools.partial(near_kernel, pair_count * owners, pair_c...  4.25 us
    pallas_call x1, Pallas kernels, local(): pl.pallas_call(far_kernel, out_shape=jax.ShapeDtypeStruct((owners, 2 * SU...  3.67 us
    pallas_call x1, Pallas kernels, local(): pl.pallas_call(functools.partial(legendre_kernel, level_count, field_coun...  3.02 us
    all_gather x1, blocking collectives, local(): totals = lax.all_gather(total, 'lev')  1.85 us
  transfers between devices with their start and end apart: 2, of which 1 were waited for; matrix products, arithmetic and copies ran while one was open for 0% of the time, Pallas kernels for 13%

profile of v6, /device:TPU:0, one launch (start us, length us, event | category | flops | bytes accessed | tf_op | source)
XLA Modules:
  0.0 33.4 jit_solution(18445224032564379805)
XLA Ops:
  0.0 0.0 copy-start.1
  0.0 0.0 copy-start
  0.0 0.8 %collective-permute-start = (bf16[2,4,2,2816]{3,2,1,0:T(2,128)(2,1)}, bf16[2,4,2,2816]{3,2,1,0:T(2,128)(2,1)S(1)}, u32[]{:S(2)}, u32[]{:S(2)}) collective-permute-start(bf16[2,4,2,2816]{3,2,1,0:T(2,128)(2,1)} %fields_far.1), channel_id=1, source_target_pairs={{2,4},{6,8},{10,12},{14,16},{18,20},{22,24},{26,28},{4,2},{8,6},{1... | collective-permute-start | bytes 270344 | tf_op jit(solution)/shard_map/ppermute | solution.py:370
  0.8 5.9 %collective-permute-start.1 = (bf16[2,4,2,2816]{3,2,1,0:T(2,128)(2,1)}, bf16[2,4,2,2816]{3,2,1,0:T(2,128)(2,1)S(1)}, u32[]{:S(2)}, u32[]{:S(2)}) collective-permute-start(bf16[2,4,2,2816]{3,2,1,0:T(2,128)(2,1)} %fields_far.1), channel_id=1, source_target_pairs={{0,2},{4,6},{8,10},{12,14},{16,18},{20,22},{24,26},{28,30},{2,0},{... | collective-permute-start | bytes 270344 | tf_op jit(solution)/shard_map/ppermute | solution.py:370
  6.7 4.3 %near_rows.1 = (f32[2,11,8,256]{3,2,1,0:T(8,128)S(1)}, bf16[2,256,2560]{2,1,0:T(8,128)(2,1)S(1)}, f32[2,11,2560]{2,1,0:T(8,128)S(1)}, s32[2,4,22,1,128]{4,3,2,1,0:T(1,128)S(1)}, f32[704,128]{1,0:T(8,128)S(1)}) custom-call(s32[2]{0:T(128)} %rows_first_far.3, s32[32]{0:T(128)} %points_far.3, bf16[2,4,2,2816]{3,2,1,0:T(2,128)(2,1)} %fields_far.1, ...), custom_call_target="tpu_custom_call" | custom-call | flops 10000000 | bytes 4000000 | tf_op jit(solution)/shard_map/near_rows/pallas_call | solution.py:380
  10.9 0.0 collective-permute-done.first_side
  10.9 0.1 collective-permute-done.1.second_side
  11.1 3.7 %far_rows.1 = bf16[16,32,128]{2,1,0:T(8,128)(2,1)S(1)} custom-call(s32[2]{0:T(128)} %rows_first_far.3, s32[32]{0:T(128)} %points_far.3, bf16[2,4,2,2816]{3,2,1,0:T(2,128)(2,1)S(1)} %collective-permute-done.first_side, bf16[2,4,2,2816]{3,2,1,0:T(2,128)(2,1)S(1)} %collective-permute-done.1.second_side, s32[2,4,22,1,128]{4,3,2,1,0:T(1,128)S(1)} %get-tuple-element.10.begins, ...), custom_call_target="tpu_custom_call" | custom-call | tf_op jit(solution)/shard_map/far_rows/pallas_call | solution.py:405
  14.7 13.5 %all_to_all.5.received = bf16[16,32,128]{2,1,0:T(8,128)(2,1)S(1)} all-to-all(bf16[16,32,128]{2,1,0:T(8,128)(2,1)S(1)} %far_rows.1), channel_id=1, replica_groups=mesh['lat'=16,'lev'=2] {'lat'}, dimensions={0} | all-to-all | bytes 262144 | tf_op jit(solution)/shard_map/all_to_all | solution.py:422
  28.2 0.1 fusion.1
  28.3 0.0 copy-done.1
  28.3 0.2 fusion
  28.5 1.9 %all-gather = f32[4,32,128]{2,1,0:T(8,128)S(1)} all-gather(f32[2,32,128]{2,1,0:T(8,128)S(1)} %copy.10), channel_id=2, replica_groups=mesh['lat'=16,'lev'=2] {'lev'}, dimensions={0}, use_global_device_ids=true | all-gather | bytes 98304 | tf_op jit(solution)/shard_map/all_gather | solution.py:426
  30.4 0.0 copy-done
  30.4 3.0 %degree_sums.1 = bf16[2,5,2,40,1281]{4,3,2,1,0:T(8,128)(2,1)} custom-call(f32[2]{0:T(128)S(1)} %copy-done.1, bf16[16,32,128]{2,1,0:T(8,128)(2,1)S(1)} %all_to_all.5.received, f32[2,2,32,128]{3,2,1,0:T(8,128)S(1)} %bitcast.11, bf16[40,32,1281]{2,1,0:T(8,128)(2,1)S(1)} %copy-done), custom_call_target="tpu_custom_call" | custom-call | tf_op jit(solution)/shard_map/degree_sums/pallas_call | solution.py:431
  (1 shorter events, 0.0 us)
Async XLA Ops:
  0.0 28.3 %copy-start.1 = (f32[2]{0:T(128)S(1)}, f32[2]{0:T(128)}, u32[]{:S(2)}) copy-start(f32[2]{0:T(128)} %thickness.1) | copy-start | bytes 28
  0.0 30.4 %copy-start = (bf16[40,32,1281]{2,1,0:T(8,128)(2,1)S(1)}, bf16[40,32,1281]{2,1,0:T(8,128)(2,1)}, u32[]{:S(2)}) copy-start(bf16[40,32,1281]{2,1,0:T(8,128)(2,1)} %legendre.1) | copy-start | bytes 9838084
  0.0 10.9 %collective-permute-start = (bf16[2,4,2,2816]{3,2,1,0:T(2,128)(2,1)}, bf16[2,4,2,2816]{3,2,1,0:T(2,128)(2,1)S(1)}, u32[]{:S(2)}, u32[]{:S(2)}) collective-permute-start(bf16[2,4,2,2816]{3,2,1,0:T(2,128)(2,1)} %fields_far.1), channel_id=1, source_target_pairs={{2,4},{6,8},{10,12},{14,16},{18,20},{22,24},{26,28},{4,2},{8,6},{1... | collective-permute-start | bytes 270344 | tf_op jit(solution)/shard_map/ppermute | solution.py:370
  0.8 10.3 %collective-permute-start.1 = (bf16[2,4,2,2816]{3,2,1,0:T(2,128)(2,1)}, bf16[2,4,2,2816]{3,2,1,0:T(2,128)(2,1)S(1)}, u32[]{:S(2)}, u32[]{:S(2)}) collective-permute-start(bf16[2,4,2,2816]{3,2,1,0:T(2,128)(2,1)} %fields_far.1), channel_id=1, source_target_pairs={{0,2},{4,6},{8,10},{12,14},{16,18},{20,22},{24,26},{28,30},{2,0},{... | collective-permute-start | bytes 270344 | tf_op jit(solution)/shard_map/ppermute | solution.py:370

commit v7 on v5

--- a/solution.py
+++ b/solution.py
@@ -206,8 +206,8 @@
     first_lat = lax.axis_index("lat") * lat_count
     lat_total = points.shape[0]
     toward = 1 - lax.axis_index("lat") % 2
-    spread_lines(near_side, lines.at[toward])
-    spread_lines(far_side, lines.at[1 - toward])
+    spread_lines(near_side.at[toward], lines.at[toward])
+    spread_lines(far_side.at[1 - toward], lines.at[1 - toward])
     for fetch in fetches:
         fetch.wait()
     for side in range(2):
@@ -366,8 +366,8 @@
     columns = 2 * owners * pair_count
     sides = []
     for first in range(2):
-        edges = [(i, i + 1) for i in range(first, owners - 1, 2)]
-        sides.append(lax.ppermute(fields, "lat", edges + [(j, i) for i, j in edges]))
+        pairs = [[i, (i + 1) % owners] for i in range(first, owners, 2)]
+        sides.append(lax.all_gather(fields, "lat", axis_index_groups=pairs))
 
     scalar = pl.BlockSpec(memory_space=pltpu.SMEM)
     vector = pl.BlockSpec(memory_space=pltpu.VMEM)

time: 33.2 us -> 44.7 us (1.35)
  blocking collectives: 18.1 us -> 31.9 us
  starting transfers between devices: 3.59 us -> 0 us
  local copies, waits for them, and re-layouts: 0.13 us -> 1.34 us
    all_gather x0 -> x2, blocking collectives: none -> 15.4 us  [local(): sides.append(lax.all_gather(fields, 'lat', axis_index_groups=pairs))]
    ppermute x2 -> x0, starting transfers between devices: 3.59 us -> none  [local(): lax.ppermute(fields, 'lat', edges + [(j, i) for i, j in edges])]
    all_to_all x1, blocking collectives: 16.2 us -> 14.6 us  [local(): lax.all_to_all(coefficients, 'lat', split_axis=0, concat_axis=0, tiled=True)]
    unnamed x4 -> x5, local copies, waits for them, and re-layouts: 0.01 us -> 0.94 us
  transfers between devices with their start and end apart: 2 -> 0, of which waited for: 0 -> 0; matrix products, arithmetic and copies ran while one was open for 0% -> 0% of each run, Pallas kernels for 13% -> 0%
where the time goes in v7:
time: 44.7 us; the launch traced here: 44.5 us
  blocking collectives  31.9 us (71%)
  Pallas kernels  11.1 us (25%)
  local copies, waits for them, and re-layouts  1.34 us (3%)
    all_gather x2, blocking collectives, local(): sides.append(lax.all_gather(fields, 'lat', axis_index_groups=pairs))  15.4 us
    all_to_all x1, blocking collectives, local(): lax.all_to_all(coefficients, 'lat', split_axis=0, concat_axis=0, tiled=True)  14.6 us
    pallas_call x1, Pallas kernels, local(): pl.pallas_call(functools.partial(near_kernel, pair_count * owners, pair_c...  4.39 us
    pallas_call x1, Pallas kernels, local(): pl.pallas_call(far_kernel, out_shape=jax.ShapeDtypeStruct((owners, 2 * SU...  3.67 us
    pallas_call x1, Pallas kernels, local(): pl.pallas_call(functools.partial(legendre_kernel, level_count, field_coun...  3.02 us
    all_gather x1, blocking collectives, local(): totals = lax.all_gather(total, 'lev')  1.85 us
    unnamed x5, local copies, waits for them, and re-layouts  0.94 us

profile of v7, /device:TPU:0, one launch (start us, length us, event | category | flops | bytes accessed | tf_op | source)
XLA Modules:
  0.0 44.5 jit_solution(16229362545704837762)
XLA Ops:
  0.0 0.9 %copy.8 = bf16[2,4,2,2816]{3,1,2,0:T(4,128)(2,1)S(1)} copy(bf16[2,4,2,2816]{3,2,1,0:T(2,128)(2,1)} %fields_far.1) | data formatting | bytes 180224 | tf_op args[0]
  0.9 10.2 %all-gather.1 = bf16[4,4,2,2816]{3,1,2,0:T(4,128)(2,1)S(1)} all-gather(bf16[2,4,2,2816]{3,1,2,0:T(4,128)(2,1)S(1)} %copy.8), channel_id=3, replica_groups={{2,4},{6,8},{10,12},{14,16},{18,20},{22,24},{26,28},{30,0},{3,5},{7,9},..., dimensions={0}, use_global_device_ids=true | all-gather | bytes 270336 | tf_op jit(solution)/shard_map/all_gather | solution.py:370
  11.1 5.2 %all-gather = bf16[4,4,2,2816]{3,1,2,0:T(4,128)(2,1)S(1)} all-gather(bf16[2,4,2,2816]{3,1,2,0:T(4,128)(2,1)S(1)} %copy.8), channel_id=2, replica_groups={{0,2},{4,6},{8,10},{12,14},{16,18},{20,22},{24,26},{28,30},{1,3},{5,7},..., dimensions={0}, use_global_device_ids=true | all-gather | bytes 270336 | tf_op jit(solution)/shard_map/all_gather | solution.py:370
  16.3 0.1 copy.11
  16.5 0.0 copy-start.1
  16.5 0.1 copy.9
  16.6 0.0 copy-start
  16.6 4.4 %near_rows.1 = (f32[2,11,8,256]{3,2,1,0:T(8,128)S(1)}, bf16[2,256,2560]{2,1,0:T(8,128)(2,1)S(1)}, f32[2,11,2560]{2,1,0:T(8,128)S(1)}, s32[2,4,22,1,128]{4,3,2,1,0:T(1,128)S(1)}, f32[704,128]{1,0:T(8,128)S(1)}) custom-call(s32[2]{0:T(128)} %rows_first_far.3, s32[32]{0:T(128)} %points_far.3, bf16[2,4,2,2816]{3,2,1,0:T(2,128)(2,1)} %fields_far.1, ...), custom_call_target="tpu_custom_call" | custom-call | flops 10000000 | bytes 4000000 | tf_op jit(solution)/shard_map/near_rows/pallas_call | solution.py:380
  21.0 3.7 %far_rows.1 = bf16[16,32,128]{2,1,0:T(8,128)(2,1)S(1)} custom-call(s32[2]{0:T(128)} %rows_first_far.3, s32[32]{0:T(128)} %points_far.3, bf16[2,2,4,2,2816]{4,3,2,1,0:T(2,128)(2,1)S(1)} %bitcast.14, bf16[2,2,4,2,2816]{4,3,2,1,0:T(2,128)(2,1)S(1)} %bitcast.13, s32[2,4,22,1,128]{4,3,2,1,0:T(1,128)S(1)} %get-tuple-element.10.begins, ...), custom_call_target="tpu_custom_call" | custom-call | tf_op jit(solution)/shard_map/far_rows/pallas_call | solution.py:405
  24.7 14.6 %all_to_all.5.received = bf16[16,32,128]{2,1,0:T(8,128)(2,1)S(1)} all-to-all(bf16[16,32,128]{2,1,0:T(8,128)(2,1)S(1)} %far_rows.1), channel_id=1, replica_groups=mesh['lat'=16,'lev'=2] {'lat'}, dimensions={0} | all-to-all | bytes 262144 | tf_op jit(solution)/shard_map/all_to_all | solution.py:422
  39.3 0.1 fusion.1
  39.4 0.0 copy-done.1
  39.5 0.2 fusion
  39.6 1.9 %all-gather.2 = f32[4,32,128]{2,1,0:T(8,128)S(1)} all-gather(f32[2,32,128]{2,1,0:T(8,128)S(1)} %copy.14), channel_id=4, replica_groups=mesh['lat'=16,'lev'=2] {'lev'}, dimensions={0}, use_global_device_ids=true | all-gather | bytes 98304 | tf_op jit(solution)/shard_map/all_gather | solution.py:426
  41.5 0.0 copy-done
  41.5 3.0 %degree_sums.1 = bf16[2,5,2,40,1281]{4,3,2,1,0:T(8,128)(2,1)} custom-call(f32[2]{0:T(128)S(1)} %copy-done.1, bf16[16,32,128]{2,1,0:T(8,128)(2,1)S(1)} %all_to_all.5.received, f32[2,2,32,128]{3,2,1,0:T(8,128)S(1)} %bitcast.15, bf16[40,32,1281]{2,1,0:T(8,128)(2,1)S(1)} %copy-done), custom_call_target="tpu_custom_call" | custom-call | tf_op jit(solution)/shard_map/degree_sums/pallas_call | solution.py:431
  (1 shorter events, 0.0 us)
Async XLA Ops:
  16.5 23.0 %copy-start.1 = (f32[2]{0:T(128)S(1)}, f32[2]{0:T(128)}, u32[]{:S(2)}) copy-start(f32[2]{0:T(128)} %thickness.1) | copy-start | bytes 28
  16.6 24.9 %copy-start = (bf16[40,32,1281]{2,1,0:T(8,128)(2,1)S(1)}, bf16[40,32,1281]{2,1,0:T(8,128)(2,1)}, u32[]{:S(2)}) copy-start(bf16[40,32,1281]{2,1,0:T(8,128)(2,1)} %legendre.1) | copy-start | bytes 9838084

commit v8 on v5

--- a/solution.py
+++ b/solution.py
@@ -99,30 +99,22 @@
                 at += rows
 
 
-def gathered(couple, latitude, picks, ext, begins, factors):
-    totals = [jnp.zeros((SUB, LANES), jnp.float32) for _ in range(2)]
-    couples = begins.shape[2] // 2
-    for row, slot in picks:
-        at = ((latitude * STENCIL + row) * couples + couple) * SUB
-        scale = factors[pl.ds(pl.multiple_of(at, SUB), SUB), :]
-        parts = [ext[slot, 2 * couple + piece] for piece in range(4)]
-        for side in range(2):
-            start = jnp.broadcast_to(begins[latitude, row, 2 * couple + side], (SUB, LANES))
-            for column in range(4):
-                place = start + column
-                lane = place & (LANES - 1)
-                low, middle, high = [
-                    lane_gather(part, lane) for part in parts[side : side + 3]
-                ]
-                value = jnp.where(place < LANES, low, jnp.where(place < 2 * LANES, middle, high))
-                line = STENCIL * side + column
-                totals[side] = totals[side] + scale[line : line + 1] * value
+def gathered(totals, starts, scale, parts):
+    for side in range(2):
+        start = jnp.broadcast_to(starts[side], (SUB, LANES))
+        for column in range(4):
+            place = start + column
+            lane = place & (LANES - 1)
+            low, middle, high = [lane_gather(part, lane) for part in parts[side : side + 3]]
+            value = jnp.where(place < LANES, low, jnp.where(place < 2 * LANES, middle, high))
+            line = STENCIL * side + column
+            totals[side] = totals[side] + scale[line : line + 1] * value
     return totals
 
 
 def near_kernel(
     pair_total, pair_count, rows_first_far, points_far, fields_far, starts_far, weights_far,
-    partial, table, twiddle, begins, factors,
+    partial, table, twiddle, begins, factors, facts,
     rows_first, points, fields, starts, weights, lines, ext, arrived,
 ):
     lat_count, couples = partial.shape[:2]
@@ -175,6 +167,13 @@
                 table[latitude, rows, there] = turned[1].astype(jnp.bfloat16)
     for fetch in fetches[1:]:
         fetch.wait()
+    known = [first_lat - rows_first[latitude] for latitude in range(lat_count)]
+    known += [points[first_lat + latitude] for latitude in range(lat_count)]
+    for place in range(-lat_count, 2 * lat_count):
+        if place < 0 or place >= lat_count:
+            place = jnp.clip(first_lat + place, 0, points.shape[0] - 1)
+            known.append(lon - points[place])
+    facts[...] = jnp.concatenate([jnp.full((1, LANES), one, jnp.int32) for one in known], axis=0)
     spread_rows(starts, begins)
     spread_lines(weights, factors)
     spread_lines(fields, lines)
@@ -182,59 +181,69 @@
         extend(lines, latitude, lat_count, lon - points[first_lat + latitude], ext, latitude)
     for latitude in range(lat_count):
         mine = first_lat - rows_first[latitude]
-        picks = [(mine + row, row) for row in range(lat_count)]
         for couple in range(couples):
-            totals = gathered(couple, latitude, picks, ext, begins, factors)
+            totals = [jnp.zeros((SUB, LANES), jnp.float32) for _ in range(2)]
+            for slot in range(lat_count):
+                row = mine + slot
+                at = ((latitude * STENCIL + row) * couples + couple) * SUB
+                totals = gathered(
+                    totals,
+                    [begins[latitude, row, 2 * couple + side] for side in range(2)],
+                    factors[pl.ds(pl.multiple_of(at, SUB), SUB), :],
+                    [ext[slot, 2 * couple + piece] for piece in range(4)],
+                )
             for side in range(2):
                 partial[latitude, couple, :, side * LANES : (side + 1) * LANES] = totals[side]
 
 
 def far_kernel(
-    rows_first_far, points_far, near_side, far_side, begins, factors, partial, table, twiddle,
-    out, rows_first, points, lines, ext, grid, waves, arrived,
+    near_side, far_side, begins, factors, facts, partial, table, twiddle,
+    out, lines, ext, grid, waves,
 ):
-    fetches = [
-        pltpu.make_async_copy(points_far, points, arrived.at[0]),
-        pltpu.make_async_copy(rows_first_far, rows_first, arrived.at[1]),
-    ]
-    for fetch in fetches:
-        fetch.start()
     lat_count, couples = partial.shape[:2]
-    lon = 2 * couples * LANES
     columns = table.shape[2] // 2
     owners = out.shape[0]
-    first_lat = lax.axis_index("lat") * lat_count
-    lat_total = points.shape[0]
     toward = 1 - lax.axis_index("lat") % 2
     spread_lines(near_side, lines.at[toward])
     spread_lines(far_side, lines.at[1 - toward])
-    for fetch in fetches:
-        fetch.wait()
-    for side in range(2):
-        for row in range(lat_count):
-            if side == 0:
-                place = jnp.maximum(first_lat - lat_count + row, 0)
-            else:
-                place = jnp.minimum(first_lat + lat_count + row, lat_total - 1)
-            extend(
-                lines.at[side], row, lat_count, lon - points[place], ext, side * lat_count + row
-            )
+    fact = [jnp.broadcast_to(facts[row : row + 1], (SUB, LANES)) for row in range(4 * lat_count)]
+    for slot in range(2 * lat_count):
+        side, row = divmod(slot, lat_count)
+        extend(lines.at[side], row, lat_count, fact[2 * lat_count + slot], ext, slot)
     lane = lax.broadcasted_iota(jnp.int32, (SUB, LANES), 1)
     width = 256
-    for latitude in range(lat_count):
-        mine = first_lat - rows_first[latitude]
-        one_row = jnp.where(mine >= 1, 0, 2)
-        two_row = jnp.where(mine <= 1, 3, 1)
-        picks = []
-        for row in (one_row, two_row):
-            picks.append((row, jnp.where(row < mine, row - mine + lat_count, row - mine)))
+    choices = (((2, 0, 0), (2, 1, 0)), ((3, 3, 1), (3, 2, 1)))
+    for latitude in range(lat_count):
+        at_zero = fact[latitude] == 0
+        at_one = fact[latitude] == 1
+
+        def pick(values):
+            return jnp.where(at_zero, values[0], jnp.where(at_one, values[1], values[2]))
+
+        def pick_line(values):
+            return jnp.where(
+                at_zero[:1], values[0], jnp.where(at_one[:1], values[1], values[2])
+            )
+
         for couple in range(couples):
-            totals = gathered(couple, latitude, picks, ext, begins, factors)
+            sides = [pl.ds(side * LANES, LANES) for side in range(2)]
+            totals = [partial[latitude, couple, :, lanes] for lanes in sides]
+            for rows, slots in choices:
+                scales = [
+                    factors[pl.ds(((latitude * STENCIL + row) * couples + couple) * SUB, SUB), :]
+                    for row in rows
+                ]
+                starts = [
+                    pick_line([begins[latitude, row, 2 * couple + side] for row in rows])
+                    for side in range(2)
+                ]
+                parts = [
+                    pick([ext[slot, 2 * couple + piece] for slot in slots]) for piece in range(4)
+                ]
+                totals = gathered(totals, starts, pick(scales), parts)
             for side in range(2):
-                lanes = pl.ds(side * LANES, LANES)
-                live = lane + (2 * couple + side) * LANES < points[first_lat + latitude]
-                value = partial[latitude, couple, :, lanes] + totals[side]
-                grid[latitude, couple, :, lanes] = jnp.where(live, value, 0.0)
+                live = lane + (2 * couple + side) * LANES < fact[lat_count + latitude]
+                grid[latitude, couple, :, sides[side]] = jnp.where(live, totals[side], 0.0)
     for latitude in range(lat_count):
         rows = grid[latitude].reshape(couples * SUB, 2 * LANES).astype(jnp.bfloat16)
         for at in range(0, columns, width):
@@ -265,7 +274,7 @@
 
 
 def legendre_kernel(
-    level_count, field_count, thickness, received, totals, legendre, out, wide, left, planes, sent,
+    level_owners, level_count, field_count, thickness, received, totals, legendre, out, wide, left, planes, sent,
 ):
     owners = received.shape[0]
     lat_total = wide.shape[0] // (2 * SUB)
@@ -279,8 +288,9 @@
     lines = {}
     for part in range(2):
         running = jnp.zeros((lat_total, LANES), jnp.float32)
-        for other in range(1, totals.shape[0]):
-            running = running + jnp.where(other > level_place, totals[other, part], 0.0)
+        for place in range(totals.shape[0]):
+            other = 1 - level_place if level_owners == 2 else place
+            running = running + jnp.where(other > level_place, totals[place, part], 0.0)
         for level in reversed(range(level_count)):
             for field in range(field_count):
                 place = part * SUB + level * field_count + field
@@ -373,11 +383,7 @@
     vector = pl.BlockSpec(memory_space=pltpu.VMEM)
     params = pltpu.CompilerParams(vmem_limit_bytes=LIMIT)
     remote = pl.BlockSpec(memory_space=pltpu.HBM)
-    scalars = [
-        pltpu.SMEM(rows_first.shape, jnp.int32),
-        pltpu.SMEM(points.shape, jnp.int32),
-    ]
-    partial, table, twiddle, begins, factors = pl.pallas_call(
+    partial, table, twiddle, begins, factors, facts = pl.pallas_call(
         functools.partial(near_kernel, pair_count * owners, pair_count),
         out_shape=(
             jax.ShapeDtypeStruct((lat_count, couples, SUB, 2 * LANES), jnp.float32),
@@ -385,11 +391,13 @@
             jax.ShapeDtypeStruct((lat_count, couples, 2 * columns), jnp.float32),
             jax.ShapeDtypeStruct((lat_count, STENCIL, blocks, 1, LANES), jnp.int32),
             jax.ShapeDtypeStruct((weights.size // LANES, LANES), jnp.float32),
+            jax.ShapeDtypeStruct((4 * lat_count, LANES), jnp.int32),
         ),
         in_specs=[remote] * 5,
-        out_specs=(vector,) * 5,
-        scratch_shapes=scalars
-        + [
+        out_specs=(vector,) * 6,
+        scratch_shapes=[
+            pltpu.SMEM(rows_first.shape, jnp.int32),
+            pltpu.SMEM(points.shape, jnp.int32),
             pltpu.VMEM(fields.shape, fields.dtype),
             pltpu.VMEM(starts.shape, starts.dtype),
             pltpu.VMEM(weights.shape, weights.dtype),
@@ -405,31 +413,33 @@
     coefficients = pl.pallas_call(
         far_kernel,
         out_shape=jax.ShapeDtypeStruct((owners, 2 * SUB * lat_count, LANES), jnp.bfloat16),
-        in_specs=[remote] * 2 + [vector] * 7,
+        in_specs=[vector] * 8,
         out_specs=vector,
-        scratch_shapes=scalars
-        + [
+        scratch_shapes=[
             pltpu.VMEM((2, fields.size // LANES, LANES), jnp.float32),
             pltpu.VMEM((2 * lat_count, blocks + 2, SUB, LANES), jnp.float32),
             pltpu.VMEM((lat_count, couples, SUB, 2 * LANES), jnp.float32),
             pltpu.VMEM((lat_count, 2 * SUB, columns + LANES), jnp.float32),
-            pltpu.SemaphoreType.DMA((2,)),
         ],
         compiler_params=params,
         name="far_rows",
-    )(held(rows_first), held(points), *sides, begins, factors, partial, table, twiddle)
+    )(*sides, begins, factors, facts, partial, table, twiddle)
 
     received = lax.all_to_all(coefficients, "lat", split_axis=0, concat_axis=0, tiled=True)
     by_level = received.reshape(lat_total, 2, level_count, field_count, LANES).astype(jnp.float32)
     virtual = by_level[:, :, :, 2] + 0.61 * by_level[:, :, :, 3]
     total = jnp.sum(thickness[None, None, :, None] * virtual, axis=2).transpose(1, 0, 2)
-    totals = lax.all_gather(total, "lev")
+    level_owners = lax.axis_size("lev")
+    if level_owners == 2:
+        totals = lax.ppermute(total, "lev", [(0, 1), (1, 0)])[None]
+    else:
+        totals = lax.all_gather(total, "lev")
 
     out_shape = (level_count, field_count + 1, 2, pair_count, degrees)
     half = level_count * (field_count + 1) * 2 * SUB
     group_count = (pair_count + SUB - 1) // SUB
     return pl.pallas_call(
-        functools.partial(legendre_kernel, level_count, field_count),
+        functools.partial(legendre_kernel, level_owners, level_count, field_count),
         out_shape=jax.ShapeDtypeStruct(out_shape, jnp.bfloat16),
         in_specs=[scalar, vector, vector, vector],
         out_specs=pl.BlockSpec(memory_space=pl.ANY),

time: 33.2 us -> 31.9 us (0.961)
  blocking collectives: 18.1 us -> 16.2 us
  waiting for transfers between devices: 0.01 us -> 1.2 us
  Pallas kernels: 11 us -> 10.3 us
    all_gather x1 -> x0, blocking collectives: 1.85 us -> none  [local(): totals = lax.all_gather(total, 'lev')]
    ppermute x0 -> x1, waiting for transfers between devices: none -> 1.19 us  [local(): totals = lax.ppermute(total, 'lev', [(0, 1), (1, 0)])[None]]
    pallas_call x1, Pallas kernels: 3.67 us -> 3 us  [local(): pl.pallas_call(far_kernel, out_shape=jax.ShapeDtypeStruct((owners, 2 * SU...]
  transfers between devices with their start and end apart: 2 -> 3, of which waited for: 0 -> 1; matrix products, arithmetic and copies ran while one was open for 0% -> 0% of each run, Pallas kernels for 13% -> 13%
where the time goes in v8:
time: 31.9 us; the launch traced here: 31.8 us
  blocking collectives  16.2 us (51%)
  Pallas kernels  10.3 us (32%)
  starting transfers between devices  3.66 us (11%)
  waiting for transfers between devices  1.2 us (4%)
    all_to_all x1, blocking collectives, local(): lax.all_to_all(coefficients, 'lat', split_axis=0, concat_axis=0, tiled=True)  16.2 us
    pallas_call x1, Pallas kernels, local(): pl.pallas_call(functools.partial(near_kernel, pair_count * owners, pair_c...  4.26 us
    ppermute x2, starting transfers between devices, local(): lax.ppermute(fields, 'lat', edges + [(j, i) for i, j in edges])  3.59 us
    pallas_call x1, Pallas kernels, local(): pl.pallas_call(functools.partial(legendre_kernel, level_owners, level_cou...  3.04 us
    pallas_call x1, Pallas kernels, local(): pl.pallas_call(far_kernel, out_shape=jax.ShapeDtypeStruct((owners, 2 * SU...  3 us
    ppermute x1, waiting for transfers between devices, local(): totals = lax.ppermute(total, 'lev', [(0, 1), (1, 0)])[None]  1.19 us
  transfers between devices with their start and end apart: 3, of which 1 were waited for; matrix products, arithmetic and copies ran while one was open for 0% of the time, Pallas kernels for 13%

profile of v8, /device:TPU:0, one launch (start us, length us, event | category | flops | bytes accessed | tf_op | source)
XLA Modules:
  0.0 31.8 jit_solution(7613254498621986527)
XLA Ops:
  0.0 0.0 copy-start.1
  0.0 0.0 copy-start
  0.0 2.9 %collective-permute-start = (bf16[2,4,2,2816]{3,2,1,0:T(2,128)(2,1)}, bf16[2,4,2,2816]{3,2,1,0:T(2,128)(2,1)S(1)}, u32[]{:S(2)}, u32[]{:S(2)}) collective-permute-start(bf16[2,4,2,2816]{3,2,1,0:T(2,128)(2,1)} %fields_far.1), channel_id=1, source_target_pairs={{0,2},{4,6},{8,10},{12,14},{16,18},{20,22},{24,26},{28,30},{2,0},{... | collective-permute-start | bytes 270344 | tf_op jit(solution)/shard_map/ppermute | solution.py:380
  2.9 0.7 %collective-permute-start.1 = (bf16[2,4,2,2816]{3,2,1,0:T(2,128)(2,1)}, bf16[2,4,2,2816]{3,2,1,0:T(2,128)(2,1)S(1)}, u32[]{:S(2)}, u32[]{:S(2)}) collective-permute-start(bf16[2,4,2,2816]{3,2,1,0:T(2,128)(2,1)} %fields_far.1), channel_id=1, source_target_pairs={{2,4},{6,8},{10,12},{14,16},{18,20},{22,24},{26,28},{4,2},{8,6},{1... | collective-permute-start | bytes 270344 | tf_op jit(solution)/shard_map/ppermute | solution.py:380
  3.6 4.3 %near_rows.1 = (f32[2,11,8,256]{3,2,1,0:T(8,128)S(1)}, bf16[2,256,2560]{2,1,0:T(8,128)(2,1)S(1)}, f32[2,11,2560]{2,1,0:T(8,128)S(1)}, s32[2,4,22,1,128]{4,3,2,1,...) custom-call(s32[2]{0:T(128)} %rows_first_far.1, s32[32]{0:T(128)} %points_far.1, ...), custom_call_target="tpu_custom_call" | custom-call | flops 10000000 | bytes 4000000 | tf_op jit(solution)/shard_map/near_rows/pallas_call | solution.py:386
  7.9 0.0 collective-permute-done.near_side
  7.9 0.0 collective-permute-done.1.far_side
  7.9 3.0 %far_rows.1 = bf16[16,32,128]{2,1,0:T(8,128)(2,1)S(1)} custom-call(bf16[2,4,2,2816]{3,2,1,0:T(2,128)(2,1)S(1)} %collective-permute-done.near_side, bf16[2,4,2,2816]{3,2,1,0:T(2,128)(2,1)S(1)} %collective-permute-done.1.far_side, s32[2,4,22,1,128]{4,3,2,1,0:T(1,128)S(1)} %get-tuple-element.11.begins, f32[704,128]{1,0:T(8,128)S(1)} %get-tuple-element.12.factors, ...), custom_call_target="tpu_custom_call" | custom-call | tf_op jit(solution)/shard_map/far_rows/pallas_call | solution.py:413
  10.9 16.2 %all_to_all.5.received = bf16[16,32,128]{2,1,0:T(8,128)(2,1)S(1)} all-to-all(bf16[16,32,128]{2,1,0:T(8,128)(2,1)S(1)} %far_rows.1), channel_id=1, replica_groups=mesh['lat'=16,'lev'=2] {'lat'}, dimensions={0} | all-to-all | bytes 262144 | tf_op jit(solution)/shard_map/all_to_all | solution.py:428
  27.1 0.1 fusion.1
  27.2 0.0 copy-done.1
  27.3 0.2 fusion
  27.4 0.1 collective-permute-start.2
  27.5 1.2 %collective-permute-done.2 = f32[2,32,128]{2,1,0:T(8,128)S(1)} collective-permute-done((f32[2,32,128]{2,1,0:T(8,128)S(1)}, f32[2,32,128]{2,1,0:T(8,128)S(1)}, u32[]{:S(2)}, u32[]{:S(2)}) %collective-permute-start.2) | collective-permute-done | bytes 32800 | tf_op jit(solution)/shard_map/ppermute | solution.py:434
  28.7 0.0 copy-done
  28.7 3.0 %degree_sums.1 = bf16[2,5,2,40,1281]{4,3,2,1,0:T(8,128)(2,1)} custom-call(f32[2]{0:T(128)S(1)} %copy-done.1, bf16[16,32,128]{2,1,0:T(8,128)(2,1)S(1)} %all_to_all.5.received, f32[1,2,32,128]{3,2,1,0:T(8,128)S(1)} %bitcast.13, bf16[40,32,1281]{2,1,0:T(8,128)(2,1)S(1)} %copy-done), custom_call_target="tpu_custom_call" | custom-call | tf_op jit(solution)/shard_map/degree_sums/pallas_call | solution.py:441
  (1 shorter events, 0.0 us)
Async XLA Ops:
  0.0 27.3 %copy-start.1 = (f32[2]{0:T(128)S(1)}, f32[2]{0:T(128)}, u32[]{:S(2)}) copy-start(f32[2]{0:T(128)} %thickness.1) | copy-start | bytes 28
  0.0 28.7 %copy-start = (bf16[40,32,1281]{2,1,0:T(8,128)(2,1)S(1)}, bf16[40,32,1281]{2,1,0:T(8,128)(2,1)}, u32[]{:S(2)}) copy-start(bf16[40,32,1281]{2,1,0:T(8,128)(2,1)} %legendre.1) | copy-start | bytes 9838084
  0.0 7.9 %collective-permute-start = (bf16[2,4,2,2816]{3,2,1,0:T(2,128)(2,1)}, bf16[2,4,2,2816]{3,2,1,0:T(2,128)(2,1)S(1)}, u32[]{:S(2)}, u32[]{:S(2)}) collective-permute-start(bf16[2,4,2,2816]{3,2,1,0:T(2,128)(2,1)} %fields_far.1), channel_id=1, source_target_pairs={{0,2},{4,6},{8,10},{12,14},{16,18},{20,22},{24,26},{28,30},{2,0},{... | collective-permute-start | bytes 270344 | tf_op jit(solution)/shard_map/ppermute | solution.py:380
  2.9 4.9 %collective-permute-start.1 = (bf16[2,4,2,2816]{3,2,1,0:T(2,128)(2,1)}, bf16[2,4,2,2816]{3,2,1,0:T(2,128)(2,1)S(1)}, u32[]{:S(2)}, u32[]{:S(2)}) collective-permute-start(bf16[2,4,2,2816]{3,2,1,0:T(2,128)(2,1)} %fields_far.1), channel_id=1, source_target_pairs={{2,4},{6,8},{10,12},{14,16},{18,20},{22,24},{26,28},{4,2},{8,6},{1... | collective-permute-start | bytes 270344 | tf_op jit(solution)/shard_map/ppermute | solution.py:380
  27.4 1.3 %collective-permute-start.2 = (f32[2,32,128]{2,1,0:T(8,128)S(1)}, f32[2,32,128]{2,1,0:T(8,128)S(1)}, u32[]{:S(2)}, u32[]{:S(2)}) collective-permute-start(f32[2,32,128]{2,1,0:T(8,128)S(1)} %bitcast.16), channel_id=1, source_target_pairs={{0,1},{1,0},{2,3},{3,2},{4,5},{5,4},{6,7},{7,6},{8,9},{9,8},{10,11... | collective-permute-start | bytes 98312 | tf_op jit(solution)/shard_map/ppermute | solution.py:434

commit v9 on v8

--- a/solution.py
+++ b/solution.py
@@ -113,9 +113,9 @@
 
 
 def near_kernel(
-    pair_total, pair_count, rows_first_far, points_far, fields_far, starts_far, weights_far,
-    partial, table, twiddle, begins, factors, facts,
-    rows_first, points, fields, starts, weights, lines, ext, arrived,
+    pair_total, pair_count, rows_first_far, points_far, fields_far, starts_far, weights_far, side,
+    partial, table, twiddle, begins, factors, facts, beside,
+    rows_first, points, fields, starts, weights, lines, side_lines, ext, arrived,
 ):
     lat_count, couples = partial.shape[:2]
     lon = 2 * couples * LANES
@@ -135,7 +135,20 @@
     ]
     for fetch in fetches:
         fetch.start()
-    fetches[0].wait()
+    spread_lines(side, side_lines)
+    for fetch in fetches[:2]:
+        fetch.wait()
+    known = [first_lat - rows_first[latitude] for latitude in range(lat_count)]
+    known += [points[first_lat + latitude] for latitude in range(lat_count)]
+    for place in range(-lat_count, 2 * lat_count):
+        if place < 0 or place >= lat_count:
+            place = jnp.clip(first_lat + place, 0, points.shape[0] - 1)
+            known.append(lon - points[place])
+    facts[...] = jnp.concatenate([jnp.full((1, LANES), one, jnp.int32) for one in known], axis=0)
+    upper = lax.axis_index("lat") % 2 == 0
+    for row in range(lat_count):
+        missing = jnp.where(upper, known[3 * lat_count + row], known[2 * lat_count + row])
+        extend(side_lines, row, lat_count, missing, beside, row)
     width = 256
     scales = []
     for latitude in range(lat_count):
@@ -165,15 +178,8 @@
                 rows = slice(HALF * quarter, HALF * (quarter + 1))
                 table[latitude, rows, here] = turned[0].astype(jnp.bfloat16)
                 table[latitude, rows, there] = turned[1].astype(jnp.bfloat16)
-    for fetch in fetches[1:]:
+    for fetch in fetches[2:]:
         fetch.wait()
-    known = [first_lat - rows_first[latitude] for latitude in range(lat_count)]
-    known += [points[first_lat + latitude] for latitude in range(lat_count)]
-    for place in range(-lat_count, 2 * lat_count):
-        if place < 0 or place >= lat_count:
-            place = jnp.clip(first_lat + place, 0, points.shape[0] - 1)
-            known.append(lon - points[place])
-    facts[...] = jnp.concatenate([jnp.full((1, LANES), one, jnp.int32) for one in known], axis=0)
     spread_rows(starts, begins)
     spread_lines(weights, factors)
     spread_lines(fields, lines)
@@ -197,19 +203,19 @@
 
 
 def far_kernel(
-    near_side, far_side, begins, factors, facts, partial, table, twiddle,
-    out, lines, ext, grid, waves,
+    beside, far_side, begins, factors, facts, partial, table, twiddle,
+    out, lines, ext, grid, waves, packed,
 ):
     lat_count, couples = partial.shape[:2]
     columns = table.shape[2] // 2
     owners = out.shape[0]
+    fact = [jnp.broadcast_to(facts[row : row + 1], (SUB, LANES)) for row in range(4 * lat_count)]
     toward = 1 - lax.axis_index("lat") % 2
-    spread_lines(near_side, lines.at[toward])
-    spread_lines(far_side, lines.at[1 - toward])
-    fact = [jnp.broadcast_to(facts[row : row + 1], (SUB, LANES)) for row in range(4 * lat_count)]
-    for slot in range(2 * lat_count):
-        side, row = divmod(slot, lat_count)
-        extend(lines.at[side], row, lat_count, fact[2 * lat_count + slot], ext, slot)
+    ext[pl.ds(toward * lat_count, lat_count)] = beside[...]
+    spread_lines(far_side, lines)
+    for row in range(lat_count):
+        missing = jnp.where(toward == 1, fact[2 * lat_count + row], fact[3 * lat_count + row])
+        extend(lines, row, lat_count, missing, ext, (1 - toward) * lat_count + row)
     lane = lax.broadcasted_iota(jnp.int32, (SUB, LANES), 1)
     width = 256
     choices = (((2, 0, 0), (2, 1, 0)), ((3, 3, 1), (3, 2, 1)))
@@ -265,44 +271,63 @@
                 sine = sine - (real[here] * turn_sin + imag[here] * turn_cos)
             waves[latitude, 0:SUB, at : at + width] = cosine
             waves[latitude, SUB : 2 * SUB, at : at + width] = sine
-        waves[latitude, :, columns:] = jnp.zeros((2 * SUB, waves.shape[2] - columns), jnp.float32)
-        used = columns // owners
-        for owner in range(owners):
-            out[owner, 2 * SUB * latitude : 2 * SUB * (latitude + 1), :] = waves[
-                latitude, :, owner * used : owner * used + LANES
-            ].astype(jnp.bfloat16)
+    used = columns // owners
+    for owner in range(owners):
+        for latitude in range(lat_count):
+            for part in range(2):
+                place = (2 * latitude + part) * used
+                packed[owner, :, place : place + used] = waves[
+                    latitude, part * SUB : (part + 1) * SUB, owner * used : (owner + 1) * used
+                ]
+        rest = packed.shape[2] - 2 * lat_count * used
+        if rest > 0:
+            packed[owner, :, packed.shape[2] - rest :] = jnp.zeros((SUB, rest), jnp.float32)
+        out[owner] = packed[owner].astype(jnp.bfloat16)
 
 
 def legendre_kernel(
     level_owners, level_count, field_count, thickness, received, totals, legendre, out, wide, left, planes, sent,
 ):
     owners = received.shape[0]
-    lat_total = wide.shape[0] // (2 * SUB)
-    pair_count, _, degrees = legendre.shape
+    pair_count, lat_total, degrees = legendre.shape
+    lat_count = lat_total // owners
+    used = 2 * pair_count
     pair_total = pair_count * owners
     groups = [(at, min(SUB, pair_count - at)) for at in range(0, pair_count, SUB)]
+    reach = pair_count + len(groups) * SUB
     keys = [(field, part) for field in range(field_count + 1) for part in range(2)]
     level_place = lax.axis_index("lev")
     first_pair = lax.axis_index("lat") * pair_count
-    wide[...] = received[...].astype(jnp.float32).reshape(wide.shape)
+    lane_blocks = wide.shape[0]
+    for block in range(lane_blocks):
+        values = received[:, :, block * LANES : (block + 1) * LANES].astype(jnp.float32)
+        wide[block] = values.reshape(wide.shape[1:])
+
+
+    def unpacked(values, part):
+        places = [(2 * latitude + part) * used for latitude in range(lat_count)]
+        return jnp.concatenate([values[:, place : place + reach] for place in places], axis=0)
+
     lines = {}
     for part in range(2):
-        running = jnp.zeros((lat_total, LANES), jnp.float32)
+        running = jnp.zeros((lat_total, reach), jnp.float32)
         for place in range(totals.shape[0]):
             other = 1 - level_place if level_owners == 2 else place
-            running = running + jnp.where(other > level_place, totals[place, part], 0.0)
+            running = running + jnp.where(other > level_place, unpacked(totals[place], part), 0.0)
         for level in reversed(range(level_count)):
             for field in range(field_count):
-                place = part * SUB + level * field_count + field
-                lines[level, field, part] = wide[pl.ds(place, lat_total, stride=2 * SUB), :]
+                rows = pl.ds(level * field_count + field, owners, stride=SUB)
+                values = [wide[block, rows, :] for block in range(lane_blocks)]
+                lines[level, field, part] = unpacked(jnp.concatenate(values, axis=1), part)
             running = running + thickness[level] * (
                 lines[level, 2, part] + 0.61 * lines[level, 3, part]
             )
             lines[level, field_count, part] = running
     depth = SUB * lat_total
+    row = lax.broadcasted_iota(jnp.int32, (lat_total, depth), 0)
+    latitude = row % owners * lat_count + row // owners
     spread = (
-        lax.broadcasted_iota(jnp.int32, (lat_total, depth), 0)
-        == lax.broadcasted_iota(jnp.int32, (lat_total, depth), 1) % lat_total
+        latitude == lax.broadcasted_iota(jnp.int32, (lat_total, depth), 1) % lat_total
     ).astype(jnp.bfloat16)
     keep = (
         lax.broadcasted_iota(jnp.int32, (SUB, depth), 0)
@@ -374,6 +399,7 @@
     couples = lon_count // (2 * LANES)
     blocks = 2 * couples
     columns = 2 * owners * pair_count
+    packed_lanes = -(-2 * lat_count * 2 * pair_count // LANES) * LANES
     sides = []
     for first in range(2):
         edges = [(i, i + 1) for i in range(first, owners - 1, 2)]
@@ -383,7 +409,7 @@
     vector = pl.BlockSpec(memory_space=pltpu.VMEM)
     params = pltpu.CompilerParams(vmem_limit_bytes=LIMIT)
     remote = pl.BlockSpec(memory_space=pltpu.HBM)
-    partial, table, twiddle, begins, factors, facts = pl.pallas_call(
+    partial, table, twiddle, begins, factors, facts, beside = pl.pallas_call(
         functools.partial(near_kernel, pair_count * owners, pair_count),
         out_shape=(
             jax.ShapeDtypeStruct((lat_count, couples, SUB, 2 * LANES), jnp.float32),
@@ -392,9 +418,10 @@
             jax.ShapeDtypeStruct((lat_count, STENCIL, blocks, 1, LANES), jnp.int32),
             jax.ShapeDtypeStruct((weights.size // LANES, LANES), jnp.float32),
             jax.ShapeDtypeStruct((4 * lat_count, LANES), jnp.int32),
+            jax.ShapeDtypeStruct((lat_count, blocks + 2, SUB, LANES), jnp.float32),
         ),
-        in_specs=[remote] * 5,
-        out_specs=(vector,) * 6,
+        in_specs=[remote] * 5 + [vector],
+        out_specs=(vector,) * 7,
         scratch_shapes=[
             pltpu.SMEM(rows_first.shape, jnp.int32),
             pltpu.SMEM(points.shape, jnp.int32),
@@ -402,33 +429,35 @@
             pltpu.VMEM(starts.shape, starts.dtype),
             pltpu.VMEM(weights.shape, weights.dtype),
             pltpu.VMEM((fields.size // LANES, LANES), jnp.float32),
+            pltpu.VMEM((fields.size // LANES, LANES), jnp.float32),
             pltpu.VMEM((lat_count, blocks + 2, SUB, LANES), jnp.float32),
             pltpu.SemaphoreType.DMA((5,)),
         ],
         compiler_params=params,
         cost_estimate=pl.CostEstimate(flops=10_000_000, bytes_accessed=4_000_000, transcendentals=0),
         name="near_rows",
-    )(*(held(value) for value in (rows_first, points, fields, starts, weights)))
+    )(*(held(value) for value in (rows_first, points, fields, starts, weights)), sides[0])
 
     coefficients = pl.pallas_call(
         far_kernel,
-        out_shape=jax.ShapeDtypeStruct((owners, 2 * SUB * lat_count, LANES), jnp.bfloat16),
+        out_shape=jax.ShapeDtypeStruct((owners, SUB, packed_lanes), jnp.bfloat16),
         in_specs=[vector] * 8,
         out_specs=vector,
         scratch_shapes=[
-            pltpu.VMEM((2, fields.size // LANES, LANES), jnp.float32),
+            pltpu.VMEM((fields.size // LANES, LANES), jnp.float32),
             pltpu.VMEM((2 * lat_count, blocks + 2, SUB, LANES), jnp.float32),
             pltpu.VMEM((lat_count, couples, SUB, 2 * LANES), jnp.float32),
-            pltpu.VMEM((lat_count, 2 * SUB, columns + LANES), jnp.float32),
+            pltpu.VMEM((lat_count, 2 * SUB, columns), jnp.float32),
+            pltpu.VMEM((owners, SUB, packed_lanes), jnp.float32),
         ],
         compiler_params=params,
         name="far_rows",
-    )(*sides, begins, factors, facts, partial, table, twiddle)
+    )(beside, sides[1], begins, factors, facts, partial, table, twiddle)
 
     received = lax.all_to_all(coefficients, "lat", split_axis=0, concat_axis=0, tiled=True)
-    by_level = received.reshape(lat_total, 2, level_count, field_count, LANES).astype(jnp.float32)
-    virtual = by_level[:, :, :, 2] + 0.61 * by_level[:, :, :, 3]
-    total = jnp.sum(thickness[None, None, :, None] * virtual, axis=2).transpose(1, 0, 2)
+    by_level = received.reshape(owners, level_count, field_count, packed_lanes).astype(jnp.float32)
+    virtual = by_level[:, :, 2] + 0.61 * by_level[:, :, 3]
+    total = jnp.sum(thickness[None, :, None] * virtual, axis=1)
     level_owners = lax.axis_size("lev")
     if level_owners == 2:
         totals = lax.ppermute(total, "lev", [(0, 1), (1, 0)])[None]
@@ -444,7 +473,7 @@
         in_specs=[scalar, vector, vector, vector],
         out_specs=pl.BlockSpec(memory_space=pl.ANY),
         scratch_shapes=[
-            pltpu.VMEM((lat_total * 2 * SUB, LANES), jnp.float32),
+            pltpu.VMEM((packed_lanes // LANES, owners * SUB, LANES), jnp.float32),
             pltpu.VMEM((group_count, 2 * half, SUB * lat_total), jnp.bfloat16),
             pltpu.VMEM(out_shape, jnp.bfloat16),
             pltpu.SemaphoreType.DMA(((degrees + 255) // 256,)),

time: 31.9 us -> 34.9 us (1.094)
  waiting for transfers between devices: 1.2 us -> 3.35 us
  local copies, waits for them, and re-layouts: 0.13 us -> 2.07 us
  blocking collectives: 16.2 us -> 14.8 us
    ppermute x2, waiting for transfers between devices: 0.01 us -> 2.17 us  [local(): lax.ppermute(fields, 'lat', edges + [(j, i) for i, j in edges])]
    unnamed x4, local copies, waits for them, and re-layouts: 0.01 us -> 2.02 us
    all_to_all x1, blocking collectives: 16.2 us -> 14.8 us  [local(): lax.all_to_all(coefficients, 'lat', split_axis=0, concat_axis=0, tiled=True)]
  transfers between devices with their start and end apart: 3 -> 3, of which waited for: 1 -> 2; matrix products, arithmetic and copies ran while one was open for 0% -> 0% of each run, Pallas kernels for 13% -> 12%
where the time goes in v9:
time: 34.9 us; the launch traced here: 34.7 us
  blocking collectives  14.8 us (42%)
  Pallas kernels  10.6 us (30%)
  starting transfers between devices  3.66 us (10%)
  waiting for transfers between devices  3.35 us (10%)
  local copies, waits for them, and re-layouts  2.07 us (6%)
    all_to_all x1, blocking collectives, local(): lax.all_to_all(coefficients, 'lat', split_axis=0, concat_axis=0, tiled=True)  14.8 us
    pallas_call x1, Pallas kernels, local(): pl.pallas_call(functools.partial(near_kernel, pair_count * owners, pair_c...  4.31 us
    ppermute x2, starting transfers between devices, local(): lax.ppermute(fields, 'lat', edges + [(j, i) for i, j in edges])  3.59 us
    pallas_call x1, Pallas kernels, local(): pl.pallas_call(functools.partial(legendre_kernel, level_owners, level_cou...  3.23 us
    pallas_call x1, Pallas kernels, local(): pl.pallas_call(far_kernel, out_shape=jax.ShapeDtypeStruct((owners, SUB, p...  3.05 us
    ppermute x2, waiting for transfers between devices, local(): lax.ppermute(fields, 'lat', edges + [(j, i) for i, j in edges])  2.17 us
    unnamed x4, local copies, waits for them, and re-layouts  2.02 us
    ppermute x1, waiting for transfers between devices, local(): totals = lax.ppermute(total, 'lev', [(0, 1), (1, 0)])[None]  1.18 us
  transfers between devices with their start and end apart: 3, of which 2 were waited for; matrix products, arithmetic and copies ran while one was open for 0% of the time, Pallas kernels for 12%

profile of v9, /device:TPU:0, one launch (start us, length us, event | category | flops | bytes accessed | tf_op | source)
XLA Modules:
  0.0 34.7 jit_solution(12871930120351063511)
XLA Ops:
  0.0 0.0 copy-start.1
  0.0 2.9 %collective-permute-start = (bf16[2,4,2,2816]{3,2,1,0:T(2,128)(2,1)}, bf16[2,4,2,2816]{3,2,1,0:T(2,128)(2,1)S(1)}, u32[]{:S(2)}, u32[]{:S(2)}) collective-permute-start(bf16[2,4,2,2816]{3,2,1,0:T(2,128)(2,1)} %fields_far.1), channel_id=1, source_target_pairs={{0,2},{4,6},{8,10},{12,14},{16,18},{20,22},{24,26},{28,30},{2,0},{... | collective-permute-start | bytes 270344 | tf_op jit(solution)/shard_map/ppermute | solution.py:406
  2.9 0.7 %collective-permute-start.1 = (bf16[2,4,2,2816]{3,2,1,0:T(2,128)(2,1)}, bf16[2,4,2,2816]{3,2,1,0:T(2,128)(2,1)S(1)}, u32[]{:S(2)}, u32[]{:S(2)}) collective-permute-start(bf16[2,4,2,2816]{3,2,1,0:T(2,128)(2,1)} %fields_far.1), channel_id=1, source_target_pairs={{2,4},{6,8},{10,12},{14,16},{18,20},{22,24},{26,28},{4,2},{8,6},{1... | collective-permute-start | bytes 270344 | tf_op jit(solution)/shard_map/ppermute | solution.py:406
  3.6 2.2 %collective-permute-done.side = bf16[2,4,2,2816]{3,2,1,0:T(2,128)(2,1)S(1)} collective-permute-done((bf16[2,4,2,2816]{3,2,1,0:T(2,128)(2,1)}, bf16[2,4,2,2816]{3,2,1,0:T(2,128)(2,1)S(1)}, u32[]{:S(2)}, u32[]{:S(2)}) %collective-permute-start) | collective-permute-done | bytes 90144 | tf_op jit(solution)/shard_map/ppermute | solution.py:406
  5.8 4.3 %near_rows.1 = (f32[2,11,8,256]{3,2,1,0:T(8,128)S(1)}, bf16[2,256,2560]{2,1,0:T(8,128)(2,1)S(1)}, f32[2,11,2560]{2,1,0:T(8,128)S(1)}, s32[2,4,22,1,128]{4,3,2,1,...) custom-call(s32[2]{0:T(128)} %rows_first_far.1, s32[32]{0:T(128)} %points_far.1, ...), custom_call_target="tpu_custom_call" | custom-call | flops 10000000 | bytes 4000000 | tf_op jit(solution)/shard_map/near_rows/pallas_call | solution.py:412
  10.1 0.0 collective-permute-done.1.far_side
  10.1 3.0 %far_rows.1 = bf16[16,8,384]{2,1,0:T(8,128)(2,1)S(1)} custom-call(f32[2,24,8,128]{3,2,1,0:T(8,128)S(1)} %get-tuple-element.12.beside, bf16[2,4,2,2816]{3,2,1,0:T(2,128)(2,1)S(1)} %collective-permute-done.1.far_side, s32[2,4,22,1,128]{4,3,2,1,0:T(1,128)S(1)} %get-tuple-element.13.begins, f32[704,128]{1,0:T(8,128)S(1)} %get-tuple-element.14.factors, ...), custom_call_target="tpu_custom_call" | custom-call | tf_op jit(solution)/shard_map/far_rows/pallas_call | solution.py:441
  13.1 14.8 %all_to_all.5.received = bf16[16,8,384]{2,1,0:T(8,128)(2,1)S(1)} all-to-all(bf16[16,8,384]{2,1,0:T(8,128)(2,1)S(1)} %far_rows.1), channel_id=1, replica_groups=mesh['lat'=16,'lev'=2] {'lat'}, dimensions={0} | all-to-all | bytes 196608 | tf_op jit(solution)/shard_map/all_to_all | solution.py:457
  28.0 0.1 fusion
  28.1 0.0 copy-done.1
  28.1 0.1 fusion.1
  28.2 0.1 collective-permute-start.2
  28.3 1.2 %collective-permute-done.2 = f32[16,384]{1,0:T(8,128)S(1)} collective-permute-done((f32[16,384]{1,0:T(8,128)S(1)}, f32[16,384]{1,0:T(8,128)S(1)}, u32[]{:S(2)}, u32[]{:S(2)}) %collective-permute-start.2) | collective-permute-done | bytes 24608 | tf_op jit(solution)/shard_map/ppermute | solution.py:463
  29.5 0.0 copy-start
  29.5 2.0 %copy-done = bf16[40,32,1281]{2,1,0:T(8,128)(2,1)S(1)} copy-done((bf16[40,32,1281]{2,1,0:T(8,128)(2,1)S(1)}, bf16[40,32,1281]{2,1,0:T(8,128)(2,1)}, u32[]{:S(2)}) %copy-start) | copy-done | bytes 3279384
  31.5 3.2 %degree_sums.1 = bf16[2,5,2,40,1281]{4,3,2,1,0:T(8,128)(2,1)} custom-call(f32[2]{0:T(128)S(1)} %copy-done.1, bf16[16,8,384]{2,1,0:T(8,128)(2,1)S(1)} %all_to_all.5.received, f32[1,16,384]{2,1,0:T(8,128)S(1)} %bitcast.5, bf16[40,32,1281]{2,1,0:T(8,128)(2,1)S(1)} %copy-done), custom_call_target="tpu_custom_call" | custom-call | tf_op jit(solution)/shard_map/degree_sums/pallas_call | solution.py:470
  (1 shorter events, 0.0 us)
Async XLA Ops:
  0.0 28.1 %copy-start.1 = (f32[2]{0:T(128)S(1)}, f32[2]{0:T(128)}, u32[]{:S(2)}) copy-start(f32[2]{0:T(128)} %thickness.1) | copy-start | bytes 28
  0.0 5.8 %collective-permute-start = (bf16[2,4,2,2816]{3,2,1,0:T(2,128)(2,1)}, bf16[2,4,2,2816]{3,2,1,0:T(2,128)(2,1)S(1)}, u32[]{:S(2)}, u32[]{:S(2)}) collective-permute-start(bf16[2,4,2,2816]{3,2,1,0:T(2,128)(2,1)} %fields_far.1), channel_id=1, source_target_pairs={{0,2},{4,6},{8,10},{12,14},{16,18},{20,22},{24,26},{28,30},{2,0},{... | collective-permute-start | bytes 270344 | tf_op jit(solution)/shard_map/ppermute | solution.py:406
  2.9 7.1 %collective-permute-start.1 = (bf16[2,4,2,2816]{3,2,1,0:T(2,128)(2,1)}, bf16[2,4,2,2816]{3,2,1,0:T(2,128)(2,1)S(1)}, u32[]{:S(2)}, u32[]{:S(2)}) collective-permute-start(bf16[2,4,2,2816]{3,2,1,0:T(2,128)(2,1)} %fields_far.1), channel_id=1, source_target_pairs={{2,4},{6,8},{10,12},{14,16},{18,20},{22,24},{26,28},{4,2},{8,6},{1... | collective-permute-start | bytes 270344 | tf_op jit(solution)/shard_map/ppermute | solution.py:406
  28.2 1.3 %collective-permute-start.2 = (f32[16,384]{1,0:T(8,128)S(1)}, f32[16,384]{1,0:T(8,128)S(1)}, u32[]{:S(2)}, u32[]{:S(2)}) collective-permute-start(f32[16,384]{1,0:T(8,128)S(1)} %fusion.1), channel_id=1, source_target_pairs={{0,1},{1,0},{2,3},{3,2},{4,5},{5,4},{6,7},{7,6},{8,9},{9,8},{10,11... | collective-permute-start | bytes 73736 | tf_op jit(solution)/shard_map/ppermute | solution.py:463
  29.5 2.0 %copy-start = (bf16[40,32,1281]{2,1,0:T(8,128)(2,1)S(1)}, bf16[40,32,1281]{2,1,0:T(8,128)(2,1)}, u32[]{:S(2)}) copy-start(bf16[40,32,1281]{2,1,0:T(8,128)(2,1)} %legendre.1) | copy-start | bytes 9838084

commit v10 on v9

--- a/solution.py
+++ b/solution.py
@@ -204,7 +204,7 @@
 
 def far_kernel(
     beside, far_side, begins, factors, facts, partial, table, twiddle,
-    out, lines, ext, grid, waves, packed,
+    out, lines, ext, grid, waves,
 ):
     lat_count, couples = partial.shape[:2]
     columns = table.shape[2] // 2
@@ -271,71 +271,38 @@
                 sine = sine - (real[here] * turn_sin + imag[here] * turn_cos)
             waves[latitude, 0:SUB, at : at + width] = cosine
             waves[latitude, SUB : 2 * SUB, at : at + width] = sine
-    used = columns // owners
-    for owner in range(owners):
-        for latitude in range(lat_count):
-            for part in range(2):
-                place = (2 * latitude + part) * used
-                packed[owner, :, place : place + used] = waves[
-                    latitude, part * SUB : (part + 1) * SUB, owner * used : (owner + 1) * used
-                ]
-        rest = packed.shape[2] - 2 * lat_count * used
-        if rest > 0:
-            packed[owner, :, packed.shape[2] - rest :] = jnp.zeros((SUB, rest), jnp.float32)
-        out[owner] = packed[owner].astype(jnp.bfloat16)
-
-
-def legendre_kernel(
-    level_owners, level_count, field_count, thickness, received, totals, legendre, out, wide, left, planes, sent,
-):
-    owners = received.shape[0]
-    pair_count, lat_total, degrees = legendre.shape
-    lat_count = lat_total // owners
-    used = 2 * pair_count
-    pair_total = pair_count * owners
-    groups = [(at, min(SUB, pair_count - at)) for at in range(0, pair_count, SUB)]
-    reach = pair_count + len(groups) * SUB
-    keys = [(field, part) for field in range(field_count + 1) for part in range(2)]
-    level_place = lax.axis_index("lev")
-    first_pair = lax.axis_index("lat") * pair_count
-    lane_blocks = wide.shape[0]
-    for block in range(lane_blocks):
-        values = received[:, :, block * LANES : (block + 1) * LANES].astype(jnp.float32)
-        wide[block] = values.reshape(wide.shape[1:])
-
-
-    def unpacked(values, part):
-        places = [(2 * latitude + part) * used for latitude in range(lat_count)]
-        return jnp.concatenate([values[:, place : place + reach] for place in places], axis=0)
-
-    lines = {}
-    for part in range(2):
-        running = jnp.zeros((lat_total, reach), jnp.float32)
-        for place in range(totals.shape[0]):
-            other = 1 - level_place if level_owners == 2 else place
-            running = running + jnp.where(other > level_place, unpacked(totals[place], part), 0.0)
-        for level in reversed(range(level_count)):
-            for field in range(field_count):
-                rows = pl.ds(level * field_count + field, owners, stride=SUB)
-                values = [wide[block, rows, :] for block in range(lane_blocks)]
-                lines[level, field, part] = unpacked(jnp.concatenate(values, axis=1), part)
-            running = running + thickness[level] * (
-                lines[level, 2, part] + 0.61 * lines[level, 3, part]
-            )
-            lines[level, field_count, part] = running
+        waves[latitude, :, columns:] = jnp.zeros((2 * SUB, waves.shape[2] - columns), jnp.float32)
+        used = columns // owners
+        for owner in range(owners):
+            out[owner, 2 * SUB * latitude : 2 * SUB * (latitude + 1), :] = waves[
+                latitude, :, owner * used : owner * used + LANES
+            ].astype(jnp.bfloat16)
+
+
+def row_keys(level_count, field_count):
+    return [
+        (level, field, part)
+        for level in range(level_count)
+        for field in range(field_count + 1)
+        for part in range(2)
+    ]
+
+
+def place_rows(lines, keys, pair_count, left):
+    lat_total = next(iter(lines.values())).shape[0]
     depth = SUB * lat_total
-    row = lax.broadcasted_iota(jnp.int32, (lat_total, depth), 0)
-    latitude = row % owners * lat_count + row // owners
+    half = len(keys) * SUB
     spread = (
-        latitude == lax.broadcasted_iota(jnp.int32, (lat_total, depth), 1) % lat_total
+        lax.broadcasted_iota(jnp.int32, (lat_total, depth), 0)
+        == lax.broadcasted_iota(jnp.int32, (lat_total, depth), 1) % lat_total
     ).astype(jnp.bfloat16)
     keep = (
         lax.broadcasted_iota(jnp.int32, (SUB, depth), 0)
         == lax.broadcasted_iota(jnp.int32, (SUB, depth), 1) // lat_total
     )
-    keys = [(level,) + key for level in range(level_count) for key in keys]
-    half = len(keys) * SUB
     for place in range(0, len(keys), 2):
+        if keys[place] not in lines:
+            continue
         couple = [
             lax.dot_general(
                 lines[key].astype(jnp.bfloat16),
@@ -346,13 +313,59 @@
             for key in keys[place : place + 2]
         ]
         for member in range(2):
-            for group, (at, _) in enumerate(groups):
-                begin = member * pair_count + at
+            for group in range(left.shape[0]):
+                begin = member * pair_count + group * SUB
                 pieces = [jnp.where(keep, one[begin : begin + SUB], 0.0) for one in couple]
                 into = member * half + place * SUB
                 left[group, into : into + 2 * SUB, :] = jnp.concatenate(pieces, axis=0).astype(
                     jnp.bfloat16
                 )
+
+
+def received_rows(received, wide, keys, field_count):
+    wide[...] = received[...].astype(jnp.float32).reshape(wide.shape)
+    lat_total = wide.shape[0] // (2 * SUB)
+    return {
+        (level, field, part): wide[
+            pl.ds(part * SUB + level * field_count + field, lat_total, stride=2 * SUB), :
+        ]
+        for level, field, part in keys
+    }
+
+
+def left_kernel(level_count, field_count, pair_count, received, left, wide):
+    keys = row_keys(level_count, field_count)
+    wanted = [key for key in keys if key[1] < field_count]
+    place_rows(received_rows(received, wide, wanted, field_count), keys, pair_count, left)
+
+
+def legendre_kernel(
+    level_owners, level_count, field_count, thickness, received, totals, legendre, left_given,
+    out, left, wide, planes, sent,
+):
+    owners = received.shape[0]
+    pair_count, lat_total, degrees = legendre.shape
+    pair_total = pair_count * owners
+    groups = [(at, min(SUB, pair_count - at)) for at in range(0, pair_count, SUB)]
+    keys = row_keys(level_count, field_count)
+    half = len(keys) * SUB
+    level_place = lax.axis_index("lev")
+    first_pair = lax.axis_index("lat") * pair_count
+    wanted = [(level, field, part) for level in range(level_count) for field in (2, 3) for part in range(2)]
+    lines = received_rows(received, wide, wanted, field_count)
+    sums = {}
+    for part in range(2):
+        running = jnp.zeros((lat_total, LANES), jnp.float32)
+        for place in range(totals.shape[0]):
+            other = 1 - level_place if level_owners == 2 else place
+            total = totals[place, pl.ds(part, lat_total, stride=2), :]
+            running = running + jnp.where(other > level_place, total, 0.0)
+        for level in reversed(range(level_count)):
+            running = running + thickness[level] * (
+                lines[level, 2, part] + 0.61 * lines[level, 3, part]
+            )
+            sums[level, field_count, part] = running
+    place_rows(sums, keys, pair_count, left)
     copies = []
     for start in range(0, degrees, 256):
         stop = min(start + 256, degrees)
@@ -399,7 +412,6 @@
     couples = lon_count // (2 * LANES)
     blocks = 2 * couples
     columns = 2 * owners * pair_count
-    packed_lanes = -(-2 * lat_count * 2 * pair_count // LANES) * LANES
     sides = []
     for first in range(2):
         edges = [(i, i + 1) for i in range(first, owners - 1, 2)]
@@ -440,24 +452,23 @@
 
     coefficients = pl.pallas_call(
         far_kernel,
-        out_shape=jax.ShapeDtypeStruct((owners, SUB, packed_lanes), jnp.bfloat16),
+        out_shape=jax.ShapeDtypeStruct((owners, 2 * SUB * lat_count, LANES), jnp.bfloat16),
         in_specs=[vector] * 8,
         out_specs=vector,
         scratch_shapes=[
             pltpu.VMEM((fields.size // LANES, LANES), jnp.float32),
             pltpu.VMEM((2 * lat_count, blocks + 2, SUB, LANES), jnp.float32),
             pltpu.VMEM((lat_count, couples, SUB, 2 * LANES), jnp.float32),
-            pltpu.VMEM((lat_count, 2 * SUB, columns), jnp.float32),
-            pltpu.VMEM((owners, SUB, packed_lanes), jnp.float32),
+            pltpu.VMEM((lat_count, 2 * SUB, columns + LANES), jnp.float32),
         ],
         compiler_params=params,
         name="far_rows",
     )(beside, sides[1], begins, factors, facts, partial, table, twiddle)
 
     received = lax.all_to_all(coefficients, "lat", split_axis=0, concat_axis=0, tiled=True)
-    by_level = received.reshape(owners, level_count, field_count, packed_lanes).astype(jnp.float32)
-    virtual = by_level[:, :, 2] + 0.61 * by_level[:, :, 3]
-    total = jnp.sum(thickness[None, :, None] * virtual, axis=1)
+    share = thickness[:, None] * jnp.asarray([0.0] * (field_count - 2) + [1.0, 0.61], jnp.float32)
+    by_row = received.reshape(2 * lat_total, SUB, LANES).astype(jnp.float32)
+    total = jnp.sum(by_row * share.reshape(1, SUB, 1), axis=1)
     level_owners = lax.axis_size("lev")
     if level_owners == 2:
         totals = lax.ppermute(total, "lev", [(0, 1), (1, 0)])[None]
@@ -467,20 +478,32 @@
     out_shape = (level_count, field_count + 1, 2, pair_count, degrees)
     half = level_count * (field_count + 1) * 2 * SUB
     group_count = (pair_count + SUB - 1) // SUB
+    left_shape = jax.ShapeDtypeStruct((group_count, 2 * half, SUB * lat_total), jnp.bfloat16)
+    wide = pltpu.VMEM((lat_total * 2 * SUB, LANES), jnp.float32)
+    left = pl.pallas_call(
+        functools.partial(left_kernel, level_count, field_count, pair_count),
+        out_shape=left_shape,
+        in_specs=[vector],
+        out_specs=vector,
+        scratch_shapes=[wide],
+        compiler_params=params,
+        cost_estimate=pl.CostEstimate(flops=50_000_000, bytes_accessed=2_000_000, transcendentals=0),
+        name="left_rows",
+    )(received)
     return pl.pallas_call(
         functools.partial(legendre_kernel, level_owners, level_count, field_count),
-        out_shape=jax.ShapeDtypeStruct(out_shape, jnp.bfloat16),
-        in_specs=[scalar, vector, vector, vector],
-        out_specs=pl.BlockSpec(memory_space=pl.ANY),
+        out_shape=(jax.ShapeDtypeStruct(out_shape, jnp.bfloat16), left_shape),
+        in_specs=[scalar, vector, vector, vector, vector],
+        out_specs=(pl.BlockSpec(memory_space=pl.ANY), vector),
+        input_output_aliases={4: 1},
         scratch_shapes=[
-            pltpu.VMEM((packed_lanes // LANES, owners * SUB, LANES), jnp.float32),
-            pltpu.VMEM((group_count, 2 * half, SUB * lat_total), jnp.bfloat16),
+            wide,
             pltpu.VMEM(out_shape, jnp.bfloat16),
             pltpu.SemaphoreType.DMA(((degrees + 255) // 256,)),
         ],
         compiler_params=params,
         name="degree_sums",
-    )(thickness, received, totals, legendre)
+    )(thickness, received, totals, legendre, left)[0]
 
 
 def solution(mesh):

time: 34.9 us -> 35.4 us (1.014)
  blocking collectives: 14.8 us -> 0 us
  starting transfers between devices: 3.66 us -> 11 us
  waiting for transfers between devices: 3.35 us -> 10.5 us
  Pallas kernels: 10.6 us -> 11.2 us
    all_to_all x1 -> x0, blocking collectives: 14.8 us -> none  [local(): lax.all_to_all(coefficients, 'lat', split_axis=0, concat_axis=0, tiled=True)]
    all_to_all x0 -> x1, waiting for transfers between devices: none -> 7.62 us  [local(): lax.all_to_all(coefficients, 'lat', split_axis=0, concat_axis=0, tiled=True)]
    all_to_all x0 -> x1, starting transfers between devices: none -> 7.3 us  [local(): lax.all_to_all(coefficients, 'lat', split_axis=0, concat_axis=0, tiled=True)]
    pallas_call x1 -> x2, Pallas kernels: 3.05 us -> 4.17 us  [the longest x1 3.69 us: local(): pl.pallas_call(far_kernel, out_shape=jax.ShapeDtypeStruct((owners, 2 * SU...]
    ppermute x1, waiting for transfers between devices: 1.18 us -> 0.71 us  [local(): totals = lax.ppermute(total, 'lev', [(0, 1), (1, 0)])[None]]
    pallas_call x1, Pallas kernels: 3.23 us -> 2.77 us  [local(): pl.pallas_call(functools.partial(legendre_kernel, level_owners, level_cou...]
    unnamed x4 -> x6, local copies, waits for them, and re-layouts: 2.02 us -> 2.03 us
  transfers between devices with their start and end apart: 3 -> 4, of which waited for: 2 -> 3; matrix products, arithmetic and copies ran while one was open for 0% -> 0% of each run, Pallas kernels for 12% -> 14%
where the time goes in v10:
time: 35.4 us; the launch traced here: 35.1 us
  Pallas kernels  11.2 us (32%)
  starting transfers between devices  11 us (31%)
  waiting for transfers between devices  10.5 us (30%)
  local copies, waits for them, and re-layouts  2.11 us (6%)
    all_to_all x1, waiting for transfers between devices, local(): lax.all_to_all(coefficients, 'lat', split_axis=0, concat_axis=0, tiled=True)  7.62 us
    all_to_all x1, starting transfers between devices, local(): lax.all_to_all(coefficients, 'lat', split_axis=0, concat_axis=0, tiled=True)  7.3 us
    pallas_call x1, Pallas kernels, local(): pl.pallas_call(functools.partial(near_kernel, pair_count * owners, pair_c...  4.31 us
    pallas_call x1, Pallas kernels, local(): pl.pallas_call(far_kernel, out_shape=jax.ShapeDtypeStruct((owners, 2 * SU...  3.69 us
    ppermute x2, starting transfers between devices, local(): lax.ppermute(fields, 'lat', edges + [(j, i) for i, j in edges])  3.59 us
    pallas_call x1, Pallas kernels, local(): pl.pallas_call(functools.partial(legendre_kernel, level_owners, level_cou...  2.77 us
    ppermute x2, waiting for transfers between devices, local(): lax.ppermute(fields, 'lat', edges + [(j, i) for i, j in edges])  2.17 us
    unnamed x6, local copies, waits for them, and re-layouts  2.03 us
  transfers between devices with their start and end apart: 4, of which 3 were waited for; matrix products, arithmetic and copies ran while one was open for 0% of the time, Pallas kernels for 14%

profile of v10, /device:TPU:0, one launch (start us, length us, event | category | flops | bytes accessed | tf_op | source)
XLA Modules:
  0.0 35.1 jit_solution(14589316520202120611)
XLA Ops:
  0.0 0.0 copy-start.2
  0.0 0.0 copy-start.1
  0.0 2.9 %collective-permute-start = (bf16[2,4,2,2816]{3,2,1,0:T(2,128)(2,1)}, bf16[2,4,2,2816]{3,2,1,0:T(2,128)(2,1)S(1)}, u32[]{:S(2)}, u32[]{:S(2)}) collective-permute-start(bf16[2,4,2,2816]{3,2,1,0:T(2,128)(2,1)} %fields_far.1), channel_id=1, source_target_pairs={{0,2},{4,6},{8,10},{12,14},{16,18},{20,22},{24,26},{28,30},{2,0},{... | collective-permute-start | bytes 270344 | tf_op jit(solution)/shard_map/ppermute | solution.py:418
  2.9 0.7 %collective-permute-start.1 = (bf16[2,4,2,2816]{3,2,1,0:T(2,128)(2,1)}, bf16[2,4,2,2816]{3,2,1,0:T(2,128)(2,1)S(1)}, u32[]{:S(2)}, u32[]{:S(2)}) collective-permute-start(bf16[2,4,2,2816]{3,2,1,0:T(2,128)(2,1)} %fields_far.1), channel_id=1, source_target_pairs={{2,4},{6,8},{10,12},{14,16},{18,20},{22,24},{26,28},{4,2},{8,6},{1... | collective-permute-start | bytes 270344 | tf_op jit(solution)/shard_map/ppermute | solution.py:418
  3.6 2.2 %collective-permute-done.side = bf16[2,4,2,2816]{3,2,1,0:T(2,128)(2,1)S(1)} collective-permute-done((bf16[2,4,2,2816]{3,2,1,0:T(2,128)(2,1)}, bf16[2,4,2,2816]{3,2,1,0:T(2,128)(2,1)S(1)}, u32[]{:S(2)}, u32[]{:S(2)}) %collective-permute-start) | collective-permute-done | bytes 90144 | tf_op jit(solution)/shard_map/ppermute | solution.py:418
  5.8 4.3 %near_rows.1 = (f32[2,11,8,256]{3,2,1,0:T(8,128)S(1)}, bf16[2,256,2560]{2,1,0:T(8,128)(2,1)S(1)}, f32[2,11,2560]{2,1,0:T(8,128)S(1)}, s32[2,4,22,1,128]{4,3,2,1,...) custom-call(s32[2]{0:T(128)} %rows_first_far.1, s32[32]{0:T(128)} %points_far.1, ...), custom_call_target="tpu_custom_call" | custom-call | flops 10000000 | bytes 4000000 | tf_op jit(solution)/shard_map/near_rows/pallas_call | solution.py:424
  10.1 0.0 collective-permute-done.1.far_side
  10.1 3.7 %far_rows.1 = bf16[16,32,128]{2,1,0:T(8,128)(2,1)} custom-call(f32[2,24,8,128]{3,2,1,0:T(8,128)S(1)} %get-tuple-element.13.beside, bf16[2,4,2,2816]{3,2,1,0:T(2,128)(2,1)S(1)} %collective-permute-done.1.far_side, s32[2,4,22,1,128]{4,3,2,1,0:T(1,128)S(1)} %get-tuple-element.14.begins, f32[704,128]{1,0:T(8,128)S(1)} %get-tuple-element.15.factors, ...), custom_call_target="tpu_custom_call" | custom-call | tf_op jit(solution)/shard_map/far_rows/pallas_call | solution.py:453
  13.8 7.3 %all-to-all-start = ((bf16[16,32,128]{2,1,0:T(8,128)(2,1)}), bf16[16,32,128]{2,1,0:T(8,128)(2,1)S(1)}, u32[]{:S(2)}, u32[]{:S(2)}) async-start(bf16[16,32,128]{2,1,0:T(8,128)(2,1)} %far_rows.1), calls=%async_computation | async-start | bytes 262144 | tf_op jit(solution)/shard_map/all_to_all | solution.py:468
  21.1 0.0 copy-done.2
  21.1 0.0 copy-done.1
  21.1 0.1 broadcast_multiply_fusion
  21.2 0.1 mul.31
  21.3 7.6 %all-to-all-done.received = bf16[16,32,128]{2,1,0:T(8,128)(2,1)S(1)} async-done(((bf16[16,32,128]{2,1,0:T(8,128)(2,1)}), bf16[16,32,128]{2,1,0:T(8,128)(2,1)S(1)}, u32[]{:S(2)}, u32[]{:S(2)}) %all-to-all-start) | async-done | bytes 131104 | tf_op jit(solution)/shard_map/all_to_all | solution.py:468
  28.9 0.1 fusion
  29.0 0.1 collective-permute-start.2
  29.1 0.5 %left_rows.1.left_given = bf16[5,320,256]{2,1,0:T(8,128)(2,1)S(1)} custom-call(bf16[16,32,128]{2,1,0:T(8,128)(2,1)S(1)} %all-to-all-done.received), custom_call_target="tpu_custom_call" | custom-call | flops 50000000 | bytes 2000000 | tf_op jit(solution)/shard_map/left_rows/pallas_call | solution.py:483
  29.6 0.7 %collective-permute-done.2 = f32[64,128]{1,0:T(8,128)S(1)} collective-permute-done((f32[64,128]{1,0:T(8,128)S(1)}, f32[64,128]{1,0:T(8,128)S(1)}, u32[]{:S(2)}, u32[]{:S(2)}) %collective-permute-start.2) | collective-permute-done | bytes 32800 | tf_op jit(solution)/shard_map/ppermute | solution.py:474
  30.3 0.0 copy-start
  30.3 2.0 %copy-done = bf16[40,32,1281]{2,1,0:T(8,128)(2,1)S(1)} copy-done((bf16[40,32,1281]{2,1,0:T(8,128)(2,1)S(1)}, bf16[40,32,1281]{2,1,0:T(8,128)(2,1)}, u32[]{:S(2)}) %copy-start) | copy-done | bytes 3279384
  32.3 2.8 %degree_sums.1 = (bf16[2,5,2,40,1281]{4,3,2,1,0:T(8,128)(2,1)}, bf16[5,320,256]{2,1,0:T(8,128)(2,1)S(1)}) custom-call(f32[2]{0:T(128)S(1)} %copy-done.1, bf16[16,32,128]{2,1,0:T(8,128)(2,1)S(1)} %all-to-all-done.received, f32[1,64,128]{2,1,0:T(8,128)S(1)} %bitcast.4, bf16[40,32,1281]{2,1,0:T(8,128)(2,1)S(1)} %copy-done, ...), custom_call_target="tpu_custom_call", output_to_operand_aliasing={{1}: (4, {})} | custom-call | tf_op jit(solution)/shard_map/degree_sums/pallas_call | solution.py:493
Async XLA Ops:
  0.0 21.1 %copy-start.2 = (f32[4]{0:T(128)S(1)}, f32[4]{0:T(128)}, u32[]{:S(2)}) copy-start(f32[4]{0:T(128)} %constant.4.clone) | copy-start | bytes 52
  0.0 21.1 %copy-start.1 = (f32[2]{0:T(128)S(1)}, f32[2]{0:T(128)}, u32[]{:S(2)}) copy-start(f32[2]{0:T(128)} %thickness.1) | copy-start | bytes 28
  0.0 5.8 %collective-permute-start = (bf16[2,4,2,2816]{3,2,1,0:T(2,128)(2,1)}, bf16[2,4,2,2816]{3,2,1,0:T(2,128)(2,1)S(1)}, u32[]{:S(2)}, u32[]{:S(2)}) collective-permute-start(bf16[2,4,2,2816]{3,2,1,0:T(2,128)(2,1)} %fields_far.1), channel_id=1, source_target_pairs={{0,2},{4,6},{8,10},{12,14},{16,18},{20,22},{24,26},{28,30},{2,0},{... | collective-permute-start | bytes 270344 | tf_op jit(solution)/shard_map/ppermute | solution.py:418
  2.9 7.1 %collective-permute-start.1 = (bf16[2,4,2,2816]{3,2,1,0:T(2,128)(2,1)}, bf16[2,4,2,2816]{3,2,1,0:T(2,128)(2,1)S(1)}, u32[]{:S(2)}, u32[]{:S(2)}) collective-permute-start(bf16[2,4,2,2816]{3,2,1,0:T(2,128)(2,1)} %fields_far.1), channel_id=1, source_target_pairs={{2,4},{6,8},{10,12},{14,16},{18,20},{22,24},{26,28},{4,2},{8,6},{1... | collective-permute-start | bytes 270344 | tf_op jit(solution)/shard_map/ppermute | solution.py:418
  13.8 15.1 %all-to-all-start = ((bf16[16,32,128]{2,1,0:T(8,128)(2,1)}), bf16[16,32,128]{2,1,0:T(8,128)(2,1)S(1)}, u32[]{:S(2)}, u32[]{:S(2)}) async-start(bf16[16,32,128]{2,1,0:T(8,128)(2,1)} %far_rows.1), calls=%async_computation | async-start | bytes 262144 | tf_op jit(solution)/shard_map/all_to_all | solution.py:468
  29.0 1.3 %collective-permute-start.2 = (f32[64,128]{1,0:T(8,128)S(1)}, f32[64,128]{1,0:T(8,128)S(1)}, u32[]{:S(2)}, u32[]{:S(2)}) collective-permute-start(f32[64,128]{1,0:T(8,128)S(1)} %fusion), channel_id=1, source_target_pairs={{0,1},{1,0},{2,3},{3,2},{4,5},{5,4},{6,7},{7,6},{8,9},{9,8},{10,11... | collective-permute-start | bytes 98312 | tf_op jit(solution)/shard_map/ppermute | solution.py:474
  30.3 2.0 %copy-start = (bf16[40,32,1281]{2,1,0:T(8,128)(2,1)S(1)}, bf16[40,32,1281]{2,1,0:T(8,128)(2,1)}, u32[]{:S(2)}) copy-start(bf16[40,32,1281]{2,1,0:T(8,128)(2,1)} %legendre.1) | copy-start | bytes 9838084

commit v11 on v10

--- a/solution.py
+++ b/solution.py
@@ -358,8 +358,7 @@
         running = jnp.zeros((lat_total, LANES), jnp.float32)
         for place in range(totals.shape[0]):
             other = 1 - level_place if level_owners == 2 else place
-            total = totals[place, pl.ds(part, lat_total, stride=2), :]
-            running = running + jnp.where(other > level_place, total, 0.0)
+            running = running + jnp.where(other > level_place, totals[place, part], 0.0)
         for level in reversed(range(level_count)):
             running = running + thickness[level] * (
                 lines[level, 2, part] + 0.61 * lines[level, 3, part]
@@ -466,9 +465,9 @@
     )(beside, sides[1], begins, factors, facts, partial, table, twiddle)
 
     received = lax.all_to_all(coefficients, "lat", split_axis=0, concat_axis=0, tiled=True)
-    share = thickness[:, None] * jnp.asarray([0.0] * (field_count - 2) + [1.0, 0.61], jnp.float32)
-    by_row = received.reshape(2 * lat_total, SUB, LANES).astype(jnp.float32)
-    total = jnp.sum(by_row * share.reshape(1, SUB, 1), axis=1)
+    by_level = received.reshape(lat_total, 2, level_count, field_count, LANES).astype(jnp.float32)
+    virtual = by_level[:, :, :, 2] + 0.61 * by_level[:, :, :, 3]
+    total = jnp.sum(thickness[None, None, :, None] * virtual, axis=2).transpose(1, 0, 2)
     level_owners = lax.axis_size("lev")
     if level_owners == 2:
         totals = lax.ppermute(total, "lev", [(0, 1), (1, 0)])[None]

time: 35.4 us -> 32.6 us (0.921)
  blocking collectives: 0 us -> 14.9 us
  waiting for transfers between devices: 10.5 us -> 2.87 us
  starting transfers between devices: 11 us -> 3.66 us
  local copies, waits for them, and re-layouts: 2.11 us -> 0.13 us
  Pallas kernels: 11.2 us -> 10.6 us
    all_to_all x0 -> x1, blocking collectives: none -> 14.9 us  [local(): lax.all_to_all(coefficients, 'lat', split_axis=0, concat_axis=0, tiled=True)]
    all_to_all x1 -> x0, waiting for transfers between devices: 7.62 us -> none  [local(): lax.all_to_all(coefficients, 'lat', split_axis=0, concat_axis=0, tiled=True)]
    all_to_all x1 -> x0, starting transfers between devices: 7.3 us -> none  [local(): lax.all_to_all(coefficients, 'lat', split_axis=0, concat_axis=0, tiled=True)]
    unnamed x6 -> x4, local copies, waits for them, and re-layouts: 2.03 us -> 0.01 us
    pallas_call x1, Pallas kernels: 3.69 us -> 3.02 us  [local(): pl.pallas_call(far_kernel, out_shape=jax.ShapeDtypeStruct((owners, 2 * SU...]
  transfers between devices with their start and end apart: 4 -> 3, of which waited for: 3 -> 2; matrix products, arithmetic and copies ran while one was open for 0% -> 0% of each run, Pallas kernels for 14% -> 15%
where the time goes in v11:
time: 32.6 us; the launch traced here: 32.4 us
  blocking collectives  14.9 us (46%)
  Pallas kernels  10.6 us (33%)
  starting transfers between devices  3.66 us (11%)
  waiting for transfers between devices  2.87 us (9%)
    all_to_all x1, blocking collectives, local(): lax.all_to_all(coefficients, 'lat', split_axis=0, concat_axis=0, tiled=True)  14.9 us
    pallas_call x1, Pallas kernels, local(): pl.pallas_call(functools.partial(near_kernel, pair_count * owners, pair_c...  4.31 us
    ppermute x2, starting transfers between devices, local(): lax.ppermute(fields, 'lat', edges + [(j, i) for i, j in edges])  3.59 us
    pallas_call x1, Pallas kernels, local(): pl.pallas_call(far_kernel, out_shape=jax.ShapeDtypeStruct((owners, 2 * SU...  3.02 us
    pallas_call x1, Pallas kernels, local(): pl.pallas_call(functools.partial(legendre_kernel, level_owners, level_cou...  2.76 us
    ppermute x2, waiting for transfers between devices, local(): lax.ppermute(fields, 'lat', edges + [(j, i) for i, j in edges])  2.17 us
    ppermute x1, waiting for transfers between devices, local(): totals = lax.ppermute(total, 'lev', [(0, 1), (1, 0)])[None]  0.7 us
  transfers between devices with their start and end apart: 3, of which 2 were waited for; matrix products, arithmetic and copies ran while one was open for 0% of the time, Pallas kernels for 15%

profile of v11, /device:TPU:0, one launch (start us, length us, event | category | flops | bytes accessed | tf_op | source)
XLA Modules:
  0.0 32.4 jit_solution(7536669855153946808)
XLA Ops:
  0.0 0.0 copy-start.1
  0.0 2.9 %collective-permute-start = (bf16[2,4,2,2816]{3,2,1,0:T(2,128)(2,1)}, bf16[2,4,2,2816]{3,2,1,0:T(2,128)(2,1)S(1)}, u32[]{:S(2)}, u32[]{:S(2)}) collective-permute-start(bf16[2,4,2,2816]{3,2,1,0:T(2,128)(2,1)} %fields_far.1), channel_id=1, source_target_pairs={{0,2},{4,6},{8,10},{12,14},{16,18},{20,22},{24,26},{28,30},{2,0},{... | collective-permute-start | bytes 270344 | tf_op jit(solution)/shard_map/ppermute | solution.py:417
  2.9 0.7 %collective-permute-start.1 = (bf16[2,4,2,2816]{3,2,1,0:T(2,128)(2,1)}, bf16[2,4,2,2816]{3,2,1,0:T(2,128)(2,1)S(1)}, u32[]{:S(2)}, u32[]{:S(2)}) collective-permute-start(bf16[2,4,2,2816]{3,2,1,0:T(2,128)(2,1)} %fields_far.1), channel_id=1, source_target_pairs={{2,4},{6,8},{10,12},{14,16},{18,20},{22,24},{26,28},{4,2},{8,6},{1... | collective-permute-start | bytes 270344 | tf_op jit(solution)/shard_map/ppermute | solution.py:417
  3.6 2.2 %collective-permute-done.side = bf16[2,4,2,2816]{3,2,1,0:T(2,128)(2,1)S(1)} collective-permute-done((bf16[2,4,2,2816]{3,2,1,0:T(2,128)(2,1)}, bf16[2,4,2,2816]{3,2,1,0:T(2,128)(2,1)S(1)}, u32[]{:S(2)}, u32[]{:S(2)}) %collective-permute-start) | collective-permute-done | bytes 90144 | tf_op jit(solution)/shard_map/ppermute | solution.py:417
  5.8 4.3 %near_rows.1 = (f32[2,11,8,256]{3,2,1,0:T(8,128)S(1)}, bf16[2,256,2560]{2,1,0:T(8,128)(2,1)S(1)}, f32[2,11,2560]{2,1,0:T(8,128)S(1)}, s32[2,4,22,1,128]{4,3,2,1,...) custom-call(s32[2]{0:T(128)} %rows_first_far.1, s32[32]{0:T(128)} %points_far.1, ...), custom_call_target="tpu_custom_call" | custom-call | flops 10000000 | bytes 4000000 | tf_op jit(solution)/shard_map/near_rows/pallas_call | solution.py:423
  10.1 0.0 collective-permute-done.1.far_side
  10.1 0.0 copy-start
  10.1 3.0 %far_rows.1 = bf16[16,32,128]{2,1,0:T(8,128)(2,1)S(1)} custom-call(f32[2,24,8,128]{3,2,1,0:T(8,128)S(1)} %get-tuple-element.13.beside, bf16[2,4,2,2816]{3,2,1,0:T(2,128)(2,1)S(1)} %collective-permute-done.1.far_side, s32[2,4,22,1,128]{4,3,2,1,0:T(1,128)S(1)} %get-tuple-element.14.begins, f32[704,128]{1,0:T(8,128)S(1)} %get-tuple-element.15.factors, ...), custom_call_target="tpu_custom_call" | custom-call | tf_op jit(solution)/shard_map/far_rows/pallas_call | solution.py:452
  13.1 14.9 %all_to_all.5.received = bf16[16,32,128]{2,1,0:T(8,128)(2,1)S(1)} all-to-all(bf16[16,32,128]{2,1,0:T(8,128)(2,1)S(1)} %far_rows.1), channel_id=1, replica_groups=mesh['lat'=16,'lev'=2] {'lat'}, dimensions={0} | all-to-all | bytes 262144 | tf_op jit(solution)/shard_map/all_to_all | solution.py:467
  28.0 0.1 fusion.1
  28.1 0.0 copy-done.1
  28.2 0.2 fusion
  28.3 0.1 collective-permute-start.2
  28.4 0.5 %left_rows.1.left_given = bf16[5,320,256]{2,1,0:T(8,128)(2,1)S(1)} custom-call(bf16[16,32,128]{2,1,0:T(8,128)(2,1)S(1)} %all_to_all.5.received), custom_call_target="tpu_custom_call" | custom-call | flops 50000000 | bytes 2000000 | tf_op jit(solution)/shard_map/left_rows/pallas_call | solution.py:482
  28.9 0.7 %collective-permute-done.2 = f32[2,32,128]{2,1,0:T(8,128)S(1)} collective-permute-done((f32[2,32,128]{2,1,0:T(8,128)S(1)}, f32[2,32,128]{2,1,0:T(8,128)S(1)}, u32[]{:S(2)}, u32[]{:S(2)}) %collective-permute-start.2) | collective-permute-done | bytes 32800 | tf_op jit(solution)/shard_map/ppermute | solution.py:473
  29.6 0.0 copy-done
  29.6 2.8 %degree_sums.1 = (bf16[2,5,2,40,1281]{4,3,2,1,0:T(8,128)(2,1)}, bf16[5,320,256]{2,1,0:T(8,128)(2,1)S(1)}) custom-call(f32[2]{0:T(128)S(1)} %copy-done.1, bf16[16,32,128]{2,1,0:T(8,128)(2,1)S(1)} %all_to_all.5.received, f32[1,2,32,128]{3,2,1,0:T(8,128)S(1)} %bitcast.13, bf16[40,32,1281]{2,1,0:T(8,128)(2,1)S(1)} %copy-done, ...), custom_call_target="tpu_custom_call", output_to_operand_aliasing={{1}: (4, {})} | custom-call | tf_op jit(solution)/shard_map/degree_sums/pallas_call | solution.py:492
  (1 shorter events, 0.0 us)
Async XLA Ops:
  0.0 28.1 %copy-start.1 = (f32[2]{0:T(128)S(1)}, f32[2]{0:T(128)}, u32[]{:S(2)}) copy-start(f32[2]{0:T(128)} %thickness.1) | copy-start | bytes 28
  0.0 5.8 %collective-permute-start = (bf16[2,4,2,2816]{3,2,1,0:T(2,128)(2,1)}, bf16[2,4,2,2816]{3,2,1,0:T(2,128)(2,1)S(1)}, u32[]{:S(2)}, u32[]{:S(2)}) collective-permute-start(bf16[2,4,2,2816]{3,2,1,0:T(2,128)(2,1)} %fields_far.1), channel_id=1, source_target_pairs={{0,2},{4,6},{8,10},{12,14},{16,18},{20,22},{24,26},{28,30},{2,0},{... | collective-permute-start | bytes 270344 | tf_op jit(solution)/shard_map/ppermute | solution.py:417
  2.9 7.1 %collective-permute-start.1 = (bf16[2,4,2,2816]{3,2,1,0:T(2,128)(2,1)}, bf16[2,4,2,2816]{3,2,1,0:T(2,128)(2,1)S(1)}, u32[]{:S(2)}, u32[]{:S(2)}) collective-permute-start(bf16[2,4,2,2816]{3,2,1,0:T(2,128)(2,1)} %fields_far.1), channel_id=1, source_target_pairs={{2,4},{6,8},{10,12},{14,16},{18,20},{22,24},{26,28},{4,2},{8,6},{1... | collective-permute-start | bytes 270344 | tf_op jit(solution)/shard_map/ppermute | solution.py:417
  10.1 19.5 %copy-start = (bf16[40,32,1281]{2,1,0:T(8,128)(2,1)S(1)}, bf16[40,32,1281]{2,1,0:T(8,128)(2,1)}, u32[]{:S(2)}) copy-start(bf16[40,32,1281]{2,1,0:T(8,128)(2,1)} %legendre.1) | copy-start | bytes 9838084
  28.3 1.3 %collective-permute-start.2 = (f32[2,32,128]{2,1,0:T(8,128)S(1)}, f32[2,32,128]{2,1,0:T(8,128)S(1)}, u32[]{:S(2)}, u32[]{:S(2)}) collective-permute-start(f32[2,32,128]{2,1,0:T(8,128)S(1)} %bitcast.16), channel_id=1, source_target_pairs={{0,1},{1,0},{2,3},{3,2},{4,5},{5,4},{6,7},{7,6},{8,9},{9,8},{10,11... | collective-permute-start | bytes 98312 | tf_op jit(solution)/shard_map/ppermute | solution.py:473

commit v12 on v11

--- a/solution.py
+++ b/solution.py
@@ -99,23 +99,21 @@
                 at += rows
 
 
-def gathered(totals, starts, scale, parts):
+def gathered(totals, starts, scales, parts):
     for side in range(2):
-        start = jnp.broadcast_to(starts[side], (SUB, LANES))
         for column in range(4):
-            place = start + column
+            place = starts[side] + column
             lane = place & (LANES - 1)
             low, middle, high = [lane_gather(part, lane) for part in parts[side : side + 3]]
             value = jnp.where(place < LANES, low, jnp.where(place < 2 * LANES, middle, high))
-            line = STENCIL * side + column
-            totals[side] = totals[side] + scale[line : line + 1] * value
+            totals[side] = totals[side] + scales[STENCIL * side + column] * value
     return totals
 
 
 def near_kernel(
-    pair_total, pair_count, rows_first_far, points_far, fields_far, starts_far, weights_far, side,
-    partial, table, twiddle, begins, factors, facts, beside,
-    rows_first, points, fields, starts, weights, lines, side_lines, ext, arrived,
+    pair_total, pair_count, rows_first_far, points_far, fields_far, starts_far, weights_far,
+    partial, table, twiddle, far_starts, far_scales, facts,
+    rows_first, points, fields, starts, weights, begins, factors, lines, ext, arrived,
 ):
     lat_count, couples = partial.shape[:2]
     lon = 2 * couples * LANES
@@ -135,20 +133,7 @@
     ]
     for fetch in fetches:
         fetch.start()
-    spread_lines(side, side_lines)
-    for fetch in fetches[:2]:
-        fetch.wait()
-    known = [first_lat - rows_first[latitude] for latitude in range(lat_count)]
-    known += [points[first_lat + latitude] for latitude in range(lat_count)]
-    for place in range(-lat_count, 2 * lat_count):
-        if place < 0 or place >= lat_count:
-            place = jnp.clip(first_lat + place, 0, points.shape[0] - 1)
-            known.append(lon - points[place])
-    facts[...] = jnp.concatenate([jnp.full((1, LANES), one, jnp.int32) for one in known], axis=0)
-    upper = lax.axis_index("lat") % 2 == 0
-    for row in range(lat_count):
-        missing = jnp.where(upper, known[3 * lat_count + row], known[2 * lat_count + row])
-        extend(side_lines, row, lat_count, missing, beside, row)
+    fetches[0].wait()
     width = 256
     scales = []
     for latitude in range(lat_count):
@@ -167,8 +152,11 @@
             large = turn_parts(numbers * many, total, inverse)
             here = slice(at, at + width)
             there = slice(columns + at, columns + at + width)
-            twiddle[latitude, :, here] = scaling * large[0][:couples]
-            twiddle[latitude, :, there] = scaling * large[1][:couples]
+            for couple in range(couples):
+                for lanes, part in ((here, large[0]), (there, large[1])):
+                    twiddle[latitude, couple, :, lanes] = jnp.broadcast_to(
+                        scaling * part[couple : couple + 1], (SUB, width)
+                    )
             products = [ones] + [multiplied(row_of(eights, row), ones) for row in range(1, SUB)]
             block = tuple(jnp.concatenate(parts, axis=0) for parts in zip(*products))
             for quarter in range(4):
@@ -178,8 +166,15 @@
                 rows = slice(HALF * quarter, HALF * (quarter + 1))
                 table[latitude, rows, here] = turned[0].astype(jnp.bfloat16)
                 table[latitude, rows, there] = turned[1].astype(jnp.bfloat16)
-    for fetch in fetches[2:]:
+    for fetch in fetches[1:]:
         fetch.wait()
+    known = [first_lat - rows_first[latitude] for latitude in range(lat_count)]
+    known += [points[first_lat + latitude] for latitude in range(lat_count)]
+    for place in range(-lat_count, 2 * lat_count):
+        if place < 0 or place >= lat_count:
+            place = jnp.clip(first_lat + place, 0, points.shape[0] - 1)
+            known.append(lon - points[place])
+    facts[...] = jnp.concatenate([jnp.full((1, LANES), one, jnp.int32) for one in known], axis=0)
     spread_rows(starts, begins)
     spread_lines(weights, factors)
     spread_lines(fields, lines)
@@ -188,65 +183,68 @@
     for latitude in range(lat_count):
         mine = first_lat - rows_first[latitude]
         for couple in range(couples):
+
+            def spread_row(row):
+                at = ((latitude * STENCIL + row) * couples + couple) * SUB
+                tile = factors[pl.ds(pl.multiple_of(at, SUB), SUB), :]
+                return (
+                    [
+                        jnp.broadcast_to(begins[latitude, row, 2 * couple + side], (SUB, LANES))
+                        for side in range(2)
+                    ],
+                    [jnp.broadcast_to(tile[line : line + 1], (SUB, LANES)) for line in range(SUB)],
+                )
+
             totals = [jnp.zeros((SUB, LANES), jnp.float32) for _ in range(2)]
             for slot in range(lat_count):
-                row = mine + slot
-                at = ((latitude * STENCIL + row) * couples + couple) * SUB
-                totals = gathered(
-                    totals,
-                    [begins[latitude, row, 2 * couple + side] for side in range(2)],
-                    factors[pl.ds(pl.multiple_of(at, SUB), SUB), :],
-                    [ext[slot, 2 * couple + piece] for piece in range(4)],
-                )
+                begun, scales = spread_row(mine + slot)
+                parts = [ext[slot, 2 * couple + piece] for piece in range(4)]
+                totals = gathered(totals, begun, scales, parts)
             for side in range(2):
                 partial[latitude, couple, :, side * LANES : (side + 1) * LANES] = totals[side]
+            others = (jnp.where(mine >= 1, 0, 2), jnp.where(mine <= 1, 3, 1))
+            for choice, row in enumerate(others):
+                begun, scales = spread_row(row)
+                for side in range(2):
+                    far_starts[latitude, choice, couple, side] = begun[side]
+                for line in range(SUB):
+                    far_scales[latitude, choice, couple, line] = scales[line]
 
 
 def far_kernel(
-    beside, far_side, begins, factors, facts, partial, table, twiddle,
+    near_side, far_side, far_starts, far_scales, facts, partial, table, twiddle,
     out, lines, ext, grid, waves,
 ):
     lat_count, couples = partial.shape[:2]
     columns = table.shape[2] // 2
     owners = out.shape[0]
+    toward = 1 - lax.axis_index("lat") % 2
+    spread_lines(near_side, lines.at[toward])
+    spread_lines(far_side, lines.at[1 - toward])
     fact = [jnp.broadcast_to(facts[row : row + 1], (SUB, LANES)) for row in range(4 * lat_count)]
-    toward = 1 - lax.axis_index("lat") % 2
-    ext[pl.ds(toward * lat_count, lat_count)] = beside[...]
-    spread_lines(far_side, lines)
-    for row in range(lat_count):
-        missing = jnp.where(toward == 1, fact[2 * lat_count + row], fact[3 * lat_count + row])
-        extend(lines, row, lat_count, missing, ext, (1 - toward) * lat_count + row)
+    for slot in range(2 * lat_count):
+        side, row = divmod(slot, lat_count)
+        extend(lines.at[side], row, lat_count, fact[2 * lat_count + slot], ext, slot)
     lane = lax.broadcasted_iota(jnp.int32, (SUB, LANES), 1)
     width = 256
-    choices = (((2, 0, 0), (2, 1, 0)), ((3, 3, 1), (3, 2, 1)))
+    choices = ((2, 1, 0), (3, 2, 1))
     for latitude in range(lat_count):
         at_zero = fact[latitude] == 0
         at_one = fact[latitude] == 1
-
-        def pick(values):
-            return jnp.where(at_zero, values[0], jnp.where(at_one, values[1], values[2]))
-
-        def pick_line(values):
-            return jnp.where(
-                at_zero[:1], values[0], jnp.where(at_one[:1], values[1], values[2])
-            )
-
         for couple in range(couples):
             sides = [pl.ds(side * LANES, LANES) for side in range(2)]
             totals = [partial[latitude, couple, :, lanes] for lanes in sides]
-            for rows, slots in choices:
-                scales = [
-                    factors[pl.ds(((latitude * STENCIL + row) * couples + couple) * SUB, SUB), :]
-                    for row in rows
-                ]
-                starts = [
-                    pick_line([begins[latitude, row, 2 * couple + side] for row in rows])
-                    for side in range(2)
-                ]
-                parts = [
-                    pick([ext[slot, 2 * couple + piece] for slot in slots]) for piece in range(4)
-                ]
-                totals = gathered(totals, starts, pick(scales), parts)
+            for choice, slots in enumerate(choices):
+                parts = []
+                for piece in range(4):
+                    zero, one, two = [ext[slot, 2 * couple + piece] for slot in slots]
+                    parts.append(jnp.where(at_zero, zero, jnp.where(at_one, one, two)))
+                totals = gathered(
+                    totals,
+                    [far_starts[latitude, choice, couple, side] for side in range(2)],
+                    [far_scales[latitude, choice, couple, line] for line in range(SUB)],
+                    parts,
+                )
             for side in range(2):
                 live = lane + (2 * couple + side) * LANES < fact[lat_count + latitude]
                 grid[latitude, couple, :, sides[side]] = jnp.where(live, totals[side], 0.0)
@@ -264,8 +262,8 @@
             cosine = jnp.zeros((SUB, width), jnp.float32)
             sine = jnp.zeros((SUB, width), jnp.float32)
             for couple in range(couples):
-                turn_cos = twiddle[latitude, couple : couple + 1, at : at + width]
-                turn_sin = twiddle[latitude, couple : couple + 1, columns + at : columns + at + width]
+                turn_cos = twiddle[latitude, couple, :, at : at + width]
+                turn_sin = twiddle[latitude, couple, :, columns + at : columns + at + width]
                 here = slice(couple * SUB, (couple + 1) * SUB)
                 cosine = cosine + (real[here] * turn_cos - imag[here] * turn_sin)
                 sine = sine - (real[here] * turn_sin + imag[here] * turn_cos)
@@ -420,26 +418,26 @@
     vector = pl.BlockSpec(memory_space=pltpu.VMEM)
     params = pltpu.CompilerParams(vmem_limit_bytes=LIMIT)
     remote = pl.BlockSpec(memory_space=pltpu.HBM)
-    partial, table, twiddle, begins, factors, facts, beside = pl.pallas_call(
+    partial, table, twiddle, far_starts, far_scales, facts = pl.pallas_call(
         functools.partial(near_kernel, pair_count * owners, pair_count),
         out_shape=(
             jax.ShapeDtypeStruct((lat_count, couples, SUB, 2 * LANES), jnp.float32),
             jax.ShapeDtypeStruct((lat_count, 2 * LANES, 2 * columns), jnp.bfloat16),
-            jax.ShapeDtypeStruct((lat_count, couples, 2 * columns), jnp.float32),
-            jax.ShapeDtypeStruct((lat_count, STENCIL, blocks, 1, LANES), jnp.int32),
-            jax.ShapeDtypeStruct((weights.size // LANES, LANES), jnp.float32),
+            jax.ShapeDtypeStruct((lat_count, couples, SUB, 2 * columns), jnp.float32),
+            jax.ShapeDtypeStruct((lat_count, 2, couples, 2, SUB, LANES), jnp.int32),
+            jax.ShapeDtypeStruct((lat_count, 2, couples, SUB, SUB, LANES), jnp.float32),
             jax.ShapeDtypeStruct((4 * lat_count, LANES), jnp.int32),
-            jax.ShapeDtypeStruct((lat_count, blocks + 2, SUB, LANES), jnp.float32),
         ),
-        in_specs=[remote] * 5 + [vector],
-        out_specs=(vector,) * 7,
+        in_specs=[remote] * 5,
+        out_specs=(vector,) * 6,
         scratch_shapes=[
             pltpu.SMEM(rows_first.shape, jnp.int32),
             pltpu.SMEM(points.shape, jnp.int32),
             pltpu.VMEM(fields.shape, fields.dtype),
             pltpu.VMEM(starts.shape, starts.dtype),
             pltpu.VMEM(weights.shape, weights.dtype),
-            pltpu.VMEM((fields.size // LANES, LANES), jnp.float32),
+            pltpu.VMEM((lat_count, STENCIL, blocks, 1, LANES), jnp.int32),
+            pltpu.VMEM((weights.size // LANES, LANES), jnp.float32),
             pltpu.VMEM((fields.size // LANES, LANES), jnp.float32),
             pltpu.VMEM((lat_count, blocks + 2, SUB, LANES), jnp.float32),
             pltpu.SemaphoreType.DMA((5,)),
@@ -447,7 +445,7 @@
         compiler_params=params,
         cost_estimate=pl.CostEstimate(flops=10_000_000, bytes_accessed=4_000_000, transcendentals=0),
         name="near_rows",
-    )(*(held(value) for value in (rows_first, points, fields, starts, weights)), sides[0])
+    )(*(held(value) for value in (rows_first, points, fields, starts, weights)))
 
     coefficients = pl.pallas_call(
         far_kernel,
@@ -455,14 +453,14 @@
         in_specs=[vector] * 8,
         out_specs=vector,
         scratch_shapes=[
-            pltpu.VMEM((fields.size // LANES, LANES), jnp.float32),
+            pltpu.VMEM((2, fields.size // LANES, LANES), jnp.float32),
             pltpu.VMEM((2 * lat_count, blocks + 2, SUB, LANES), jnp.float32),
             pltpu.VMEM((lat_count, couples, SUB, 2 * LANES), jnp.float32),
             pltpu.VMEM((lat_count, 2 * SUB, columns + LANES), jnp.float32),
         ],
         compiler_params=params,
         name="far_rows",
-    )(beside, sides[1], begins, factors, facts, partial, table, twiddle)
+    )(*sides, far_starts, far_scales, facts, partial, table, twiddle)
 
     received = lax.all_to_all(coefficients, "lat", split_axis=0, concat_axis=0, tiled=True)
     by_level = received.reshape(lat_total, 2, level_count, field_count, LANES).astype(jnp.float32)

time: 32.6 us -> 31.7 us (0.972)
  waiting for transfers between devices: 2.87 us -> 0.71 us
  blocking collectives: 14.9 us -> 16.2 us
    ppermute x2, waiting for transfers between devices: 2.17 us -> 0.01 us  [local(): lax.ppermute(fields, 'lat', edges + [(j, i) for i, j in edges])]
    all_to_all x1, blocking collectives: 14.9 us -> 16.2 us  [local(): lax.all_to_all(coefficients, 'lat', split_axis=0, concat_axis=0, tiled=True)]
  transfers between devices with their start and end apart: 3 -> 3, of which waited for: 2 -> 1; matrix products, arithmetic and copies ran while one was open for 0% -> 0% of each run, Pallas kernels for 15% -> 15%
where the time goes in v12:
time: 31.7 us; the launch traced here: 31.5 us
  blocking collectives  16.2 us (51%)
  Pallas kernels  10.6 us (33%)
  starting transfers between devices  3.66 us (12%)
  waiting for transfers between devices  0.71 us (2%)
    all_to_all x1, blocking collectives, local(): lax.all_to_all(coefficients, 'lat', split_axis=0, concat_axis=0, tiled=True)  16.2 us
    pallas_call x1, Pallas kernels, local(): pl.pallas_call(functools.partial(near_kernel, pair_count * owners, pair_c...  4.34 us
    ppermute x2, starting transfers between devices, local(): lax.ppermute(fields, 'lat', edges + [(j, i) for i, j in edges])  3.59 us
    pallas_call x1, Pallas kernels, local(): pl.pallas_call(far_kernel, out_shape=jax.ShapeDtypeStruct((owners, 2 * SU...  2.96 us
    pallas_call x1, Pallas kernels, local(): pl.pallas_call(functools.partial(legendre_kernel, level_owners, level_cou...  2.76 us
    ppermute x1, waiting for transfers between devices, local(): totals = lax.ppermute(total, 'lev', [(0, 1), (1, 0)])[None]  0.7 us
  transfers between devices with their start and end apart: 3, of which 1 were waited for; matrix products, arithmetic and copies ran while one was open for 0% of the time, Pallas kernels for 15%

profile of v12, /device:TPU:0, one launch (start us, length us, event | category | flops | bytes accessed | tf_op | source)
XLA Modules:
  0.0 31.5 jit_solution(17310923499012688250)
XLA Ops:
  0.0 2.9 %collective-permute-start = (bf16[2,4,2,2816]{3,2,1,0:T(2,128)(2,1)}, bf16[2,4,2,2816]{3,2,1,0:T(2,128)(2,1)S(1)}, u32[]{:S(2)}, u32[]{:S(2)}) collective-permute-start(bf16[2,4,2,2816]{3,2,1,0:T(2,128)(2,1)} %fields_far.1), channel_id=1, source_target_pairs={{0,2},{4,6},{8,10},{12,14},{16,18},{20,22},{24,26},{28,30},{2,0},{... | collective-permute-start | bytes 270344 | tf_op jit(solution)/shard_map/ppermute | solution.py:415
  2.9 0.7 %collective-permute-start.1 = (bf16[2,4,2,2816]{3,2,1,0:T(2,128)(2,1)}, bf16[2,4,2,2816]{3,2,1,0:T(2,128)(2,1)S(1)}, u32[]{:S(2)}, u32[]{:S(2)}) collective-permute-start(bf16[2,4,2,2816]{3,2,1,0:T(2,128)(2,1)} %fields_far.1), channel_id=1, source_target_pairs={{2,4},{6,8},{10,12},{14,16},{18,20},{22,24},{26,28},{4,2},{8,6},{1... | collective-permute-start | bytes 270344 | tf_op jit(solution)/shard_map/ppermute | solution.py:415
  3.6 4.3 %near_rows.1 = (f32[2,11,8,256]{3,2,1,0:T(8,128)S(1)}, bf16[2,256,2560]{2,1,0:T(8,128)(2,1)S(1)}, f32[2,11,8,2560]{3,2,1,0:T(8,128)S(1)}, s32[2,2,11,2,8,128]{5,...) custom-call(s32[2]{0:T(128)} %rows_first_far.1, s32[32]{0:T(128)} %points_far.1, ...), custom_call_target="tpu_custom_call" | custom-call | flops 10000000 | bytes 4000000 | tf_op jit(solution)/shard_map/near_rows/pallas_call | solution.py:421
  7.9 0.0 collective-permute-done.near_side
  8.0 0.0 collective-permute-done.1.far_side
  8.0 0.0 copy-start.1
  8.0 0.0 copy-start
  8.0 3.0 %far_rows.1 = bf16[16,32,128]{2,1,0:T(8,128)(2,1)S(1)} custom-call(bf16[2,4,2,2816]{3,2,1,0:T(2,128)(2,1)S(1)} %collective-permute-done.near_side, bf16[2,4,2,2816]{3,2,1,0:T(2,128)(2,1)S(1)} %collective-permute-done.1.far_side, s32[2,2,11,2,8,128]{5,4,3,2,1,0:T(8,128)S(1)} %get-tuple-element.12.far_starts, ...), custom_call_target="tpu_custom_call" | custom-call | tf_op jit(solution)/shard_map/far_rows/pallas_call | solution.py:450
  11.0 16.2 %all_to_all.5.received = bf16[16,32,128]{2,1,0:T(8,128)(2,1)S(1)} all-to-all(bf16[16,32,128]{2,1,0:T(8,128)(2,1)S(1)} %far_rows.1), channel_id=1, replica_groups=mesh['lat'=16,'lev'=2] {'lat'}, dimensions={0} | all-to-all | bytes 262144 | tf_op jit(solution)/shard_map/all_to_all | solution.py:465
  27.2 0.1 fusion.1
  27.3 0.0 copy-done.1
  27.3 0.2 fusion
  27.5 0.1 collective-permute-start.2
  27.6 0.5 %left_rows.1.left_given = bf16[5,320,256]{2,1,0:T(8,128)(2,1)S(1)} custom-call(bf16[16,32,128]{2,1,0:T(8,128)(2,1)S(1)} %all_to_all.5.received), custom_call_target="tpu_custom_call" | custom-call | flops 50000000 | bytes 2000000 | tf_op jit(solution)/shard_map/left_rows/pallas_call | solution.py:480
  28.1 0.7 %collective-permute-done.2 = f32[2,32,128]{2,1,0:T(8,128)S(1)} collective-permute-done((f32[2,32,128]{2,1,0:T(8,128)S(1)}, f32[2,32,128]{2,1,0:T(8,128)S(1)}, u32[]{:S(2)}, u32[]{:S(2)}) %collective-permute-start.2) | collective-permute-done | bytes 32800 | tf_op jit(solution)/shard_map/ppermute | solution.py:471
  28.8 0.0 copy-done
  28.8 2.8 %degree_sums.1 = (bf16[2,5,2,40,1281]{4,3,2,1,0:T(8,128)(2,1)}, bf16[5,320,256]{2,1,0:T(8,128)(2,1)S(1)}) custom-call(f32[2]{0:T(128)S(1)} %copy-done.1, bf16[16,32,128]{2,1,0:T(8,128)(2,1)S(1)} %all_to_all.5.received, f32[1,2,32,128]{3,2,1,0:T(8,128)S(1)} %bitcast.13, bf16[40,32,1281]{2,1,0:T(8,128)(2,1)S(1)} %copy-done, ...), custom_call_target="tpu_custom_call", output_to_operand_aliasing={{1}: (4, {})} | custom-call | tf_op jit(solution)/shard_map/degree_sums/pallas_call | solution.py:490
  (1 shorter events, 0.0 us)
Async XLA Ops:
  0.0 7.9 %collective-permute-start = (bf16[2,4,2,2816]{3,2,1,0:T(2,128)(2,1)}, bf16[2,4,2,2816]{3,2,1,0:T(2,128)(2,1)S(1)}, u32[]{:S(2)}, u32[]{:S(2)}) collective-permute-start(bf16[2,4,2,2816]{3,2,1,0:T(2,128)(2,1)} %fields_far.1), channel_id=1, source_target_pairs={{0,2},{4,6},{8,10},{12,14},{16,18},{20,22},{24,26},{28,30},{2,0},{... | collective-permute-start | bytes 270344 | tf_op jit(solution)/shard_map/ppermute | solution.py:415
  2.9 5.0 %collective-permute-start.1 = (bf16[2,4,2,2816]{3,2,1,0:T(2,128)(2,1)}, bf16[2,4,2,2816]{3,2,1,0:T(2,128)(2,1)S(1)}, u32[]{:S(2)}, u32[]{:S(2)}) collective-permute-start(bf16[2,4,2,2816]{3,2,1,0:T(2,128)(2,1)} %fields_far.1), channel_id=1, source_target_pairs={{2,4},{6,8},{10,12},{14,16},{18,20},{22,24},{26,28},{4,2},{8,6},{1... | collective-permute-start | bytes 270344 | tf_op jit(solution)/shard_map/ppermute | solution.py:415
  8.0 19.3 %copy-start.1 = (f32[2]{0:T(128)S(1)}, f32[2]{0:T(128)}, u32[]{:S(2)}) copy-start(f32[2]{0:T(128)} %thickness.1) | copy-start | bytes 28
  8.0 20.8 %copy-start = (bf16[40,32,1281]{2,1,0:T(8,128)(2,1)S(1)}, bf16[40,32,1281]{2,1,0:T(8,128)(2,1)}, u32[]{:S(2)}) copy-start(bf16[40,32,1281]{2,1,0:T(8,128)(2,1)} %legendre.1) | copy-start | bytes 9838084
  27.5 1.3 %collective-permute-start.2 = (f32[2,32,128]{2,1,0:T(8,128)S(1)}, f32[2,32,128]{2,1,0:T(8,128)S(1)}, u32[]{:S(2)}, u32[]{:S(2)}) collective-permute-start(f32[2,32,128]{2,1,0:T(8,128)S(1)} %bitcast.16), channel_id=1, source_target_pairs={{0,1},{1,0},{2,3},{3,2},{4,5},{5,4},{6,7},{7,6},{8,9},{9,8},{10,11... | collective-permute-start | bytes 98312 | tf_op jit(solution)/shard_map/ppermute | solution.py:471

commit v13 on v12

--- a/solution.py
+++ b/solution.py
@@ -19,6 +19,20 @@
     return jnp.take_along_axis(values, lanes, axis=1, mode="promise_in_bounds")
 
 
+TAKE = lax.GatherDimensionNumbers(
+    offset_dims=(),
+    collapsed_slice_dims=(1,),
+    start_index_map=(1,),
+    operand_batching_dims=(0,),
+    start_indices_batching_dims=(0,),
+)
+
+
+def short_gather(values, lanes):
+    mode = lax.GatherScatterMode.PROMISE_IN_BOUNDS
+    return lax.gather(values, lanes[:, :, None], TAKE, (1, 1), mode=mode)
+
+
 SINE = (-70.99342854244645, 81.34076844400118, -41.337142359536955, 6.283164044230117)
 COSINE = (
     56.2423804697887, -85.2403304160897, 64.93459063550272, -19.739171434929204, 0.9999999534680867,
@@ -60,21 +74,26 @@
 
 def extend(lines, row, rows_each, missing, ext, slot):
     blocks = ext.shape[1] - 2
-    for block in range(blocks):
-        ext[slot, block + 1] = lines[
-            pl.ds(block * rows_each + row, SUB, stride=blocks * rows_each), :
-        ]
+
+    def block_of(block):
+        return lines[pl.ds(block * rows_each + row, SUB, stride=blocks * rows_each), :]
+
+    def place(block, values):
+        ext[slot, block] = jnp.concatenate([values, values], axis=0).astype(jnp.bfloat16)
+
+    for block in range(blocks - 1):
+        place(block + 1, block_of(block))
     lane = lax.broadcasted_iota(jnp.int32, (SUB, LANES), 1)
     ahead = lane + missing
     behind = lane - missing
-    first = lane_gather(ext[slot, 1], ahead & (LANES - 1))
-    second = lane_gather(ext[slot, 2], ahead & (LANES - 1))
-    last = ext[slot, blocks]
+    first = lane_gather(block_of(0), ahead & (LANES - 1))
+    second = lane_gather(block_of(1), ahead & (LANES - 1))
+    last = block_of(blocks - 1)
     final = lane_gather(last, behind & (LANES - 1))
-    before = lane_gather(ext[slot, blocks - 1], behind & (LANES - 1))
-    ext[slot, 0] = jnp.where(behind >= 0, final, before)
-    ext[slot, blocks] = jnp.where(ahead < LANES, last, first)
-    ext[slot, blocks + 1] = jnp.where(ahead < LANES, first, second)
+    before = lane_gather(block_of(blocks - 2), behind & (LANES - 1))
+    place(0, jnp.where(behind >= 0, final, before))
+    place(blocks, jnp.where(ahead < LANES, last, first))
+    place(blocks + 1, jnp.where(ahead < LANES, first, second))
 
 
 def spread_rows(starts, begins):
@@ -101,12 +120,19 @@
 
 def gathered(totals, starts, scales, parts):
     for side in range(2):
-        for column in range(4):
-            place = starts[side] + column
-            lane = place & (LANES - 1)
-            low, middle, high = [lane_gather(part, lane) for part in parts[side : side + 3]]
-            value = jnp.where(place < LANES, low, jnp.where(place < 2 * LANES, middle, high))
-            totals[side] = totals[side] + scales[STENCIL * side + column] * value
+        for pair in range(2):
+            spot = starts[side] + jnp.int16(2 * pair)
+            lane = spot & jnp.int16(LANES - 1)
+            low, middle, high = [short_gather(part, lane) for part in parts[side : side + 3]]
+            value = jnp.where(
+                spot < jnp.int16(LANES),
+                low,
+                jnp.where(spot < jnp.int16(2 * LANES), middle, high),
+            ).astype(jnp.float32)
+            line = STENCIL * side + 2 * pair
+            totals[side] = (
+                totals[side] + scales[line] * value[:SUB] + scales[line + 1] * value[SUB:]
+            )
     return totals
 
 
@@ -180,6 +206,7 @@
     spread_lines(fields, lines)
     for latitude in range(lat_count):
         extend(lines, latitude, lat_count, lon - points[first_lat + latitude], ext, latitude)
+    lower = (lax.broadcasted_iota(jnp.int32, (2 * SUB, LANES), 0) >= SUB).astype(jnp.int32)
     for latitude in range(lat_count):
         mine = first_lat - rows_first[latitude]
         for couple in range(couples):
@@ -187,11 +214,14 @@
             def spread_row(row):
                 at = ((latitude * STENCIL + row) * couples + couple) * SUB
                 tile = factors[pl.ds(pl.multiple_of(at, SUB), SUB), :]
+                begun = []
+                for side in range(2):
+                    start = jnp.broadcast_to(
+                        begins[latitude, row, 2 * couple + side], (2 * SUB, LANES)
+                    )
+                    begun.append((start + lower).astype(jnp.int16))
                 return (
-                    [
-                        jnp.broadcast_to(begins[latitude, row, 2 * couple + side], (SUB, LANES))
-                        for side in range(2)
-                    ],
+                    begun,
                     [jnp.broadcast_to(tile[line : line + 1], (SUB, LANES)) for line in range(SUB)],
                 )
 
@@ -229,8 +259,9 @@
     width = 256
     choices = ((2, 1, 0), (3, 2, 1))
     for latitude in range(lat_count):
-        at_zero = fact[latitude] == 0
-        at_one = fact[latitude] == 1
+        own = jnp.broadcast_to(facts[latitude : latitude + 1], (2 * SUB, LANES)).astype(jnp.int16)
+        at_zero = own == jnp.int16(0)
+        at_one = own == jnp.int16(1)
         for couple in range(couples):
             sides = [pl.ds(side * LANES, LANES) for side in range(2)]
             totals = [partial[latitude, couple, :, lanes] for lanes in sides]
@@ -424,7 +455,7 @@
             jax.ShapeDtypeStruct((lat_count, couples, SUB, 2 * LANES), jnp.float32),
             jax.ShapeDtypeStruct((lat_count, 2 * LANES, 2 * columns), jnp.bfloat16),
             jax.ShapeDtypeStruct((lat_count, couples, SUB, 2 * columns), jnp.float32),
-            jax.ShapeDtypeStruct((lat_count, 2, couples, 2, SUB, LANES), jnp.int32),
+            jax.ShapeDtypeStruct((lat_count, 2, couples, 2, 2 * SUB, LANES), jnp.int16),
             jax.ShapeDtypeStruct((lat_count, 2, couples, SUB, SUB, LANES), jnp.float32),
             jax.ShapeDtypeStruct((4 * lat_count, LANES), jnp.int32),
         ),
@@ -439,7 +470,7 @@
             pltpu.VMEM((lat_count, STENCIL, blocks, 1, LANES), jnp.int32),
             pltpu.VMEM((weights.size // LANES, LANES), jnp.float32),
             pltpu.VMEM((fields.size // LANES, LANES), jnp.float32),
-            pltpu.VMEM((lat_count, blocks + 2, SUB, LANES), jnp.float32),
+            pltpu.VMEM((lat_count, blocks + 2, 2 * SUB, LANES), jnp.bfloat16),
             pltpu.SemaphoreType.DMA((5,)),
         ],
         compiler_params=params,
@@ -454,7 +485,7 @@
         out_specs=vector,
         scratch_shapes=[
             pltpu.VMEM((2, fields.size // LANES, LANES), jnp.float32),
-            pltpu.VMEM((2 * lat_count, blocks + 2, SUB, LANES), jnp.float32),
+            pltpu.VMEM((2 * lat_count, blocks + 2, 2 * SUB, LANES), jnp.bfloat16),
             pltpu.VMEM((lat_count, couples, SUB, 2 * LANES), jnp.float32),
             pltpu.VMEM((lat_count, 2 * SUB, columns + LANES), jnp.float32),
         ],

time: 31.7 us -> 30.4 us (0.959)
  Pallas kernels: 10.6 us -> 8.45 us
  blocking collectives: 16.2 us -> 17 us
    pallas_call x1, Pallas kernels: 2.96 us -> 1.88 us  [local(): pl.pallas_call(far_kernel, out_shape=jax.ShapeDtypeStruct((owners, 2 * SU...]
    pallas_call x1, Pallas kernels: 4.34 us -> 3.33 us  [local(): pl.pallas_call(functools.partial(near_kernel, pair_count * owners, pair_c...]
    all_to_all x1, blocking collectives: 16.2 us -> 17 us  [local(): lax.all_to_all(coefficients, 'lat', split_axis=0, concat_axis=0, tiled=True)]
  transfers between devices with their start and end apart: 3 -> 3, of which waited for: 1 -> 1; matrix products, arithmetic and copies ran while one was open for 0% -> 0% of each run, Pallas kernels for 15% -> 13%
where the time goes in v13:
time: 30.4 us; the launch traced here: 30.2 us
  blocking collectives  17 us (56%)
  Pallas kernels  8.45 us (28%)
  starting transfers between devices  3.66 us (12%)
  waiting for transfers between devices  0.71 us (2%)
    all_to_all x1, blocking collectives, local(): lax.all_to_all(coefficients, 'lat', split_axis=0, concat_axis=0, tiled=True)  17 us
    ppermute x2, starting transfers between devices, local(): lax.ppermute(fields, 'lat', edges + [(j, i) for i, j in edges])  3.59 us
    pallas_call x1, Pallas kernels, local(): pl.pallas_call(functools.partial(near_kernel, pair_count * owners, pair_c...  3.33 us
    pallas_call x1, Pallas kernels, local(): pl.pallas_call(functools.partial(legendre_kernel, level_owners, level_cou...  2.76 us
    pallas_call x1, Pallas kernels, local(): pl.pallas_call(far_kernel, out_shape=jax.ShapeDtypeStruct((owners, 2 * SU...  1.88 us
    ppermute x1, waiting for transfers between devices, local(): totals = lax.ppermute(total, 'lev', [(0, 1), (1, 0)])[None]  0.7 us
  transfers between devices with their start and end apart: 3, of which 1 were waited for; matrix products, arithmetic and copies ran while one was open for 0% of the time, Pallas kernels for 13%

profile of v13, /device:TPU:0, one launch (start us, length us, event | category | flops | bytes accessed | tf_op | source)
XLA Modules:
  0.0 30.2 jit_solution(3456240698856544660)
XLA Ops:
  0.0 2.9 %collective-permute-start = (bf16[2,4,2,2816]{3,2,1,0:T(2,128)(2,1)}, bf16[2,4,2,2816]{3,2,1,0:T(2,128)(2,1)S(1)}, u32[]{:S(2)}, u32[]{:S(2)}) collective-permute-start(bf16[2,4,2,2816]{3,2,1,0:T(2,128)(2,1)} %fields_far.1), channel_id=1, source_target_pairs={{0,2},{4,6},{8,10},{12,14},{16,18},{20,22},{24,26},{28,30},{2,0},{... | collective-permute-start | bytes 270344 | tf_op jit(solution)/shard_map/ppermute | solution.py:446
  2.9 0.7 %collective-permute-start.1 = (bf16[2,4,2,2816]{3,2,1,0:T(2,128)(2,1)}, bf16[2,4,2,2816]{3,2,1,0:T(2,128)(2,1)S(1)}, u32[]{:S(2)}, u32[]{:S(2)}) collective-permute-start(bf16[2,4,2,2816]{3,2,1,0:T(2,128)(2,1)} %fields_far.1), channel_id=1, source_target_pairs={{2,4},{6,8},{10,12},{14,16},{18,20},{22,24},{26,28},{4,2},{8,6},{1... | collective-permute-start | bytes 270344 | tf_op jit(solution)/shard_map/ppermute | solution.py:446
  3.6 3.3 %near_rows.1 = (f32[2,11,8,256]{3,2,1,0:T(8,128)S(1)}, bf16[2,256,2560]{2,1,0:T(8,128)(2,1)S(1)}, f32[2,11,8,2560]{3,2,1,0:T(8,128)S(1)}, s16[2,2,11,2,16,128]{5...) custom-call(s32[2]{0:T(128)} %rows_first_far.1, s32[32]{0:T(128)} %points_far.1, ...), custom_call_target="tpu_custom_call" | custom-call | flops 10000000 | bytes 4000000 | tf_op jit(solution)/shard_map/near_rows/pallas_call | solution.py:452
  6.9 0.0 collective-permute-done.near_side
  6.9 0.0 collective-permute-done.1.far_side
  7.0 0.0 copy-start.1
  7.0 0.0 copy-start
  7.0 1.9 %far_rows.1 = bf16[16,32,128]{2,1,0:T(8,128)(2,1)S(1)} custom-call(bf16[2,4,2,2816]{3,2,1,0:T(2,128)(2,1)S(1)} %collective-permute-done.near_side, bf16[2,4,2,2816]{3,2,1,0:T(2,128)(2,1)S(1)} %collective-permute-done.1.far_side, s16[2,2,11,2,16,128]{5,4,3,2,1,0:T(8,128)(2,1)S(1)} %get-tuple-element.12.far_starts, ...), custom_call_target="tpu_custom_call" | custom-call | tf_op jit(solution)/shard_map/far_rows/pallas_call | solution.py:481
  8.9 17.0 %all_to_all.5.received = bf16[16,32,128]{2,1,0:T(8,128)(2,1)S(1)} all-to-all(bf16[16,32,128]{2,1,0:T(8,128)(2,1)S(1)} %far_rows.1), channel_id=1, replica_groups=mesh['lat'=16,'lev'=2] {'lat'}, dimensions={0} | all-to-all | bytes 262144 | tf_op jit(solution)/shard_map/all_to_all | solution.py:496
  25.9 0.1 fusion.1
  26.0 0.0 copy-done.1
  26.0 0.2 fusion
  26.2 0.1 collective-permute-start.2
  26.3 0.5 %left_rows.1.left_given = bf16[5,320,256]{2,1,0:T(8,128)(2,1)S(1)} custom-call(bf16[16,32,128]{2,1,0:T(8,128)(2,1)S(1)} %all_to_all.5.received), custom_call_target="tpu_custom_call" | custom-call | flops 50000000 | bytes 2000000 | tf_op jit(solution)/shard_map/left_rows/pallas_call | solution.py:511
  26.7 0.7 %collective-permute-done.2 = f32[2,32,128]{2,1,0:T(8,128)S(1)} collective-permute-done((f32[2,32,128]{2,1,0:T(8,128)S(1)}, f32[2,32,128]{2,1,0:T(8,128)S(1)}, u32[]{:S(2)}, u32[]{:S(2)}) %collective-permute-start.2) | collective-permute-done | bytes 32800 | tf_op jit(solution)/shard_map/ppermute | solution.py:502
  27.4 0.0 copy-done
  27.4 2.8 %degree_sums.1 = (bf16[2,5,2,40,1281]{4,3,2,1,0:T(8,128)(2,1)}, bf16[5,320,256]{2,1,0:T(8,128)(2,1)S(1)}) custom-call(f32[2]{0:T(128)S(1)} %copy-done.1, bf16[16,32,128]{2,1,0:T(8,128)(2,1)S(1)} %all_to_all.5.received, f32[1,2,32,128]{3,2,1,0:T(8,128)S(1)} %bitcast.13, bf16[40,32,1281]{2,1,0:T(8,128)(2,1)S(1)} %copy-done, ...), custom_call_target="tpu_custom_call", output_to_operand_aliasing={{1}: (4, {})} | custom-call | tf_op jit(solution)/shard_map/degree_sums/pallas_call | solution.py:521
  (1 shorter events, 0.0 us)
Async XLA Ops:
  0.0 6.9 %collective-permute-start = (bf16[2,4,2,2816]{3,2,1,0:T(2,128)(2,1)}, bf16[2,4,2,2816]{3,2,1,0:T(2,128)(2,1)S(1)}, u32[]{:S(2)}, u32[]{:S(2)}) collective-permute-start(bf16[2,4,2,2816]{3,2,1,0:T(2,128)(2,1)} %fields_far.1), channel_id=1, source_target_pairs={{0,2},{4,6},{8,10},{12,14},{16,18},{20,22},{24,26},{28,30},{2,0},{... | collective-permute-start | bytes 270344 | tf_op jit(solution)/shard_map/ppermute | solution.py:446
  2.9 4.0 %collective-permute-start.1 = (bf16[2,4,2,2816]{3,2,1,0:T(2,128)(2,1)}, bf16[2,4,2,2816]{3,2,1,0:T(2,128)(2,1)S(1)}, u32[]{:S(2)}, u32[]{:S(2)}) collective-permute-start(bf16[2,4,2,2816]{3,2,1,0:T(2,128)(2,1)} %fields_far.1), channel_id=1, source_target_pairs={{2,4},{6,8},{10,12},{14,16},{18,20},{22,24},{26,28},{4,2},{8,6},{1... | collective-permute-start | bytes 270344 | tf_op jit(solution)/shard_map/ppermute | solution.py:446
  7.0 19.0 %copy-start.1 = (f32[2]{0:T(128)S(1)}, f32[2]{0:T(128)}, u32[]{:S(2)}) copy-start(f32[2]{0:T(128)} %thickness.1) | copy-start | bytes 28
  7.0 20.5 %copy-start = (bf16[40,32,1281]{2,1,0:T(8,128)(2,1)S(1)}, bf16[40,32,1281]{2,1,0:T(8,128)(2,1)}, u32[]{:S(2)}) copy-start(bf16[40,32,1281]{2,1,0:T(8,128)(2,1)} %legendre.1) | copy-start | bytes 9838084
  26.2 1.3 %collective-permute-start.2 = (f32[2,32,128]{2,1,0:T(8,128)S(1)}, f32[2,32,128]{2,1,0:T(8,128)S(1)}, u32[]{:S(2)}, u32[]{:S(2)}) collective-permute-start(f32[2,32,128]{2,1,0:T(8,128)S(1)} %bitcast.16), channel_id=1, source_target_pairs={{0,1},{1,0},{2,3},{3,2},{4,5},{5,4},{6,7},{7,6},{8,9},{9,8},{10,11... | collective-permute-start | bytes 98312 | tf_op jit(solution)/shard_map/ppermute | solution.py:502

commit v14 on v13

--- a/solution.py
+++ b/solution.py
@@ -136,10 +136,23 @@
     return totals
 
 
+def add_unit(latitude, choice, slot, far_starts, far_scales, ext, into):
+    for couple in range(into.shape[1]):
+        sides = [pl.ds(side * LANES, LANES) for side in range(2)]
+        totals = gathered(
+            [into[latitude, couple, :, lanes] for lanes in sides],
+            [far_starts[latitude, choice, couple, side] for side in range(2)],
+            [far_scales[latitude, choice, couple, line] for line in range(SUB)],
+            [ext[slot, 2 * couple + piece] for piece in range(4)],
+        )
+        for lanes, total in zip(sides, totals):
+            into[latitude, couple, :, lanes] = total
+
+
 def near_kernel(
-    pair_total, pair_count, rows_first_far, points_far, fields_far, starts_far, weights_far,
+    pair_total, pair_count, rows_first_far, points_far, fields_far, starts_far, weights_far, side_rows,
     partial, table, twiddle, far_starts, far_scales, facts,
-    rows_first, points, fields, starts, weights, begins, factors, lines, ext, arrived,
+    rows_first, points, fields, starts, weights, begins, factors, lines, side_lines, ext, arrived,
 ):
     lat_count, couples = partial.shape[:2]
     lon = 2 * couples * LANES
@@ -159,6 +172,7 @@
     ]
     for fetch in fetches:
         fetch.start()
+    spread_lines(side_rows, side_lines)
     fetches[0].wait()
     width = 256
     scales = []
@@ -194,18 +208,29 @@
                 table[latitude, rows, there] = turned[1].astype(jnp.bfloat16)
     for fetch in fetches[1:]:
         fetch.wait()
-    known = [first_lat - rows_first[latitude] for latitude in range(lat_count)]
-    known += [points[first_lat + latitude] for latitude in range(lat_count)]
-    for place in range(-lat_count, 2 * lat_count):
-        if place < 0 or place >= lat_count:
-            place = jnp.clip(first_lat + place, 0, points.shape[0] - 1)
-            known.append(lon - points[place])
+    upper = lax.axis_index("lat") % 2 == 0
+
+    def missing_of(slot, above):
+        place = jnp.where(above, first_lat + lat_count + slot, first_lat - lat_count + slot)
+        return lon - points[jnp.clip(place, 0, points.shape[0] - 1)]
+
+    units = {}
+    for latitude in range(lat_count):
+        for choice in range(2):
+            slot = 2 + choice - (first_lat - rows_first[latitude])
+            units[latitude, choice] = ((slot >= 2) == upper, slot % 2)
+    known = [points[first_lat + latitude] for latitude in range(lat_count)]
+    known += [jnp.where(ours, -1, row) for ours, row in units.values()]
+    known += [missing_of(row, jnp.logical_not(upper)) for row in range(lat_count)]
     facts[...] = jnp.concatenate([jnp.full((1, LANES), one, jnp.int32) for one in known], axis=0)
     spread_rows(starts, begins)
     spread_lines(weights, factors)
     spread_lines(fields, lines)
     for latitude in range(lat_count):
         extend(lines, latitude, lat_count, lon - points[first_lat + latitude], ext, latitude)
+        extend(
+            side_lines, latitude, lat_count, missing_of(latitude, upper), ext, lat_count + latitude
+        )
     lower = (lax.broadcasted_iota(jnp.int32, (2 * SUB, LANES), 0) >= SUB).astype(jnp.int32)
     for latitude in range(lat_count):
         mine = first_lat - rows_first[latitude]
@@ -239,46 +264,45 @@
                     far_starts[latitude, choice, couple, side] = begun[side]
                 for line in range(SUB):
                     far_scales[latitude, choice, couple, line] = scales[line]
+        for choice in range(2):
+            ours, row = units[latitude, choice]
+
+            @pl.when(ours)
+            def add(latitude=latitude, choice=choice, row=row):
+                add_unit(latitude, choice, lat_count + row, far_starts, far_scales, ext, partial)
 
 
 def far_kernel(
-    near_side, far_side, far_starts, far_scales, facts, partial, table, twiddle,
+    far_side, far_starts, far_scales, facts, partial, table, twiddle,
     out, lines, ext, grid, waves,
 ):
     lat_count, couples = partial.shape[:2]
     columns = table.shape[2] // 2
     owners = out.shape[0]
-    toward = 1 - lax.axis_index("lat") % 2
-    spread_lines(near_side, lines.at[toward])
-    spread_lines(far_side, lines.at[1 - toward])
+    spread_lines(far_side, lines)
     fact = [jnp.broadcast_to(facts[row : row + 1], (SUB, LANES)) for row in range(4 * lat_count)]
-    for slot in range(2 * lat_count):
-        side, row = divmod(slot, lat_count)
-        extend(lines.at[side], row, lat_count, fact[2 * lat_count + slot], ext, slot)
+    for row in range(lat_count):
+        extend(lines, row, lat_count, fact[3 * lat_count + row], ext, row)
+    grid[...] = partial[...]
+    for latitude in range(lat_count):
+        for choice in range(2):
+            code = fact[lat_count + 2 * latitude + choice].astype(jnp.float32)
+            place = jnp.max(code).astype(jnp.int32)
+
+            @pl.when(place >= 0)
+            def add(latitude=latitude, choice=choice, place=place):
+                add_unit(latitude, choice, place, far_starts, far_scales, ext, grid)
+
     lane = lax.broadcasted_iota(jnp.int32, (SUB, LANES), 1)
     width = 256
-    choices = ((2, 1, 0), (3, 2, 1))
-    for latitude in range(lat_count):
-        own = jnp.broadcast_to(facts[latitude : latitude + 1], (2 * SUB, LANES)).astype(jnp.int16)
-        at_zero = own == jnp.int16(0)
-        at_one = own == jnp.int16(1)
+    for latitude in range(lat_count):
         for couple in range(couples):
-            sides = [pl.ds(side * LANES, LANES) for side in range(2)]
-            totals = [partial[latitude, couple, :, lanes] for lanes in sides]
-            for choice, slots in enumerate(choices):
-                parts = []
-                for piece in range(4):
-                    zero, one, two = [ext[slot, 2 * couple + piece] for slot in slots]
-                    parts.append(jnp.where(at_zero, zero, jnp.where(at_one, one, two)))
-                totals = gathered(
-                    totals,
-                    [far_starts[latitude, choice, couple, side] for side in range(2)],
-                    [far_scales[latitude, choice, couple, line] for line in range(SUB)],
-                    parts,
+            for side in range(2):
+                lanes = pl.ds(side * LANES, LANES)
+                live = lane + (2 * couple + side) * LANES < fact[latitude]
+                grid[latitude, couple, :, lanes] = jnp.where(
+                    live, grid[latitude, couple, :, lanes], 0.0
                 )
-            for side in range(2):
-                live = lane + (2 * couple + side) * LANES < fact[lat_count + latitude]
-                grid[latitude, couple, :, sides[side]] = jnp.where(live, totals[side], 0.0)
     for latitude in range(lat_count):
         rows = grid[latitude].reshape(couples * SUB, 2 * LANES).astype(jnp.bfloat16)
         for at in range(0, columns, width):
@@ -459,7 +483,7 @@
             jax.ShapeDtypeStruct((lat_count, 2, couples, SUB, SUB, LANES), jnp.float32),
             jax.ShapeDtypeStruct((4 * lat_count, LANES), jnp.int32),
         ),
-        in_specs=[remote] * 5,
+        in_specs=[remote] * 5 + [vector],
         out_specs=(vector,) * 6,
         scratch_shapes=[
             pltpu.SMEM(rows_first.shape, jnp.int32),
@@ -470,28 +494,29 @@
             pltpu.VMEM((lat_count, STENCIL, blocks, 1, LANES), jnp.int32),
             pltpu.VMEM((weights.size // LANES, LANES), jnp.float32),
             pltpu.VMEM((fields.size // LANES, LANES), jnp.float32),
-            pltpu.VMEM((lat_count, blocks + 2, 2 * SUB, LANES), jnp.bfloat16),
+            pltpu.VMEM((fields.size // LANES, LANES), jnp.float32),
+            pltpu.VMEM((2 * lat_count, blocks + 2, 2 * SUB, LANES), jnp.bfloat16),
             pltpu.SemaphoreType.DMA((5,)),
         ],
         compiler_params=params,
         cost_estimate=pl.CostEstimate(flops=10_000_000, bytes_accessed=4_000_000, transcendentals=0),
         name="near_rows",
-    )(*(held(value) for value in (rows_first, points, fields, starts, weights)))
+    )(*(held(value) for value in (rows_first, points, fields, starts, weights)), sides[0])
 
     coefficients = pl.pallas_call(
         far_kernel,
         out_shape=jax.ShapeDtypeStruct((owners, 2 * SUB * lat_count, LANES), jnp.bfloat16),
-        in_specs=[vector] * 8,
+        in_specs=[vector] * 7,
         out_specs=vector,
         scratch_shapes=[
-            pltpu.VMEM((2, fields.size // LANES, LANES), jnp.float32),
-            pltpu.VMEM((2 * lat_count, blocks + 2, 2 * SUB, LANES), jnp.bfloat16),
+            pltpu.VMEM((fields.size // LANES, LANES), jnp.float32),
+            pltpu.VMEM((lat_count, blocks + 2, 2 * SUB, LANES), jnp.bfloat16),
             pltpu.VMEM((lat_count, couples, SUB, 2 * LANES), jnp.float32),
             pltpu.VMEM((lat_count, 2 * SUB, columns + LANES), jnp.float32),
         ],
         compiler_params=params,
         name="far_rows",
-    )(*sides, far_starts, far_scales, facts, partial, table, twiddle)
+    )(sides[1], far_starts, far_scales, facts, partial, table, twiddle)
 
     received = lax.all_to_all(coefficients, "lat", split_axis=0, concat_axis=0, tiled=True)
     by_level = received.reshape(lat_total, 2, level_count, field_count, LANES).astype(jnp.float32)

time: 30.4 us -> 31.3 us (1.030)
  waiting for transfers between devices: 0.71 us -> 2.87 us
  blocking collectives: 17 us -> 14.9 us
  Pallas kernels: 8.45 us -> 9.32 us
    ppermute x2, waiting for transfers between devices: 0.01 us -> 2.17 us  [local(): lax.ppermute(fields, 'lat', edges + [(j, i) for i, j in edges])]
    all_to_all x1, blocking collectives: 17 us -> 14.9 us  [local(): lax.all_to_all(coefficients, 'lat', split_axis=0, concat_axis=0, tiled=True)]
    pallas_call x1, Pallas kernels: 3.33 us -> 4.88 us  [local(): pl.pallas_call(functools.partial(near_kernel, pair_count * owners, pair_c...]
    pallas_call x1, Pallas kernels: 1.88 us -> 1.19 us  [local(): pl.pallas_call(far_kernel, out_shape=jax.ShapeDtypeStruct((owners, 2 * SU...]
  transfers between devices with their start and end apart: 3 -> 3, of which waited for: 1 -> 2; matrix products, arithmetic and copies ran while one was open for 0% -> 0% of each run, Pallas kernels for 13% -> 17%
where the time goes in v14:
time: 31.3 us; the launch traced here: 31.1 us
  blocking collectives  14.9 us (48%)
  Pallas kernels  9.32 us (30%)
  starting transfers between devices  3.66 us (12%)
  waiting for transfers between devices  2.87 us (9%)
    all_to_all x1, blocking collectives, local(): lax.all_to_all(coefficients, 'lat', split_axis=0, concat_axis=0, tiled=True)  14.9 us
    pallas_call x1, Pallas kernels, local(): pl.pallas_call(functools.partial(near_kernel, pair_count * owners, pair_c...  4.88 us
    ppermute x2, starting transfers between devices, local(): lax.ppermute(fields, 'lat', edges + [(j, i) for i, j in edges])  3.59 us
    pallas_call x1, Pallas kernels, local(): pl.pallas_call(functools.partial(legendre_kernel, level_owners, level_cou...  2.76 us
    ppermute x2, waiting for transfers between devices, local(): lax.ppermute(fields, 'lat', edges + [(j, i) for i, j in edges])  2.17 us
    pallas_call x1, Pallas kernels, local(): pl.pallas_call(far_kernel, out_shape=jax.ShapeDtypeStruct((owners, 2 * SU...  1.19 us
    ppermute x1, waiting for transfers between devices, local(): totals = lax.ppermute(total, 'lev', [(0, 1), (1, 0)])[None]  0.7 us
  transfers between devices with their start and end apart: 3, of which 2 were waited for; matrix products, arithmetic and copies ran while one was open for 0% of the time, Pallas kernels for 17%

profile of v14, /device:TPU:0, one launch (start us, length us, event | category | flops | bytes accessed | tf_op | source)
XLA Modules:
  0.0 31.1 jit_solution(2093586381948536343)
XLA Ops:
  0.0 2.9 %collective-permute-start.1 = (bf16[2,4,2,2816]{3,2,1,0:T(2,128)(2,1)}, bf16[2,4,2,2816]{3,2,1,0:T(2,128)(2,1)S(1)}, u32[]{:S(2)}, u32[]{:S(2)}) collective-permute-start(bf16[2,4,2,2816]{3,2,1,0:T(2,128)(2,1)} %fields_far.1), channel_id=1, source_target_pairs={{0,2},{4,6},{8,10},{12,14},{16,18},{20,22},{24,26},{28,30},{2,0},{... | collective-permute-start | bytes 270344 | tf_op jit(solution)/shard_map/ppermute | solution.py:470
  2.9 0.7 %collective-permute-start = (bf16[2,4,2,2816]{3,2,1,0:T(2,128)(2,1)}, bf16[2,4,2,2816]{3,2,1,0:T(2,128)(2,1)S(1)}, u32[]{:S(2)}, u32[]{:S(2)}) collective-permute-start(bf16[2,4,2,2816]{3,2,1,0:T(2,128)(2,1)} %fields_far.1), channel_id=1, source_target_pairs={{2,4},{6,8},{10,12},{14,16},{18,20},{22,24},{26,28},{4,2},{8,6},{1... | collective-permute-start | bytes 270344 | tf_op jit(solution)/shard_map/ppermute | solution.py:470
  3.6 2.2 %collective-permute-done.1.side_rows = bf16[2,4,2,2816]{3,2,1,0:T(2,128)(2,1)S(1)} collective-permute-done((bf16[2,4,2,2816]{3,2,1,0:T(2,128)(2,1)}, bf16[2,4,2,2816]{3,2,1,0:T(2,128)(2,1)S(1)}, u32[]{:S(2)}, u32[]{:S(2)}) %collective-permute-start.1) | collective-permute-done | bytes 90144 | tf_op jit(solution)/shard_map/ppermute | solution.py:470
  5.8 4.9 %near_rows.1 = (f32[2,11,8,256]{3,2,1,0:T(8,128)S(1)}, bf16[2,256,2560]{2,1,0:T(8,128)(2,1)S(1)}, f32[2,11,8,2560]{3,2,1,0:T(8,128)S(1)}, s16[2,2,11,2,16,128]{5...) custom-call(s32[2]{0:T(128)} %rows_first_far.1, s32[32]{0:T(128)} %points_far.1, ...), custom_call_target="tpu_custom_call" | custom-call | flops 10000000 | bytes 4000000 | tf_op jit(solution)/shard_map/near_rows/pallas_call | solution.py:476
  10.7 0.0 collective-permute-done.far_side
  10.7 0.0 copy-start.1
  10.7 0.0 copy-start
  10.7 1.2 %far_rows.1 = bf16[16,32,128]{2,1,0:T(8,128)(2,1)S(1)} custom-call(bf16[2,4,2,2816]{3,2,1,0:T(2,128)(2,1)S(1)} %collective-permute-done.far_side, s16[2,2,11,2,16,128]{5,4,3,2,1,0:T(8,128)(2,1)S(1)} %get-tuple-element.12.far_starts, f32[2,2,11,8,8,128]{5,4,3,2,1,0:T(8,128)S(1)} %get-tuple-element.13.far_scales, s32[8,128]{1,0:T(8,128)S(1)} %get-tuple-element.14.facts, ...), custom_call_target="tpu_custom_call" | custom-call | tf_op jit(solution)/shard_map/far_rows/pallas_call | solution.py:506
  11.9 14.9 %all_to_all.5.received = bf16[16,32,128]{2,1,0:T(8,128)(2,1)S(1)} all-to-all(bf16[16,32,128]{2,1,0:T(8,128)(2,1)S(1)} %far_rows.1), channel_id=1, replica_groups=mesh['lat'=16,'lev'=2] {'lat'}, dimensions={0} | all-to-all | bytes 262144 | tf_op jit(solution)/shard_map/all_to_all | solution.py:521
  26.8 0.1 fusion.1
  26.9 0.0 copy-done.1
  26.9 0.2 fusion
  27.1 0.1 collective-permute-start.2
  27.2 0.5 %left_rows.1.left_given = bf16[5,320,256]{2,1,0:T(8,128)(2,1)S(1)} custom-call(bf16[16,32,128]{2,1,0:T(8,128)(2,1)S(1)} %all_to_all.5.received), custom_call_target="tpu_custom_call" | custom-call | flops 50000000 | bytes 2000000 | tf_op jit(solution)/shard_map/left_rows/pallas_call | solution.py:536
  27.7 0.7 %collective-permute-done.2 = f32[2,32,128]{2,1,0:T(8,128)S(1)} collective-permute-done((f32[2,32,128]{2,1,0:T(8,128)S(1)}, f32[2,32,128]{2,1,0:T(8,128)S(1)}, u32[]{:S(2)}, u32[]{:S(2)}) %collective-permute-start.2) | collective-permute-done | bytes 32800 | tf_op jit(solution)/shard_map/ppermute | solution.py:527
  28.4 0.0 copy-done
  28.4 2.8 %degree_sums.1 = (bf16[2,5,2,40,1281]{4,3,2,1,0:T(8,128)(2,1)}, bf16[5,320,256]{2,1,0:T(8,128)(2,1)S(1)}) custom-call(f32[2]{0:T(128)S(1)} %copy-done.1, bf16[16,32,128]{2,1,0:T(8,128)(2,1)S(1)} %all_to_all.5.received, f32[1,2,32,128]{3,2,1,0:T(8,128)S(1)} %bitcast.13, bf16[40,32,1281]{2,1,0:T(8,128)(2,1)S(1)} %copy-done, ...), custom_call_target="tpu_custom_call", output_to_operand_aliasing={{1}: (4, {})} | custom-call | tf_op jit(solution)/shard_map/degree_sums/pallas_call | solution.py:546
  (1 shorter events, 0.0 us)
Async XLA Ops:
  0.0 5.8 %collective-permute-start.1 = (bf16[2,4,2,2816]{3,2,1,0:T(2,128)(2,1)}, bf16[2,4,2,2816]{3,2,1,0:T(2,128)(2,1)S(1)}, u32[]{:S(2)}, u32[]{:S(2)}) collective-permute-start(bf16[2,4,2,2816]{3,2,1,0:T(2,128)(2,1)} %fields_far.1), channel_id=1, source_target_pairs={{0,2},{4,6},{8,10},{12,14},{16,18},{20,22},{24,26},{28,30},{2,0},{... | collective-permute-start | bytes 270344 | tf_op jit(solution)/shard_map/ppermute | solution.py:470
  2.9 7.7 %collective-permute-start = (bf16[2,4,2,2816]{3,2,1,0:T(2,128)(2,1)}, bf16[2,4,2,2816]{3,2,1,0:T(2,128)(2,1)S(1)}, u32[]{:S(2)}, u32[]{:S(2)}) collective-permute-start(bf16[2,4,2,2816]{3,2,1,0:T(2,128)(2,1)} %fields_far.1), channel_id=1, source_target_pairs={{2,4},{6,8},{10,12},{14,16},{18,20},{22,24},{26,28},{4,2},{8,6},{1... | collective-permute-start | bytes 270344 | tf_op jit(solution)/shard_map/ppermute | solution.py:470
  10.7 16.2 %copy-start.1 = (f32[2]{0:T(128)S(1)}, f32[2]{0:T(128)}, u32[]{:S(2)}) copy-start(f32[2]{0:T(128)} %thickness.1) | copy-start | bytes 28
  10.7 17.7 %copy-start = (bf16[40,32,1281]{2,1,0:T(8,128)(2,1)S(1)}, bf16[40,32,1281]{2,1,0:T(8,128)(2,1)}, u32[]{:S(2)}) copy-start(bf16[40,32,1281]{2,1,0:T(8,128)(2,1)} %legendre.1) | copy-start | bytes 9838084
  27.1 1.3 %collective-permute-start.2 = (f32[2,32,128]{2,1,0:T(8,128)S(1)}, f32[2,32,128]{2,1,0:T(8,128)S(1)}, u32[]{:S(2)}, u32[]{:S(2)}) collective-permute-start(f32[2,32,128]{2,1,0:T(8,128)S(1)} %bitcast.16), channel_id=1, source_target_pairs={{0,1},{1,0},{2,3},{3,2},{4,5},{5,4},{6,7},{7,6},{8,9},{9,8},{10,11... | collective-permute-start | bytes 98312 | tf_op jit(solution)/shard_map/ppermute | solution.py:527

commit v15 on v13

--- a/solution.py
+++ b/solution.py
@@ -137,9 +137,9 @@
 
 
 def near_kernel(
-    pair_total, pair_count, rows_first_far, points_far, fields_far, starts_far, weights_far,
-    partial, table, twiddle, far_starts, far_scales, facts,
-    rows_first, points, fields, starts, weights, begins, factors, lines, ext, arrived,
+    pair_total, pair_count, rows_first_far, points_far, fields_far, starts_far, weights_far, side,
+    partial, table, twiddle, far_starts, far_scales, facts, beside,
+    rows_first, points, fields, starts, weights, begins, factors, lines, side_lines, ext, arrived,
 ):
     lat_count, couples = partial.shape[:2]
     lon = 2 * couples * LANES
@@ -159,6 +159,7 @@
     ]
     for fetch in fetches:
         fetch.start()
+    spread_lines(side, side_lines)
     fetches[0].wait()
     width = 256
     scales = []
@@ -201,6 +202,10 @@
             place = jnp.clip(first_lat + place, 0, points.shape[0] - 1)
             known.append(lon - points[place])
     facts[...] = jnp.concatenate([jnp.full((1, LANES), one, jnp.int32) for one in known], axis=0)
+    upper = lax.axis_index("lat") % 2 == 0
+    for row in range(lat_count):
+        missing = jnp.where(upper, known[3 * lat_count + row], known[2 * lat_count + row])
+        extend(side_lines, row, lat_count, missing, beside, row)
     spread_rows(starts, begins)
     spread_lines(weights, factors)
     spread_lines(fields, lines)
@@ -242,19 +247,19 @@
 
 
 def far_kernel(
-    near_side, far_side, far_starts, far_scales, facts, partial, table, twiddle,
+    beside, far_side, far_starts, far_scales, facts, partial, table, twiddle,
     out, lines, ext, grid, waves,
 ):
     lat_count, couples = partial.shape[:2]
     columns = table.shape[2] // 2
     owners = out.shape[0]
+    fact = [jnp.broadcast_to(facts[row : row + 1], (SUB, LANES)) for row in range(4 * lat_count)]
     toward = 1 - lax.axis_index("lat") % 2
-    spread_lines(near_side, lines.at[toward])
-    spread_lines(far_side, lines.at[1 - toward])
-    fact = [jnp.broadcast_to(facts[row : row + 1], (SUB, LANES)) for row in range(4 * lat_count)]
-    for slot in range(2 * lat_count):
-        side, row = divmod(slot, lat_count)
-        extend(lines.at[side], row, lat_count, fact[2 * lat_count + slot], ext, slot)
+    ext[pl.ds(toward * lat_count, lat_count)] = beside[...]
+    spread_lines(far_side, lines)
+    for row in range(lat_count):
+        missing = jnp.where(toward == 1, fact[2 * lat_count + row], fact[3 * lat_count + row])
+        extend(lines, row, lat_count, missing, ext, (1 - toward) * lat_count + row)
     lane = lax.broadcasted_iota(jnp.int32, (SUB, LANES), 1)
     width = 256
     choices = ((2, 1, 0), (3, 2, 1))
@@ -395,7 +400,9 @@
             sums[level, field_count, part] = running
     place_rows(sums, keys, pair_count, left)
     copies = []
-    for start in range(0, degrees, 256):
+    starts = list(range(0, degrees, 256))
+    starts = starts[-1:] + starts[:-1]
+    for start in starts:
         stop = min(start + 256, degrees)
         low = 0 if start < 2 * pair_total else half
         high = 2 * half if stop > pair_total + 1 else half
@@ -418,7 +425,10 @@
         planes[:, :, :, :, start:stop] = (
             jnp.concatenate(parts, axis=1).astype(jnp.bfloat16).reshape(planes.shape[:4] + (stop - start,))
         )
-        here = pl.ds(start, stop - start)
+        if start == starts[0]:
+            continue
+        end = degrees if start == starts[-1] else stop
+        here = pl.ds(start, end - start)
         copies.append(
             pltpu.make_async_copy(
                 planes.at[:, :, :, :, here], out.at[:, :, :, :, here], sent.at[len(copies)]
@@ -449,7 +459,7 @@
     vector = pl.BlockSpec(memory_space=pltpu.VMEM)
     params = pltpu.CompilerParams(vmem_limit_bytes=LIMIT)
     remote = pl.BlockSpec(memory_space=pltpu.HBM)
-    partial, table, twiddle, far_starts, far_scales, facts = pl.pallas_call(
+    partial, table, twiddle, far_starts, far_scales, facts, beside = pl.pallas_call(
         functools.partial(near_kernel, pair_count * owners, pair_count),
         out_shape=(
             jax.ShapeDtypeStruct((lat_count, couples, SUB, 2 * LANES), jnp.float32),
@@ -458,9 +468,10 @@
             jax.ShapeDtypeStruct((lat_count, 2, couples, 2, 2 * SUB, LANES), jnp.int16),
             jax.ShapeDtypeStruct((lat_count, 2, couples, SUB, SUB, LANES), jnp.float32),
             jax.ShapeDtypeStruct((4 * lat_count, LANES), jnp.int32),
+            jax.ShapeDtypeStruct((lat_count, blocks + 2, 2 * SUB, LANES), jnp.bfloat16),
         ),
-        in_specs=[remote] * 5,
-        out_specs=(vector,) * 6,
+        in_specs=[remote] * 5 + [vector],
+        out_specs=(vector,) * 7,
         scratch_shapes=[
             pltpu.SMEM(rows_first.shape, jnp.int32),
             pltpu.SMEM(points.shape, jnp.int32),
@@ -470,13 +481,14 @@
             pltpu.VMEM((lat_count, STENCIL, blocks, 1, LANES), jnp.int32),
             pltpu.VMEM((weights.size // LANES, LANES), jnp.float32),
             pltpu.VMEM((fields.size // LANES, LANES), jnp.float32),
+            pltpu.VMEM((fields.size // LANES, LANES), jnp.float32),
             pltpu.VMEM((lat_count, blocks + 2, 2 * SUB, LANES), jnp.bfloat16),
             pltpu.SemaphoreType.DMA((5,)),
         ],
         compiler_params=params,
         cost_estimate=pl.CostEstimate(flops=10_000_000, bytes_accessed=4_000_000, transcendentals=0),
         name="near_rows",
-    )(*(held(value) for value in (rows_first, points, fields, starts, weights)))
+    )(*(held(value) for value in (rows_first, points, fields, starts, weights)), sides[0])
 
     coefficients = pl.pallas_call(
         far_kernel,
@@ -484,14 +496,14 @@
         in_specs=[vector] * 8,
         out_specs=vector,
         scratch_shapes=[
-            pltpu.VMEM((2, fields.size // LANES, LANES), jnp.float32),
+            pltpu.VMEM((fields.size // LANES, LANES), jnp.float32),
             pltpu.VMEM((2 * lat_count, blocks + 2, 2 * SUB, LANES), jnp.bfloat16),
             pltpu.VMEM((lat_count, couples, SUB, 2 * LANES), jnp.float32),
             pltpu.VMEM((lat_count, 2 * SUB, columns + LANES), jnp.float32),
         ],
         compiler_params=params,
         name="far_rows",
-    )(*sides, far_starts, far_scales, facts, partial, table, twiddle)
+    )(beside, sides[1], far_starts, far_scales, facts, partial, table, twiddle)
 
     received = lax.all_to_all(coefficients, "lat", split_axis=0, concat_axis=0, tiled=True)
     by_level = received.reshape(lat_total, 2, level_count, field_count, LANES).astype(jnp.float32)

time: 30.4 us -> 30.6 us (level)
  waiting for transfers between devices: 0.71 us -> 2.87 us
  blocking collectives: 17 us -> 14.9 us
    ppermute x2, waiting for transfers between devices: 0.01 us -> 2.17 us  [local(): lax.ppermute(fields, 'lat', edges + [(j, i) for i, j in edges])]
    all_to_all x1, blocking collectives: 17 us -> 14.9 us  [local(): lax.all_to_all(coefficients, 'lat', split_axis=0, concat_axis=0, tiled=True)]
  transfers between devices with their start and end apart: 3 -> 3, of which waited for: 1 -> 2; matrix products, arithmetic and copies ran while one was open for 0% -> 0% of each run, Pallas kernels for 13% -> 13%
where the time goes in v15:
time: 30.6 us; the launch traced here: 30.4 us
  blocking collectives  14.9 us (49%)
  Pallas kernels  8.56 us (28%)
  starting transfers between devices  3.66 us (12%)
  waiting for transfers between devices  2.87 us (9%)
    all_to_all x1, blocking collectives, local(): lax.all_to_all(coefficients, 'lat', split_axis=0, concat_axis=0, tiled=True)  14.9 us
    ppermute x2, starting transfers between devices, local(): lax.ppermute(fields, 'lat', edges + [(j, i) for i, j in edges])  3.59 us
    pallas_call x1, Pallas kernels, local(): pl.pallas_call(functools.partial(near_kernel, pair_count * owners, pair_c...  3.34 us
    pallas_call x1, Pallas kernels, local(): pl.pallas_call(functools.partial(legendre_kernel, level_owners, level_cou...  2.82 us
    ppermute x2, waiting for transfers between devices, local(): lax.ppermute(fields, 'lat', edges + [(j, i) for i, j in edges])  2.17 us
    pallas_call x1, Pallas kernels, local(): pl.pallas_call(far_kernel, out_shape=jax.ShapeDtypeStruct((owners, 2 * SU...  1.92 us
    ppermute x1, waiting for transfers between devices, local(): totals = lax.ppermute(total, 'lev', [(0, 1), (1, 0)])[None]  0.7 us
  transfers between devices with their start and end apart: 3, of which 2 were waited for; matrix products, arithmetic and copies ran while one was open for 0% of the time, Pallas kernels for 13%

profile of v15, /device:TPU:0, one launch (start us, length us, event | category | flops | bytes accessed | tf_op | source)
XLA Modules:
  0.0 30.4 jit_solution(3397907855151887074)
XLA Ops:
  0.0 2.9 %collective-permute-start = (bf16[2,4,2,2816]{3,2,1,0:T(2,128)(2,1)}, bf16[2,4,2,2816]{3,2,1,0:T(2,128)(2,1)S(1)}, u32[]{:S(2)}, u32[]{:S(2)}) collective-permute-start(bf16[2,4,2,2816]{3,2,1,0:T(2,128)(2,1)} %fields_far.1), channel_id=1, source_target_pairs={{0,2},{4,6},{8,10},{12,14},{16,18},{20,22},{24,26},{28,30},{2,0},{... | collective-permute-start | bytes 270344 | tf_op jit(solution)/shard_map/ppermute | solution.py:456
  2.9 0.7 %collective-permute-start.1 = (bf16[2,4,2,2816]{3,2,1,0:T(2,128)(2,1)}, bf16[2,4,2,2816]{3,2,1,0:T(2,128)(2,1)S(1)}, u32[]{:S(2)}, u32[]{:S(2)}) collective-permute-start(bf16[2,4,2,2816]{3,2,1,0:T(2,128)(2,1)} %fields_far.1), channel_id=1, source_target_pairs={{2,4},{6,8},{10,12},{14,16},{18,20},{22,24},{26,28},{4,2},{8,6},{1... | collective-permute-start | bytes 270344 | tf_op jit(solution)/shard_map/ppermute | solution.py:456
  3.6 2.2 %collective-permute-done.side = bf16[2,4,2,2816]{3,2,1,0:T(2,128)(2,1)S(1)} collective-permute-done((bf16[2,4,2,2816]{3,2,1,0:T(2,128)(2,1)}, bf16[2,4,2,2816]{3,2,1,0:T(2,128)(2,1)S(1)}, u32[]{:S(2)}, u32[]{:S(2)}) %collective-permute-start) | collective-permute-done | bytes 90144 | tf_op jit(solution)/shard_map/ppermute | solution.py:456
  5.8 3.3 %near_rows.1 = (f32[2,11,8,256]{3,2,1,0:T(8,128)S(1)}, bf16[2,256,2560]{2,1,0:T(8,128)(2,1)S(1)}, f32[2,11,8,2560]{3,2,1,0:T(8,128)S(1)}, s16[2,2,11,2,16,128]{5...) custom-call(s32[2]{0:T(128)} %rows_first_far.1, ...), custom_call_target="tpu_custom_call" | custom-call | flops 10000000 | bytes 4000000 | tf_op jit(solution)/shard_map/near_rows/pallas_call | solution.py:462
  9.1 0.0 collective-permute-done.1.far_side
  9.1 0.0 copy-start.1
  9.1 0.0 copy-start
  9.1 1.9 %far_rows.1 = bf16[16,32,128]{2,1,0:T(8,128)(2,1)S(1)} custom-call(bf16[2,24,16,128]{3,2,1,0:T(8,128)(2,1)S(1)} %get-tuple-element.13.beside, bf16[2,4,2,2816]{3,2,1,0:T(2,128)(2,1)S(1)} %collective-permute-done.1.far_side, s16[2,2,11,2,16,128]{5,4,3,2,1,0:T(8,128)(2,1)S(1)} %get-tuple-element.14.far_starts, ...), custom_call_target="tpu_custom_call" | custom-call | tf_op jit(solution)/shard_map/far_rows/pallas_call | solution.py:493
  11.1 14.9 %all_to_all.5.received = bf16[16,32,128]{2,1,0:T(8,128)(2,1)S(1)} all-to-all(bf16[16,32,128]{2,1,0:T(8,128)(2,1)S(1)} %far_rows.1), channel_id=1, replica_groups=mesh['lat'=16,'lev'=2] {'lat'}, dimensions={0} | all-to-all | bytes 262144 | tf_op jit(solution)/shard_map/all_to_all | solution.py:508
  26.0 0.1 fusion.1
  26.1 0.0 copy-done.1
  26.1 0.2 fusion
  26.3 0.1 collective-permute-start.2
  26.3 0.5 %left_rows.1.left_given = bf16[5,320,256]{2,1,0:T(8,128)(2,1)S(1)} custom-call(bf16[16,32,128]{2,1,0:T(8,128)(2,1)S(1)} %all_to_all.5.received), custom_call_target="tpu_custom_call" | custom-call | flops 50000000 | bytes 2000000 | tf_op jit(solution)/shard_map/left_rows/pallas_call | solution.py:523
  26.8 0.7 %collective-permute-done.2 = f32[2,32,128]{2,1,0:T(8,128)S(1)} collective-permute-done((f32[2,32,128]{2,1,0:T(8,128)S(1)}, f32[2,32,128]{2,1,0:T(8,128)S(1)}, u32[]{:S(2)}, u32[]{:S(2)}) %collective-permute-start.2) | collective-permute-done | bytes 32800 | tf_op jit(solution)/shard_map/ppermute | solution.py:514
  27.5 0.0 copy-done
  27.5 2.8 %degree_sums.1 = (bf16[2,5,2,40,1281]{4,3,2,1,0:T(8,128)(2,1)}, bf16[5,320,256]{2,1,0:T(8,128)(2,1)S(1)}) custom-call(f32[2]{0:T(128)S(1)} %copy-done.1, bf16[16,32,128]{2,1,0:T(8,128)(2,1)S(1)} %all_to_all.5.received, f32[1,2,32,128]{3,2,1,0:T(8,128)S(1)} %bitcast.13, bf16[40,32,1281]{2,1,0:T(8,128)(2,1)S(1)} %copy-done, ...), custom_call_target="tpu_custom_call", output_to_operand_aliasing={{1}: (4, {})} | custom-call | tf_op jit(solution)/shard_map/degree_sums/pallas_call | solution.py:533
  (1 shorter events, 0.0 us)
Async XLA Ops:
  0.0 5.8 %collective-permute-start = (bf16[2,4,2,2816]{3,2,1,0:T(2,128)(2,1)}, bf16[2,4,2,2816]{3,2,1,0:T(2,128)(2,1)S(1)}, u32[]{:S(2)}, u32[]{:S(2)}) collective-permute-start(bf16[2,4,2,2816]{3,2,1,0:T(2,128)(2,1)} %fields_far.1), channel_id=1, source_target_pairs={{0,2},{4,6},{8,10},{12,14},{16,18},{20,22},{24,26},{28,30},{2,0},{... | collective-permute-start | bytes 270344 | tf_op jit(solution)/shard_map/ppermute | solution.py:456
  2.9 6.2 %collective-permute-start.1 = (bf16[2,4,2,2816]{3,2,1,0:T(2,128)(2,1)}, bf16[2,4,2,2816]{3,2,1,0:T(2,128)(2,1)S(1)}, u32[]{:S(2)}, u32[]{:S(2)}) collective-permute-start(bf16[2,4,2,2816]{3,2,1,0:T(2,128)(2,1)} %fields_far.1), channel_id=1, source_target_pairs={{2,4},{6,8},{10,12},{14,16},{18,20},{22,24},{26,28},{4,2},{8,6},{1... | collective-permute-start | bytes 270344 | tf_op jit(solution)/shard_map/ppermute | solution.py:456
  9.1 17.0 %copy-start.1 = (f32[2]{0:T(128)S(1)}, f32[2]{0:T(128)}, u32[]{:S(2)}) copy-start(f32[2]{0:T(128)} %thickness.1) | copy-start | bytes 28
  9.1 18.4 %copy-start = (bf16[40,32,1281]{2,1,0:T(8,128)(2,1)S(1)}, bf16[40,32,1281]{2,1,0:T(8,128)(2,1)}, u32[]{:S(2)}) copy-start(bf16[40,32,1281]{2,1,0:T(8,128)(2,1)} %legendre.1) | copy-start | bytes 9838084
  26.3 1.3 %collective-permute-start.2 = (f32[2,32,128]{2,1,0:T(8,128)S(1)}, f32[2,32,128]{2,1,0:T(8,128)S(1)}, u32[]{:S(2)}, u32[]{:S(2)}) collective-permute-start(f32[2,32,128]{2,1,0:T(8,128)S(1)} %bitcast.16), channel_id=1, source_target_pairs={{0,1},{1,0},{2,3},{3,2},{4,5},{5,4},{6,7},{7,6},{8,9},{9,8},{10,11... | collective-permute-start | bytes 98312 | tf_op jit(solution)/shard_map/ppermute | solution.py:514

commit v16 on v13

--- a/solution.py
+++ b/solution.py
@@ -248,7 +248,7 @@
     lat_count, couples = partial.shape[:2]
     columns = table.shape[2] // 2
     owners = out.shape[0]
-    toward = 1 - lax.axis_index("lat") % 2
+    toward = 1 - (lax.axis_index("lat") + lax.axis_index("lev")) % 2
     spread_lines(near_side, lines.at[toward])
     spread_lines(far_side, lines.at[1 - toward])
     fact = [jnp.broadcast_to(facts[row : row + 1], (SUB, LANES)) for row in range(4 * lat_count)]
@@ -440,10 +440,15 @@
     couples = lon_count // (2 * LANES)
     blocks = 2 * couples
     columns = 2 * owners * pair_count
+    level_owners = lax.axis_size("lev")
     sides = []
     for first in range(2):
-        edges = [(i, i + 1) for i in range(first, owners - 1, 2)]
-        sides.append(lax.ppermute(fields, "lat", edges + [(j, i) for i, j in edges]))
+        edges = [
+            (i * level_owners + place, (i + 1) * level_owners + place)
+            for place in range(level_owners)
+            for i in range((first + place) % 2, owners - 1, 2)
+        ]
+        sides.append(lax.ppermute(fields, ("lat", "lev"), edges + [(j, i) for i, j in edges]))
 
     scalar = pl.BlockSpec(memory_space=pltpu.SMEM)
     vector = pl.BlockSpec(memory_space=pltpu.VMEM)
@@ -497,7 +502,6 @@
     by_level = received.reshape(lat_total, 2, level_count, field_count, LANES).astype(jnp.float32)
     virtual = by_level[:, :, :, 2] + 0.61 * by_level[:, :, :, 3]
     total = jnp.sum(thickness[None, None, :, None] * virtual, axis=2).transpose(1, 0, 2)
-    level_owners = lax.axis_size("lev")
     if level_owners == 2:
         totals = lax.ppermute(total, "lev", [(0, 1), (1, 0)])[None]
     else:

time: 30.4 us -> 32.3 us (1.062)
  starting transfers between devices: 3.66 us -> 5.57 us
    ppermute x2, starting transfers between devices: 3.59 us -> 5.5 us  [local(): lax.ppermute(fields, ('lat', 'lev'), edges + [(j, i) for i, j in edges])]
  transfers between devices with their start and end apart: 3 -> 3, of which waited for: 1 -> 1; matrix products, arithmetic and copies ran while one was open for 0% -> 0% of each run, Pallas kernels for 13% -> 12%
where the time goes in v16:
time: 32.3 us; the launch traced here: 32.1 us
  blocking collectives  17 us (53%)
  Pallas kernels  8.45 us (26%)
  starting transfers between devices  5.57 us (17%)
  waiting for transfers between devices  0.71 us (2%)
    all_to_all x1, blocking collectives, local(): lax.all_to_all(coefficients, 'lat', split_axis=0, concat_axis=0, tiled=True)  17 us
    ppermute x2, starting transfers between devices, local(): lax.ppermute(fields, ('lat', 'lev'), edges + [(j, i) for i, j in edges])  5.5 us
    pallas_call x1, Pallas kernels, local(): pl.pallas_call(functools.partial(near_kernel, pair_count * owners, pair_c...  3.33 us
    pallas_call x1, Pallas kernels, local(): pl.pallas_call(functools.partial(legendre_kernel, level_owners, level_cou...  2.76 us
    pallas_call x1, Pallas kernels, local(): pl.pallas_call(far_kernel, out_shape=jax.ShapeDtypeStruct((owners, 2 * SU...  1.88 us
    ppermute x1, waiting for transfers between devices, local(): totals = lax.ppermute(total, 'lev', [(0, 1), (1, 0)])[None]  0.7 us
  transfers between devices with their start and end apart: 3, of which 1 were waited for; matrix products, arithmetic and copies ran while one was open for 0% of the time, Pallas kernels for 12%

profile of v16, /device:TPU:0, one launch (start us, length us, event | category | flops | bytes accessed | tf_op | source)
XLA Modules:
  0.0 32.1 jit_solution(4543917106966621503)
XLA Ops:
  0.0 4.8 %collective-permute-start = (bf16[2,4,2,2816]{3,2,1,0:T(2,128)(2,1)}, bf16[2,4,2,2816]{3,2,1,0:T(2,128)(2,1)S(1)}, u32[]{:S(2)}, u32[]{:S(2)}) collective-permute-start(bf16[2,4,2,2816]{3,2,1,0:T(2,128)(2,1)} %fields_far.1), channel_id=1, source_target_pairs={{0,2},{4,6},{8,10},{12,14},{16,18},{20,22},{24,26},{28,30},{3,5},{... | collective-permute-start | bytes 270344 | tf_op jit(solution)/shard_map/ppermute | solution.py:451
  4.8 0.7 %collective-permute-start.1 = (bf16[2,4,2,2816]{3,2,1,0:T(2,128)(2,1)}, bf16[2,4,2,2816]{3,2,1,0:T(2,128)(2,1)S(1)}, u32[]{:S(2)}, u32[]{:S(2)}) collective-permute-start(bf16[2,4,2,2816]{3,2,1,0:T(2,128)(2,1)} %fields_far.1), channel_id=1, source_target_pairs={{2,4},{6,8},{10,12},{14,16},{18,20},{22,24},{26,28},{1,3},{5,7},{9... | collective-permute-start | bytes 270344 | tf_op jit(solution)/shard_map/ppermute | solution.py:451
  5.5 3.3 %near_rows.1 = (f32[2,11,8,256]{3,2,1,0:T(8,128)S(1)}, bf16[2,256,2560]{2,1,0:T(8,128)(2,1)S(1)}, f32[2,11,8,2560]{3,2,1,0:T(8,128)S(1)}, s16[2,2,11,2,16,128]{5...) custom-call(s32[2]{0:T(128)} %rows_first_far.1, s32[32]{0:T(128)} %points_far.1, ...), custom_call_target="tpu_custom_call" | custom-call | flops 10000000 | bytes 4000000 | tf_op jit(solution)/shard_map/near_rows/pallas_call | solution.py:457
  8.9 0.0 collective-permute-done.near_side
  8.9 0.0 collective-permute-done.1.far_side
  8.9 0.0 copy-start.1
  8.9 0.0 copy-start
  8.9 1.9 %far_rows.1 = bf16[16,32,128]{2,1,0:T(8,128)(2,1)S(1)} custom-call(bf16[2,4,2,2816]{3,2,1,0:T(2,128)(2,1)S(1)} %collective-permute-done.near_side, bf16[2,4,2,2816]{3,2,1,0:T(2,128)(2,1)S(1)} %collective-permute-done.1.far_side, s16[2,2,11,2,16,128]{5,4,3,2,1,0:T(8,128)(2,1)S(1)} %get-tuple-element.12.far_starts, ...), custom_call_target="tpu_custom_call" | custom-call | tf_op jit(solution)/shard_map/far_rows/pallas_call | solution.py:486
  10.8 17.0 %all_to_all.5.received = bf16[16,32,128]{2,1,0:T(8,128)(2,1)S(1)} all-to-all(bf16[16,32,128]{2,1,0:T(8,128)(2,1)S(1)} %far_rows.1), channel_id=1, replica_groups=mesh['lat'=16,'lev'=2] {'lat'}, dimensions={0} | all-to-all | bytes 262144 | tf_op jit(solution)/shard_map/all_to_all | solution.py:501
  27.8 0.1 fusion.1
  27.9 0.0 copy-done.1
  27.9 0.2 fusion
  28.1 0.1 collective-permute-start.2
  28.2 0.5 %left_rows.1.left_given = bf16[5,320,256]{2,1,0:T(8,128)(2,1)S(1)} custom-call(bf16[16,32,128]{2,1,0:T(8,128)(2,1)S(1)} %all_to_all.5.received), custom_call_target="tpu_custom_call" | custom-call | flops 50000000 | bytes 2000000 | tf_op jit(solution)/shard_map/left_rows/pallas_call | solution.py:515
  28.7 0.7 %collective-permute-done.2 = f32[2,32,128]{2,1,0:T(8,128)S(1)} collective-permute-done((f32[2,32,128]{2,1,0:T(8,128)S(1)}, f32[2,32,128]{2,1,0:T(8,128)S(1)}, u32[]{:S(2)}, u32[]{:S(2)}) %collective-permute-start.2) | collective-permute-done | bytes 32800 | tf_op jit(solution)/shard_map/ppermute | solution.py:506
  29.4 0.0 copy-done
  29.4 2.8 %degree_sums.1 = (bf16[2,5,2,40,1281]{4,3,2,1,0:T(8,128)(2,1)}, bf16[5,320,256]{2,1,0:T(8,128)(2,1)S(1)}) custom-call(f32[2]{0:T(128)S(1)} %copy-done.1, bf16[16,32,128]{2,1,0:T(8,128)(2,1)S(1)} %all_to_all.5.received, f32[1,2,32,128]{3,2,1,0:T(8,128)S(1)} %bitcast.13, bf16[40,32,1281]{2,1,0:T(8,128)(2,1)S(1)} %copy-done, ...), custom_call_target="tpu_custom_call", output_to_operand_aliasing={{1}: (4, {})} | custom-call | tf_op jit(solution)/shard_map/degree_sums/pallas_call | solution.py:525
  (1 shorter events, 0.0 us)
Async XLA Ops:
  0.0 8.9 %collective-permute-start = (bf16[2,4,2,2816]{3,2,1,0:T(2,128)(2,1)}, bf16[2,4,2,2816]{3,2,1,0:T(2,128)(2,1)S(1)}, u32[]{:S(2)}, u32[]{:S(2)}) collective-permute-start(bf16[2,4,2,2816]{3,2,1,0:T(2,128)(2,1)} %fields_far.1), channel_id=1, source_target_pairs={{0,2},{4,6},{8,10},{12,14},{16,18},{20,22},{24,26},{28,30},{3,5},{... | collective-permute-start | bytes 270344 | tf_op jit(solution)/shard_map/ppermute | solution.py:451
  4.8 4.0 %collective-permute-start.1 = (bf16[2,4,2,2816]{3,2,1,0:T(2,128)(2,1)}, bf16[2,4,2,2816]{3,2,1,0:T(2,128)(2,1)S(1)}, u32[]{:S(2)}, u32[]{:S(2)}) collective-permute-start(bf16[2,4,2,2816]{3,2,1,0:T(2,128)(2,1)} %fields_far.1), channel_id=1, source_target_pairs={{2,4},{6,8},{10,12},{14,16},{18,20},{22,24},{26,28},{1,3},{5,7},{9... | collective-permute-start | bytes 270344 | tf_op jit(solution)/shard_map/ppermute | solution.py:451
  8.9 19.0 %copy-start.1 = (f32[2]{0:T(128)S(1)}, f32[2]{0:T(128)}, u32[]{:S(2)}) copy-start(f32[2]{0:T(128)} %thickness.1) | copy-start | bytes 28
  8.9 20.5 %copy-start = (bf16[40,32,1281]{2,1,0:T(8,128)(2,1)S(1)}, bf16[40,32,1281]{2,1,0:T(8,128)(2,1)}, u32[]{:S(2)}) copy-start(bf16[40,32,1281]{2,1,0:T(8,128)(2,1)} %legendre.1) | copy-start | bytes 9838084
  28.1 1.3 %collective-permute-start.2 = (f32[2,32,128]{2,1,0:T(8,128)S(1)}, f32[2,32,128]{2,1,0:T(8,128)S(1)}, u32[]{:S(2)}, u32[]{:S(2)}) collective-permute-start(f32[2,32,128]{2,1,0:T(8,128)S(1)} %bitcast.16), channel_id=1, source_target_pairs={{0,1},{1,0},{2,3},{3,2},{4,5},{5,4},{6,7},{7,6},{8,9},{9,8},{10,11... | collective-permute-start | bytes 98312 | tf_op jit(solution)/shard_map/ppermute | solution.py:506

commit v17 on v13

--- a/solution.py
+++ b/solution.py
@@ -362,17 +362,26 @@
     }
 
 
-def left_kernel(level_count, field_count, pair_count, received, left, wide):
+def left_kernel(
+    level_count, field_count, pair_count, thickness, received, left, base, wide,
+):
     keys = row_keys(level_count, field_count)
     wanted = [key for key in keys if key[1] < field_count]
-    place_rows(received_rows(received, wide, wanted, field_count), keys, pair_count, left)
+    lines = received_rows(received, wide, wanted, field_count)
+    place_rows(lines, keys, pair_count, left)
+    for part in range(2):
+        running = jnp.zeros(base.shape[1:], jnp.float32)
+        for level in reversed(range(level_count)):
+            running = running + thickness[level] * (
+                lines[level, 2, part] + 0.61 * lines[level, 3, part]
+            )
+            base[2 * level + part] = running
 
 
 def legendre_kernel(
-    level_owners, level_count, field_count, thickness, received, totals, legendre, left_given,
-    out, left, wide, planes, sent,
+    level_owners, level_count, field_count, owners, base, totals, legendre, left_given,
+    out, left, planes, sent,
 ):
-    owners = received.shape[0]
     pair_count, lat_total, degrees = legendre.shape
     pair_total = pair_count * owners
     groups = [(at, min(SUB, pair_count - at)) for at in range(0, pair_count, SUB)]
@@ -380,19 +389,14 @@
     half = len(keys) * SUB
     level_place = lax.axis_index("lev")
     first_pair = lax.axis_index("lat") * pair_count
-    wanted = [(level, field, part) for level in range(level_count) for field in (2, 3) for part in range(2)]
-    lines = received_rows(received, wide, wanted, field_count)
     sums = {}
     for part in range(2):
-        running = jnp.zeros((lat_total, LANES), jnp.float32)
+        deeper = jnp.zeros((lat_total, LANES), jnp.float32)
         for place in range(totals.shape[0]):
             other = 1 - level_place if level_owners == 2 else place
-            running = running + jnp.where(other > level_place, totals[place, part], 0.0)
-        for level in reversed(range(level_count)):
-            running = running + thickness[level] * (
-                lines[level, 2, part] + 0.61 * lines[level, 3, part]
-            )
-            sums[level, field_count, part] = running
+            deeper = deeper + jnp.where(other > level_place, totals[place, part], 0.0)
+        for level in range(level_count):
+            sums[level, field_count, part] = base[2 * level + part] + deeper
     place_rows(sums, keys, pair_count, left)
     copies = []
     for start in range(0, degrees, 256):
@@ -508,30 +512,32 @@
     group_count = (pair_count + SUB - 1) // SUB
     left_shape = jax.ShapeDtypeStruct((group_count, 2 * half, SUB * lat_total), jnp.bfloat16)
     wide = pltpu.VMEM((lat_total * 2 * SUB, LANES), jnp.float32)
-    left = pl.pallas_call(
+    left, base = pl.pallas_call(
         functools.partial(left_kernel, level_count, field_count, pair_count),
-        out_shape=left_shape,
-        in_specs=[vector],
-        out_specs=vector,
+        out_shape=(
+            left_shape,
+            jax.ShapeDtypeStruct((2 * level_count, lat_total, LANES), jnp.float32),
+        ),
+        in_specs=[scalar, vector],
+        out_specs=(vector, vector),
         scratch_shapes=[wide],
         compiler_params=params,
         cost_estimate=pl.CostEstimate(flops=50_000_000, bytes_accessed=2_000_000, transcendentals=0),
         name="left_rows",
-    )(received)
+    )(thickness, received)
     return pl.pallas_call(
-        functools.partial(legendre_kernel, level_owners, level_count, field_count),
+        functools.partial(legendre_kernel, level_owners, level_count, field_count, owners),
         out_shape=(jax.ShapeDtypeStruct(out_shape, jnp.bfloat16), left_shape),
-        in_specs=[scalar, vector, vector, vector, vector],
+        in_specs=[vector, vector, vector, vector],
         out_specs=(pl.BlockSpec(memory_space=pl.ANY), vector),
-        input_output_aliases={4: 1},
+        input_output_aliases={3: 1},
         scratch_shapes=[
-            wide,
             pltpu.VMEM(out_shape, jnp.bfloat16),
             pltpu.SemaphoreType.DMA(((degrees + 255) // 256,)),
         ],
         compiler_params=params,
         name="degree_sums",
-    )(thickness, received, totals, legendre, left)[0]
+    )(base, totals, legendre, left)[0]
 
 
 def solution(mesh):

time: 30.4 us -> 29.8 us (0.980)
  waiting for transfers between devices: 0.71 us -> 0.16 us
    pallas_call x1, Pallas kernels: 2.76 us -> 2.19 us  [local(): pl.pallas_call(functools.partial(legendre_kernel, level_owners, level_cou...]
    pallas_call x1, Pallas kernels: 0.49 us -> 1.03 us  [local(): pl.pallas_call(functools.partial(left_kernel, level_count, field_count, p...]
    ppermute x1, waiting for transfers between devices: 0.7 us -> 0.16 us  [local(): totals = lax.ppermute(total, 'lev', [(0, 1), (1, 0)])[None]]
  transfers between devices with their start and end apart: 3 -> 3, of which waited for: 1 -> 1; matrix products, arithmetic and copies ran while one was open for 0% -> 0% of each run, Pallas kernels for 13% -> 15%
where the time goes in v17:
time: 29.8 us; the launch traced here: 29.6 us
  blocking collectives  17 us (57%)
  Pallas kernels  8.43 us (28%)
  starting transfers between devices  3.66 us (12%)
    all_to_all x1, blocking collectives, local(): lax.all_to_all(coefficients, 'lat', split_axis=0, concat_axis=0, tiled=True)  17 us
    ppermute x2, starting transfers between devices, local(): lax.ppermute(fields, 'lat', edges + [(j, i) for i, j in edges])  3.59 us
    pallas_call x1, Pallas kernels, local(): pl.pallas_call(functools.partial(near_kernel, pair_count * owners, pair_c...  3.33 us
    pallas_call x1, Pallas kernels, local(): pl.pallas_call(functools.partial(legendre_kernel, level_owners, level_cou...  2.19 us
    pallas_call x1, Pallas kernels, local(): pl.pallas_call(far_kernel, out_shape=jax.ShapeDtypeStruct((owners, 2 * SU...  1.88 us
    pallas_call x1, Pallas kernels, local(): pl.pallas_call(functools.partial(left_kernel, level_count, field_count, p...  1.03 us
  transfers between devices with their start and end apart: 3, of which 1 were waited for; matrix products, arithmetic and copies ran while one was open for 0% of the time, Pallas kernels for 15%

profile of v17, /device:TPU:0, one launch (start us, length us, event | category | flops | bytes accessed | tf_op | source)
XLA Modules:
  0.0 29.6 jit_solution(16110158493085632665)
XLA Ops:
  0.0 2.9 %collective-permute-start = (bf16[2,4,2,2816]{3,2,1,0:T(2,128)(2,1)}, bf16[2,4,2,2816]{3,2,1,0:T(2,128)(2,1)S(1)}, u32[]{:S(2)}, u32[]{:S(2)}) collective-permute-start(bf16[2,4,2,2816]{3,2,1,0:T(2,128)(2,1)} %fields_far.1), channel_id=1, source_target_pairs={{0,2},{4,6},{8,10},{12,14},{16,18},{20,22},{24,26},{28,30},{2,0},{... | collective-permute-start | bytes 270344 | tf_op jit(solution)/shard_map/ppermute | solution.py:450
  2.9 0.7 %collective-permute-start.1 = (bf16[2,4,2,2816]{3,2,1,0:T(2,128)(2,1)}, bf16[2,4,2,2816]{3,2,1,0:T(2,128)(2,1)S(1)}, u32[]{:S(2)}, u32[]{:S(2)}) collective-permute-start(bf16[2,4,2,2816]{3,2,1,0:T(2,128)(2,1)} %fields_far.1), channel_id=1, source_target_pairs={{2,4},{6,8},{10,12},{14,16},{18,20},{22,24},{26,28},{4,2},{8,6},{1... | collective-permute-start | bytes 270344 | tf_op jit(solution)/shard_map/ppermute | solution.py:450
  3.6 3.3 %near_rows.1 = (f32[2,11,8,256]{3,2,1,0:T(8,128)S(1)}, bf16[2,256,2560]{2,1,0:T(8,128)(2,1)S(1)}, f32[2,11,8,2560]{3,2,1,0:T(8,128)S(1)}, s16[2,2,11,2,16,128]{5...) custom-call(s32[2]{0:T(128)} %rows_first_far.1, s32[32]{0:T(128)} %points_far.1, ...), custom_call_target="tpu_custom_call" | custom-call | flops 10000000 | bytes 4000000 | tf_op jit(solution)/shard_map/near_rows/pallas_call | solution.py:456
  6.9 0.0 collective-permute-done.near_side
  6.9 0.0 collective-permute-done.1.far_side
  7.0 0.0 copy-start.1
  7.0 0.0 copy-start
  7.0 1.9 %far_rows.1 = bf16[16,32,128]{2,1,0:T(8,128)(2,1)S(1)} custom-call(bf16[2,4,2,2816]{3,2,1,0:T(2,128)(2,1)S(1)} %collective-permute-done.near_side, bf16[2,4,2,2816]{3,2,1,0:T(2,128)(2,1)S(1)} %collective-permute-done.1.far_side, s16[2,2,11,2,16,128]{5,4,3,2,1,0:T(8,128)(2,1)S(1)} %get-tuple-element.14.far_starts, ...), custom_call_target="tpu_custom_call" | custom-call | tf_op jit(solution)/shard_map/far_rows/pallas_call | solution.py:485
  8.9 17.0 %all_to_all.5.received = bf16[16,32,128]{2,1,0:T(8,128)(2,1)S(1)} all-to-all(bf16[16,32,128]{2,1,0:T(8,128)(2,1)S(1)} %far_rows.1), channel_id=1, replica_groups=mesh['lat'=16,'lev'=2] {'lat'}, dimensions={0} | all-to-all | bytes 262144 | tf_op jit(solution)/shard_map/all_to_all | solution.py:500
  25.9 0.1 fusion.1
  26.0 0.0 copy-done.1
  26.0 0.2 fusion
  26.2 0.1 collective-permute-start.2
  26.3 1.0 %left_rows.1 = (bf16[5,320,256]{2,1,0:T(8,128)(2,1)S(1)}, f32[4,32,128]{2,1,0:T(8,128)S(1)}) custom-call(f32[2]{0:T(128)S(1)} %copy-done.1, bf16[16,32,128]{2,1,0:T(8,128)(2,1)S(1)} %all_to_all.5.received), custom_call_target="tpu_custom_call" | custom-call | flops 50000000 | bytes 2000000 | tf_op jit(solution)/shard_map/left_rows/pallas_call | solution.py:515
  27.3 0.2 collective-permute-done.2
  27.4 0.0 copy-done
  27.4 2.2 %degree_sums.1 = (bf16[2,5,2,40,1281]{4,3,2,1,0:T(8,128)(2,1)}, bf16[5,320,256]{2,1,0:T(8,128)(2,1)S(1)}) custom-call(f32[4,32,128]{2,1,0:T(8,128)S(1)} %get-tuple-element.20.base, f32[1,2,32,128]{3,2,1,0:T(8,128)S(1)} %bitcast.13, bf16[40,32,1281]{2,1,0:T(8,128)(2,1)S(1)} %copy-done, ...), custom_call_target="tpu_custom_call", output_to_operand_aliasing={{1}: (3, {})} | custom-call | tf_op jit(solution)/shard_map/degree_sums/pallas_call | solution.py:528
  (1 shorter events, 0.0 us)
Async XLA Ops:
  0.0 6.9 %collective-permute-start = (bf16[2,4,2,2816]{3,2,1,0:T(2,128)(2,1)}, bf16[2,4,2,2816]{3,2,1,0:T(2,128)(2,1)S(1)}, u32[]{:S(2)}, u32[]{:S(2)}) collective-permute-start(bf16[2,4,2,2816]{3,2,1,0:T(2,128)(2,1)} %fields_far.1), channel_id=1, source_target_pairs={{0,2},{4,6},{8,10},{12,14},{16,18},{20,22},{24,26},{28,30},{2,0},{... | collective-permute-start | bytes 270344 | tf_op jit(solution)/shard_map/ppermute | solution.py:450
  2.9 4.0 %collective-permute-start.1 = (bf16[2,4,2,2816]{3,2,1,0:T(2,128)(2,1)}, bf16[2,4,2,2816]{3,2,1,0:T(2,128)(2,1)S(1)}, u32[]{:S(2)}, u32[]{:S(2)}) collective-permute-start(bf16[2,4,2,2816]{3,2,1,0:T(2,128)(2,1)} %fields_far.1), channel_id=1, source_target_pairs={{2,4},{6,8},{10,12},{14,16},{18,20},{22,24},{26,28},{4,2},{8,6},{1... | collective-permute-start | bytes 270344 | tf_op jit(solution)/shard_map/ppermute | solution.py:450
  7.0 19.0 %copy-start.1 = (f32[2]{0:T(128)S(1)}, f32[2]{0:T(128)}, u32[]{:S(2)}) copy-start(f32[2]{0:T(128)} %thickness.1) | copy-start | bytes 28
  7.0 20.5 %copy-start = (bf16[40,32,1281]{2,1,0:T(8,128)(2,1)S(1)}, bf16[40,32,1281]{2,1,0:T(8,128)(2,1)}, u32[]{:S(2)}) copy-start(bf16[40,32,1281]{2,1,0:T(8,128)(2,1)} %legendre.1) | copy-start | bytes 9838084
  26.2 1.3 %collective-permute-start.2 = (f32[2,32,128]{2,1,0:T(8,128)S(1)}, f32[2,32,128]{2,1,0:T(8,128)S(1)}, u32[]{:S(2)}, u32[]{:S(2)}) collective-permute-start(f32[2,32,128]{2,1,0:T(8,128)S(1)} %bitcast.16), channel_id=1, source_target_pairs={{0,1},{1,0},{2,3},{3,2},{4,5},{5,4},{6,7},{7,6},{8,9},{9,8},{10,11... | collective-permute-start | bytes 98312 | tf_op jit(solution)/shard_map/ppermute | solution.py:506

commit v18 on v17

--- a/solution.py
+++ b/solution.py
@@ -167,8 +167,8 @@
         inverse = 1.0 / total
         scales.append((total, inverse, jnp.sqrt(2.0 * inverse)))
     few = lax.broadcasted_iota(jnp.int32, (SUB, width), 0).astype(jnp.float32)
-    many = lax.broadcasted_iota(jnp.int32, (couples + 3, width), 0)
-    many = jnp.where(many < couples, many * (2 * LANES), (many - (couples - 1)) * HALF)
+    many = lax.broadcasted_iota(jnp.int32, (2 * couples + 1, width), 0)
+    many = jnp.where(many < 2 * couples, many * LANES, HALF)
     many = many.astype(jnp.float32)
     for at in range(0, columns, width):
         numbers = wavenumbers(at, width, pair_count, pair_total)
@@ -178,18 +178,18 @@
             large = turn_parts(numbers * many, total, inverse)
             here = slice(at, at + width)
             there = slice(columns + at, columns + at + width)
-            for couple in range(couples):
+            for block in range(2 * couples):
                 for lanes, part in ((here, large[0]), (there, large[1])):
-                    twiddle[latitude, couple, :, lanes] = jnp.broadcast_to(
-                        scaling * part[couple : couple + 1], (SUB, width)
+                    twiddle[latitude, block, :, lanes] = jnp.broadcast_to(
+                        scaling * part[block : block + 1], (SUB, width)
                     )
             products = [ones] + [multiplied(row_of(eights, row), ones) for row in range(1, SUB)]
-            block = tuple(jnp.concatenate(parts, axis=0) for parts in zip(*products))
-            for quarter in range(4):
-                turned = block
-                if quarter > 0:
-                    turned = multiplied(row_of(large, couples + quarter - 1), block)
-                rows = slice(HALF * quarter, HALF * (quarter + 1))
+            products = tuple(jnp.concatenate(parts, axis=0) for parts in zip(*products))
+            for upper_half in range(2):
+                turned = products
+                if upper_half:
+                    turned = multiplied(row_of(large, 2 * couples), products)
+                rows = slice(HALF * upper_half, HALF * (upper_half + 1))
                 table[latitude, rows, here] = turned[0].astype(jnp.bfloat16)
                 table[latitude, rows, there] = turned[1].astype(jnp.bfloat16)
     for fetch in fetches[1:]:
@@ -278,9 +278,9 @@
                 )
             for side in range(2):
                 live = lane + (2 * couple + side) * LANES < fact[lat_count + latitude]
-                grid[latitude, couple, :, sides[side]] = jnp.where(live, totals[side], 0.0)
+                grid[latitude, 2 * couple + side] = jnp.where(live, totals[side], 0.0)
     for latitude in range(lat_count):
-        rows = grid[latitude].reshape(couples * SUB, 2 * LANES).astype(jnp.bfloat16)
+        rows = grid[latitude].reshape(2 * couples * SUB, LANES).astype(jnp.bfloat16)
         for at in range(0, columns, width):
             real = jnp.dot(
                 rows, table[latitude, :, at : at + width], preferred_element_type=jnp.float32
@@ -292,10 +292,10 @@
             )
             cosine = jnp.zeros((SUB, width), jnp.float32)
             sine = jnp.zeros((SUB, width), jnp.float32)
-            for couple in range(couples):
-                turn_cos = twiddle[latitude, couple, :, at : at + width]
-                turn_sin = twiddle[latitude, couple, :, columns + at : columns + at + width]
-                here = slice(couple * SUB, (couple + 1) * SUB)
+            for block in range(2 * couples):
+                turn_cos = twiddle[latitude, block, :, at : at + width]
+                turn_sin = twiddle[latitude, block, :, columns + at : columns + at + width]
+                here = slice(block * SUB, (block + 1) * SUB)
                 cosine = cosine + (real[here] * turn_cos - imag[here] * turn_sin)
                 sine = sine - (real[here] * turn_sin + imag[here] * turn_cos)
             waves[latitude, 0:SUB, at : at + width] = cosine
@@ -457,8 +457,8 @@
         functools.partial(near_kernel, pair_count * owners, pair_count),
         out_shape=(
             jax.ShapeDtypeStruct((lat_count, couples, SUB, 2 * LANES), jnp.float32),
-            jax.ShapeDtypeStruct((lat_count, 2 * LANES, 2 * columns), jnp.bfloat16),
-            jax.ShapeDtypeStruct((lat_count, couples, SUB, 2 * columns), jnp.float32),
+            jax.ShapeDtypeStruct((lat_count, LANES, 2 * columns), jnp.bfloat16),
+            jax.ShapeDtypeStruct((lat_count, blocks, SUB, 2 * columns), jnp.float32),
             jax.ShapeDtypeStruct((lat_count, 2, couples, 2, 2 * SUB, LANES), jnp.int16),
             jax.ShapeDtypeStruct((lat_count, 2, couples, SUB, SUB, LANES), jnp.float32),
             jax.ShapeDtypeStruct((4 * lat_count, LANES), jnp.int32),
@@ -490,7 +490,7 @@
         scratch_shapes=[
             pltpu.VMEM((2, fields.size // LANES, LANES), jnp.float32),
             pltpu.VMEM((2 * lat_count, blocks + 2, 2 * SUB, LANES), jnp.bfloat16),
-            pltpu.VMEM((lat_count, couples, SUB, 2 * LANES), jnp.float32),
+            pltpu.VMEM((lat_count, blocks, SUB, LANES), jnp.float32),
             pltpu.VMEM((lat_count, 2 * SUB, columns + LANES), jnp.float32),
         ],
         compiler_params=params,

time: 29.8 us -> 29.9 us (level)
  transfers between devices with their start and end apart: 3 -> 3, of which waited for: 1 -> 1; matrix products, arithmetic and copies ran while one was open for 0% -> 0% of each run, Pallas kernels for 15% -> 14%
where the time goes in v18:
time: 29.9 us; the launch traced here: 29.8 us
  blocking collectives  17.2 us (58%)
  Pallas kernels  8.4 us (28%)
  starting transfers between devices  3.66 us (12%)
    all_to_all x1, blocking collectives, local(): lax.all_to_all(coefficients, 'lat', split_axis=0, concat_axis=0, tiled=True)  17.2 us
    ppermute x2, starting transfers between devices, local(): lax.ppermute(fields, 'lat', edges + [(j, i) for i, j in edges])  3.59 us
    pallas_call x1, Pallas kernels, local(): pl.pallas_call(functools.partial(near_kernel, pair_count * owners, pair_c...  3.2 us
    pallas_call x1, Pallas kernels, local(): pl.pallas_call(functools.partial(legendre_kernel, level_owners, level_cou...  2.19 us
    pallas_call x1, Pallas kernels, local(): pl.pallas_call(far_kernel, out_shape=jax.ShapeDtypeStruct((owners, 2 * SU...  1.98 us
    pallas_call x1, Pallas kernels, local(): pl.pallas_call(functools.partial(left_kernel, level_count, field_count, p...  1.03 us
  transfers between devices with their start and end apart: 3, of which 1 were waited for; matrix products, arithmetic and copies ran while one was open for 0% of the time, Pallas kernels for 14%

profile of v18, /device:TPU:0, one launch (start us, length us, event | category | flops | bytes accessed | tf_op | source)
XLA Modules:
  0.0 29.8 jit_solution(8920000062513925112)
XLA Ops:
  0.0 2.9 %collective-permute-start = (bf16[2,4,2,2816]{3,2,1,0:T(2,128)(2,1)}, bf16[2,4,2,2816]{3,2,1,0:T(2,128)(2,1)S(1)}, u32[]{:S(2)}, u32[]{:S(2)}) collective-permute-start(bf16[2,4,2,2816]{3,2,1,0:T(2,128)(2,1)} %fields_far.1), channel_id=1, source_target_pairs={{0,2},{4,6},{8,10},{12,14},{16,18},{20,22},{24,26},{28,30},{2,0},{... | collective-permute-start | bytes 270344 | tf_op jit(solution)/shard_map/ppermute | solution.py:450
  2.9 0.7 %collective-permute-start.1 = (bf16[2,4,2,2816]{3,2,1,0:T(2,128)(2,1)}, bf16[2,4,2,2816]{3,2,1,0:T(2,128)(2,1)S(1)}, u32[]{:S(2)}, u32[]{:S(2)}) collective-permute-start(bf16[2,4,2,2816]{3,2,1,0:T(2,128)(2,1)} %fields_far.1), channel_id=1, source_target_pairs={{2,4},{6,8},{10,12},{14,16},{18,20},{22,24},{26,28},{4,2},{8,6},{1... | collective-permute-start | bytes 270344 | tf_op jit(solution)/shard_map/ppermute | solution.py:450
  3.6 3.2 %near_rows.1 = (f32[2,11,8,256]{3,2,1,0:T(8,128)S(1)}, bf16[2,128,2560]{2,1,0:T(8,128)(2,1)S(1)}, f32[2,22,8,2560]{3,2,1,0:T(8,128)S(1)}, s16[2,2,11,2,16,128]{5...) custom-call(s32[2]{0:T(128)} %rows_first_far.1, s32[32]{0:T(128)} %points_far.1, ...), custom_call_target="tpu_custom_call" | custom-call | flops 10000000 | bytes 4000000 | tf_op jit(solution)/shard_map/near_rows/pallas_call | solution.py:456
  6.8 0.0 collective-permute-done.near_side
  6.8 0.0 collective-permute-done.1.far_side
  6.8 0.0 copy-start.1
  6.8 0.0 copy-start
  6.9 2.0 %far_rows.1 = bf16[16,32,128]{2,1,0:T(8,128)(2,1)S(1)} custom-call(bf16[2,4,2,2816]{3,2,1,0:T(2,128)(2,1)S(1)} %collective-permute-done.near_side, bf16[2,4,2,2816]{3,2,1,0:T(2,128)(2,1)S(1)} %collective-permute-done.1.far_side, s16[2,2,11,2,16,128]{5,4,3,2,1,0:T(8,128)(2,1)S(1)} %get-tuple-element.14.far_starts, ...), custom_call_target="tpu_custom_call" | custom-call | tf_op jit(solution)/shard_map/far_rows/pallas_call | solution.py:485
  8.8 17.2 %all_to_all.5.received = bf16[16,32,128]{2,1,0:T(8,128)(2,1)S(1)} all-to-all(bf16[16,32,128]{2,1,0:T(8,128)(2,1)S(1)} %far_rows.1), channel_id=1, replica_groups=mesh['lat'=16,'lev'=2] {'lat'}, dimensions={0} | all-to-all | bytes 262144 | tf_op jit(solution)/shard_map/all_to_all | solution.py:500
  26.0 0.1 fusion.1
  26.1 0.0 copy-done.1
  26.1 0.2 fusion
  26.3 0.1 collective-permute-start.2
  26.4 1.0 %left_rows.1 = (bf16[5,320,256]{2,1,0:T(8,128)(2,1)S(1)}, f32[4,32,128]{2,1,0:T(8,128)S(1)}) custom-call(f32[2]{0:T(128)S(1)} %copy-done.1, bf16[16,32,128]{2,1,0:T(8,128)(2,1)S(1)} %all_to_all.5.received), custom_call_target="tpu_custom_call" | custom-call | flops 50000000 | bytes 2000000 | tf_op jit(solution)/shard_map/left_rows/pallas_call | solution.py:515
  27.4 0.2 collective-permute-done.2
  27.6 0.0 copy-done
  27.6 2.2 %degree_sums.1 = (bf16[2,5,2,40,1281]{4,3,2,1,0:T(8,128)(2,1)}, bf16[5,320,256]{2,1,0:T(8,128)(2,1)S(1)}) custom-call(f32[4,32,128]{2,1,0:T(8,128)S(1)} %get-tuple-element.20.base, f32[1,2,32,128]{3,2,1,0:T(8,128)S(1)} %bitcast.13, bf16[40,32,1281]{2,1,0:T(8,128)(2,1)S(1)} %copy-done, ...), custom_call_target="tpu_custom_call", output_to_operand_aliasing={{1}: (3, {})} | custom-call | tf_op jit(solution)/shard_map/degree_sums/pallas_call | solution.py:528
  (1 shorter events, 0.0 us)
Async XLA Ops:
  0.0 6.8 %collective-permute-start = (bf16[2,4,2,2816]{3,2,1,0:T(2,128)(2,1)}, bf16[2,4,2,2816]{3,2,1,0:T(2,128)(2,1)S(1)}, u32[]{:S(2)}, u32[]{:S(2)}) collective-permute-start(bf16[2,4,2,2816]{3,2,1,0:T(2,128)(2,1)} %fields_far.1), channel_id=1, source_target_pairs={{0,2},{4,6},{8,10},{12,14},{16,18},{20,22},{24,26},{28,30},{2,0},{... | collective-permute-start | bytes 270344 | tf_op jit(solution)/shard_map/ppermute | solution.py:450
  2.9 3.9 %collective-permute-start.1 = (bf16[2,4,2,2816]{3,2,1,0:T(2,128)(2,1)}, bf16[2,4,2,2816]{3,2,1,0:T(2,128)(2,1)S(1)}, u32[]{:S(2)}, u32[]{:S(2)}) collective-permute-start(bf16[2,4,2,2816]{3,2,1,0:T(2,128)(2,1)} %fields_far.1), channel_id=1, source_target_pairs={{2,4},{6,8},{10,12},{14,16},{18,20},{22,24},{26,28},{4,2},{8,6},{1... | collective-permute-start | bytes 270344 | tf_op jit(solution)/shard_map/ppermute | solution.py:450
  6.8 19.3 %copy-start.1 = (f32[2]{0:T(128)S(1)}, f32[2]{0:T(128)}, u32[]{:S(2)}) copy-start(f32[2]{0:T(128)} %thickness.1) | copy-start | bytes 28
  6.8 20.7 %copy-start = (bf16[40,32,1281]{2,1,0:T(8,128)(2,1)S(1)}, bf16[40,32,1281]{2,1,0:T(8,128)(2,1)}, u32[]{:S(2)}) copy-start(bf16[40,32,1281]{2,1,0:T(8,128)(2,1)} %legendre.1) | copy-start | bytes 9838084
  26.3 1.3 %collective-permute-start.2 = (f32[2,32,128]{2,1,0:T(8,128)S(1)}, f32[2,32,128]{2,1,0:T(8,128)S(1)}, u32[]{:S(2)}, u32[]{:S(2)}) collective-permute-start(f32[2,32,128]{2,1,0:T(8,128)S(1)} %bitcast.16), channel_id=1, source_target_pairs={{0,1},{1,0},{2,3},{3,2},{4,5},{5,4},{6,7},{7,6},{8,9},{9,8},{10,11... | collective-permute-start | bytes 98312 | tf_op jit(solution)/shard_map/ppermute | solution.py:506

commit v19 on v17

--- a/solution.py
+++ b/solution.py
@@ -298,14 +298,15 @@
                 here = slice(couple * SUB, (couple + 1) * SUB)
                 cosine = cosine + (real[here] * turn_cos - imag[here] * turn_sin)
                 sine = sine - (real[here] * turn_sin + imag[here] * turn_cos)
-            waves[latitude, 0:SUB, at : at + width] = cosine
-            waves[latitude, SUB : 2 * SUB, at : at + width] = sine
-        waves[latitude, :, columns:] = jnp.zeros((2 * SUB, waves.shape[2] - columns), jnp.float32)
+            waves[latitude, :, at : at + width] = jnp.concatenate([cosine, sine], axis=0).astype(
+                jnp.bfloat16
+            )
+        waves[latitude, :, columns:] = jnp.zeros((2 * SUB, waves.shape[2] - columns), jnp.bfloat16)
         used = columns // owners
         for owner in range(owners):
             out[owner, 2 * SUB * latitude : 2 * SUB * (latitude + 1), :] = waves[
                 latitude, :, owner * used : owner * used + LANES
-            ].astype(jnp.bfloat16)
+            ]
 
 
 def row_keys(level_count, field_count):
@@ -491,7 +492,7 @@
             pltpu.VMEM((2, fields.size // LANES, LANES), jnp.float32),
             pltpu.VMEM((2 * lat_count, blocks + 2, 2 * SUB, LANES), jnp.bfloat16),
             pltpu.VMEM((lat_count, couples, SUB, 2 * LANES), jnp.float32),
-            pltpu.VMEM((lat_count, 2 * SUB, columns + LANES), jnp.float32),
+            pltpu.VMEM((lat_count, 2 * SUB, columns + LANES), jnp.bfloat16),
         ],
         compiler_params=params,
         name="far_rows",

time: 29.8 us -> 29.8 us (level)
  no operation moved by 1% of the time
where the time goes in v19:
time: 29.8 us; the launch traced here: 29.7 us
  blocking collectives  17 us (57%)
  Pallas kernels  8.45 us (28%)
  starting transfers between devices  3.66 us (12%)
    all_to_all x1, blocking collectives, local(): lax.all_to_all(coefficients, 'lat', split_axis=0, concat_axis=0, tiled=True)  17 us
    ppermute x2, starting transfers between devices, local(): lax.ppermute(fields, 'lat', edges + [(j, i) for i, j in edges])  3.59 us
    pallas_call x1, Pallas kernels, local(): pl.pallas_call(functools.partial(near_kernel, pair_count * owners, pair_c...  3.33 us
    pallas_call x1, Pallas kernels, local(): pl.pallas_call(functools.partial(legendre_kernel, level_owners, level_cou...  2.19 us
    pallas_call x1, Pallas kernels, local(): pl.pallas_call(far_kernel, out_shape=jax.ShapeDtypeStruct((owners, 2 * SU...  1.9 us
    pallas_call x1, Pallas kernels, local(): pl.pallas_call(functools.partial(left_kernel, level_count, field_count, p...  1.03 us
  transfers between devices with their start and end apart: 3, of which 1 were waited for; matrix products, arithmetic and copies ran while one was open for 0% of the time, Pallas kernels for 15%

profile of v19, /device:TPU:0, one launch (start us, length us, event | category | flops | bytes accessed | tf_op | source)
XLA Modules:
  0.0 29.7 jit_solution(17576245210163959550)
XLA Ops:
  0.0 2.9 %collective-permute-start = (bf16[2,4,2,2816]{3,2,1,0:T(2,128)(2,1)}, bf16[2,4,2,2816]{3,2,1,0:T(2,128)(2,1)S(1)}, u32[]{:S(2)}, u32[]{:S(2)}) collective-permute-start(bf16[2,4,2,2816]{3,2,1,0:T(2,128)(2,1)} %fields_far.1), channel_id=1, source_target_pairs={{0,2},{4,6},{8,10},{12,14},{16,18},{20,22},{24,26},{28,30},{2,0},{... | collective-permute-start | bytes 270344 | tf_op jit(solution)/shard_map/ppermute | solution.py:451
  2.9 0.7 %collective-permute-start.1 = (bf16[2,4,2,2816]{3,2,1,0:T(2,128)(2,1)}, bf16[2,4,2,2816]{3,2,1,0:T(2,128)(2,1)S(1)}, u32[]{:S(2)}, u32[]{:S(2)}) collective-permute-start(bf16[2,4,2,2816]{3,2,1,0:T(2,128)(2,1)} %fields_far.1), channel_id=1, source_target_pairs={{2,4},{6,8},{10,12},{14,16},{18,20},{22,24},{26,28},{4,2},{8,6},{1... | collective-permute-start | bytes 270344 | tf_op jit(solution)/shard_map/ppermute | solution.py:451
  3.6 3.3 %near_rows.1 = (f32[2,11,8,256]{3,2,1,0:T(8,128)S(1)}, bf16[2,256,2560]{2,1,0:T(8,128)(2,1)S(1)}, f32[2,11,8,2560]{3,2,1,0:T(8,128)S(1)}, s16[2,2,11,2,16,128]{5...) custom-call(s32[2]{0:T(128)} %rows_first_far.1, s32[32]{0:T(128)} %points_far.1, ...), custom_call_target="tpu_custom_call" | custom-call | flops 10000000 | bytes 4000000 | tf_op jit(solution)/shard_map/near_rows/pallas_call | solution.py:457
  6.9 0.0 collective-permute-done.near_side
  6.9 0.0 collective-permute-done.1.far_side
  7.0 0.0 copy-start.1
  7.0 0.0 copy-start
  7.0 1.9 %far_rows.1 = bf16[16,32,128]{2,1,0:T(8,128)(2,1)S(1)} custom-call(bf16[2,4,2,2816]{3,2,1,0:T(2,128)(2,1)S(1)} %collective-permute-done.near_side, bf16[2,4,2,2816]{3,2,1,0:T(2,128)(2,1)S(1)} %collective-permute-done.1.far_side, s16[2,2,11,2,16,128]{5,4,3,2,1,0:T(8,128)(2,1)S(1)} %get-tuple-element.14.far_starts, ...), custom_call_target="tpu_custom_call" | custom-call | tf_op jit(solution)/shard_map/far_rows/pallas_call | solution.py:486
  8.9 17.0 %all_to_all.5.received = bf16[16,32,128]{2,1,0:T(8,128)(2,1)S(1)} all-to-all(bf16[16,32,128]{2,1,0:T(8,128)(2,1)S(1)} %far_rows.1), channel_id=1, replica_groups=mesh['lat'=16,'lev'=2] {'lat'}, dimensions={0} | all-to-all | bytes 262144 | tf_op jit(solution)/shard_map/all_to_all | solution.py:501
  25.9 0.1 fusion.1
  26.0 0.0 copy-done.1
  26.0 0.2 fusion
  26.2 0.1 collective-permute-start.2
  26.3 1.0 %left_rows.1 = (bf16[5,320,256]{2,1,0:T(8,128)(2,1)S(1)}, f32[4,32,128]{2,1,0:T(8,128)S(1)}) custom-call(f32[2]{0:T(128)S(1)} %copy-done.1, bf16[16,32,128]{2,1,0:T(8,128)(2,1)S(1)} %all_to_all.5.received), custom_call_target="tpu_custom_call" | custom-call | flops 50000000 | bytes 2000000 | tf_op jit(solution)/shard_map/left_rows/pallas_call | solution.py:516
  27.3 0.2 collective-permute-done.2
  27.5 0.0 copy-done
  27.5 2.2 %degree_sums.1 = (bf16[2,5,2,40,1281]{4,3,2,1,0:T(8,128)(2,1)}, bf16[5,320,256]{2,1,0:T(8,128)(2,1)S(1)}) custom-call(f32[4,32,128]{2,1,0:T(8,128)S(1)} %get-tuple-element.20.base, f32[1,2,32,128]{3,2,1,0:T(8,128)S(1)} %bitcast.13, bf16[40,32,1281]{2,1,0:T(8,128)(2,1)S(1)} %copy-done, ...), custom_call_target="tpu_custom_call", output_to_operand_aliasing={{1}: (3, {})} | custom-call | tf_op jit(solution)/shard_map/degree_sums/pallas_call | solution.py:529
  (1 shorter events, 0.0 us)
Async XLA Ops:
  0.0 6.9 %collective-permute-start = (bf16[2,4,2,2816]{3,2,1,0:T(2,128)(2,1)}, bf16[2,4,2,2816]{3,2,1,0:T(2,128)(2,1)S(1)}, u32[]{:S(2)}, u32[]{:S(2)}) collective-permute-start(bf16[2,4,2,2816]{3,2,1,0:T(2,128)(2,1)} %fields_far.1), channel_id=1, source_target_pairs={{0,2},{4,6},{8,10},{12,14},{16,18},{20,22},{24,26},{28,30},{2,0},{... | collective-permute-start | bytes 270344 | tf_op jit(solution)/shard_map/ppermute | solution.py:451
  2.9 4.0 %collective-permute-start.1 = (bf16[2,4,2,2816]{3,2,1,0:T(2,128)(2,1)}, bf16[2,4,2,2816]{3,2,1,0:T(2,128)(2,1)S(1)}, u32[]{:S(2)}, u32[]{:S(2)}) collective-permute-start(bf16[2,4,2,2816]{3,2,1,0:T(2,128)(2,1)} %fields_far.1), channel_id=1, source_target_pairs={{2,4},{6,8},{10,12},{14,16},{18,20},{22,24},{26,28},{4,2},{8,6},{1... | collective-permute-start | bytes 270344 | tf_op jit(solution)/shard_map/ppermute | solution.py:451
  7.0 19.0 %copy-start.1 = (f32[2]{0:T(128)S(1)}, f32[2]{0:T(128)}, u32[]{:S(2)}) copy-start(f32[2]{0:T(128)} %thickness.1) | copy-start | bytes 28
  7.0 20.5 %copy-start = (bf16[40,32,1281]{2,1,0:T(8,128)(2,1)S(1)}, bf16[40,32,1281]{2,1,0:T(8,128)(2,1)}, u32[]{:S(2)}) copy-start(bf16[40,32,1281]{2,1,0:T(8,128)(2,1)} %legendre.1) | copy-start | bytes 9838084
  26.2 1.3 %collective-permute-start.2 = (f32[2,32,128]{2,1,0:T(8,128)S(1)}, f32[2,32,128]{2,1,0:T(8,128)S(1)}, u32[]{:S(2)}, u32[]{:S(2)}) collective-permute-start(f32[2,32,128]{2,1,0:T(8,128)S(1)} %bitcast.16), channel_id=1, source_target_pairs={{0,1},{1,0},{2,3},{3,2},{4,5},{5,4},{6,7},{7,6},{8,9},{9,8},{10,11... | collective-permute-start | bytes 98312 | tf_op jit(solution)/shard_map/ppermute | solution.py:507

commit v20 on v17

--- a/solution.py
+++ b/solution.py
@@ -399,8 +399,8 @@
             sums[level, field_count, part] = base[2 * level + part] + deeper
     place_rows(sums, keys, pair_count, left)
     copies = []
-    for start in range(0, degrees, 256):
-        stop = min(start + 256, degrees)
+    for start in range(0, degrees, 512):
+        stop = min(start + 512, degrees)
         low = 0 if start < 2 * pair_total else half
         high = 2 * half if stop > pair_total + 1 else half
         parts = []
@@ -533,7 +533,7 @@
         input_output_aliases={3: 1},
         scratch_shapes=[
             pltpu.VMEM(out_shape, jnp.bfloat16),
-            pltpu.SemaphoreType.DMA(((degrees + 255) // 256,)),
+            pltpu.SemaphoreType.DMA(((degrees + 511) // 512,)),
         ],
         compiler_params=params,
         name="degree_sums",

time: 29.8 us -> 29.9 us (level)
  no operation moved by 1% of the time
where the time goes in v20:
time: 29.9 us; the launch traced here: 29.7 us
  blocking collectives  17 us (57%)
  Pallas kernels  8.51 us (28%)
  starting transfers between devices  3.66 us (12%)
    all_to_all x1, blocking collectives, local(): lax.all_to_all(coefficients, 'lat', split_axis=0, concat_axis=0, tiled=True)  17 us
    ppermute x2, starting transfers between devices, local(): lax.ppermute(fields, 'lat', edges + [(j, i) for i, j in edges])  3.59 us
    pallas_call x1, Pallas kernels, local(): pl.pallas_call(functools.partial(near_kernel, pair_count * owners, pair_c...  3.33 us
    pallas_call x1, Pallas kernels, local(): pl.pallas_call(functools.partial(legendre_kernel, level_owners, level_cou...  2.27 us
    pallas_call x1, Pallas kernels, local(): pl.pallas_call(far_kernel, out_shape=jax.ShapeDtypeStruct((owners, 2 * SU...  1.88 us
    pallas_call x1, Pallas kernels, local(): pl.pallas_call(functools.partial(left_kernel, level_count, field_count, p...  1.03 us
  transfers between devices with their start and end apart: 3, of which 1 were waited for; matrix products, arithmetic and copies ran while one was open for 0% of the time, Pallas kernels for 15%

profile of v20, /device:TPU:0, one launch (start us, length us, event | category | flops | bytes accessed | tf_op | source)
XLA Modules:
  0.0 29.7 jit_solution(9725103715736417625)
XLA Ops:
  0.0 2.9 %collective-permute-start = (bf16[2,4,2,2816]{3,2,1,0:T(2,128)(2,1)}, bf16[2,4,2,2816]{3,2,1,0:T(2,128)(2,1)S(1)}, u32[]{:S(2)}, u32[]{:S(2)}) collective-permute-start(bf16[2,4,2,2816]{3,2,1,0:T(2,128)(2,1)} %fields_far.1), channel_id=1, source_target_pairs={{0,2},{4,6},{8,10},{12,14},{16,18},{20,22},{24,26},{28,30},{2,0},{... | collective-permute-start | bytes 270344 | tf_op jit(solution)/shard_map/ppermute | solution.py:450
  2.9 0.7 %collective-permute-start.1 = (bf16[2,4,2,2816]{3,2,1,0:T(2,128)(2,1)}, bf16[2,4,2,2816]{3,2,1,0:T(2,128)(2,1)S(1)}, u32[]{:S(2)}, u32[]{:S(2)}) collective-permute-start(bf16[2,4,2,2816]{3,2,1,0:T(2,128)(2,1)} %fields_far.1), channel_id=1, source_target_pairs={{2,4},{6,8},{10,12},{14,16},{18,20},{22,24},{26,28},{4,2},{8,6},{1... | collective-permute-start | bytes 270344 | tf_op jit(solution)/shard_map/ppermute | solution.py:450
  3.6 3.3 %near_rows.1 = (f32[2,11,8,256]{3,2,1,0:T(8,128)S(1)}, bf16[2,256,2560]{2,1,0:T(8,128)(2,1)S(1)}, f32[2,11,8,2560]{3,2,1,0:T(8,128)S(1)}, s16[2,2,11,2,16,128]{5...) custom-call(s32[2]{0:T(128)} %rows_first_far.1, s32[32]{0:T(128)} %points_far.1, ...), custom_call_target="tpu_custom_call" | custom-call | flops 10000000 | bytes 4000000 | tf_op jit(solution)/shard_map/near_rows/pallas_call | solution.py:456
  6.9 0.0 collective-permute-done.near_side
  6.9 0.0 collective-permute-done.1.far_side
  7.0 0.0 copy-start.1
  7.0 0.0 copy-start
  7.0 1.9 %far_rows.1 = bf16[16,32,128]{2,1,0:T(8,128)(2,1)S(1)} custom-call(bf16[2,4,2,2816]{3,2,1,0:T(2,128)(2,1)S(1)} %collective-permute-done.near_side, bf16[2,4,2,2816]{3,2,1,0:T(2,128)(2,1)S(1)} %collective-permute-done.1.far_side, s16[2,2,11,2,16,128]{5,4,3,2,1,0:T(8,128)(2,1)S(1)} %get-tuple-element.14.far_starts, ...), custom_call_target="tpu_custom_call" | custom-call | tf_op jit(solution)/shard_map/far_rows/pallas_call | solution.py:485
  8.9 17.0 %all_to_all.5.received = bf16[16,32,128]{2,1,0:T(8,128)(2,1)S(1)} all-to-all(bf16[16,32,128]{2,1,0:T(8,128)(2,1)S(1)} %far_rows.1), channel_id=1, replica_groups=mesh['lat'=16,'lev'=2] {'lat'}, dimensions={0} | all-to-all | bytes 262144 | tf_op jit(solution)/shard_map/all_to_all | solution.py:500
  25.9 0.1 fusion.1
  26.0 0.0 copy-done.1
  26.0 0.2 fusion
  26.2 0.1 collective-permute-start.2
  26.3 1.0 %left_rows.1 = (bf16[5,320,256]{2,1,0:T(8,128)(2,1)S(1)}, f32[4,32,128]{2,1,0:T(8,128)S(1)}) custom-call(f32[2]{0:T(128)S(1)} %copy-done.1, bf16[16,32,128]{2,1,0:T(8,128)(2,1)S(1)} %all_to_all.5.received), custom_call_target="tpu_custom_call" | custom-call | flops 50000000 | bytes 2000000 | tf_op jit(solution)/shard_map/left_rows/pallas_call | solution.py:515
  27.3 0.2 collective-permute-done.2
  27.4 0.0 copy-done
  27.4 2.3 %degree_sums.1 = (bf16[2,5,2,40,1281]{4,3,2,1,0:T(8,128)(2,1)}, bf16[5,320,256]{2,1,0:T(8,128)(2,1)S(1)}) custom-call(f32[4,32,128]{2,1,0:T(8,128)S(1)} %get-tuple-element.20.base, f32[1,2,32,128]{3,2,1,0:T(8,128)S(1)} %bitcast.13, bf16[40,32,1281]{2,1,0:T(8,128)(2,1)S(1)} %copy-done, ...), custom_call_target="tpu_custom_call", output_to_operand_aliasing={{1}: (3, {})} | custom-call | tf_op jit(solution)/shard_map/degree_sums/pallas_call | solution.py:528
  (1 shorter events, 0.0 us)
Async XLA Ops:
  0.0 6.9 %collective-permute-start = (bf16[2,4,2,2816]{3,2,1,0:T(2,128)(2,1)}, bf16[2,4,2,2816]{3,2,1,0:T(2,128)(2,1)S(1)}, u32[]{:S(2)}, u32[]{:S(2)}) collective-permute-start(bf16[2,4,2,2816]{3,2,1,0:T(2,128)(2,1)} %fields_far.1), channel_id=1, source_target_pairs={{0,2},{4,6},{8,10},{12,14},{16,18},{20,22},{24,26},{28,30},{2,0},{... | collective-permute-start | bytes 270344 | tf_op jit(solution)/shard_map/ppermute | solution.py:450
  2.9 4.0 %collective-permute-start.1 = (bf16[2,4,2,2816]{3,2,1,0:T(2,128)(2,1)}, bf16[2,4,2,2816]{3,2,1,0:T(2,128)(2,1)S(1)}, u32[]{:S(2)}, u32[]{:S(2)}) collective-permute-start(bf16[2,4,2,2816]{3,2,1,0:T(2,128)(2,1)} %fields_far.1), channel_id=1, source_target_pairs={{2,4},{6,8},{10,12},{14,16},{18,20},{22,24},{26,28},{4,2},{8,6},{1... | collective-permute-start | bytes 270344 | tf_op jit(solution)/shard_map/ppermute | solution.py:450
  7.0 19.0 %copy-start.1 = (f32[2]{0:T(128)S(1)}, f32[2]{0:T(128)}, u32[]{:S(2)}) copy-start(f32[2]{0:T(128)} %thickness.1) | copy-start | bytes 28
  7.0 20.5 %copy-start = (bf16[40,32,1281]{2,1,0:T(8,128)(2,1)S(1)}, bf16[40,32,1281]{2,1,0:T(8,128)(2,1)}, u32[]{:S(2)}) copy-start(bf16[40,32,1281]{2,1,0:T(8,128)(2,1)} %legendre.1) | copy-start | bytes 9838084
  26.2 1.3 %collective-permute-start.2 = (f32[2,32,128]{2,1,0:T(8,128)S(1)}, f32[2,32,128]{2,1,0:T(8,128)S(1)}, u32[]{:S(2)}, u32[]{:S(2)}) collective-permute-start(f32[2,32,128]{2,1,0:T(8,128)S(1)} %bitcast.16), channel_id=1, source_target_pairs={{0,1},{1,0},{2,3},{3,2},{4,5},{5,4},{6,7},{7,6},{8,9},{9,8},{10,11... | collective-permute-start | bytes 98312 | tf_op jit(solution)/shard_map/ppermute | solution.py:506
